TPU v7x, 512 devices: a whole 4x8x8 slice. The times are simulated.
512 devices in a mesh: dp: 64 (over z_hi, x, y), group: 8 (over z_lo, core).
Axes of the slice: x: 4, y: 8, z: 8 (z_hi: 2, z_lo: 4; z = z_hi * 4 + z_lo), core: 2. Of those that a mesh axis runs over, the one named last changes fastest.
Arguments:
- sampled: bfloat16 [65536, 2304], P('dp', 'group'), may hold values from -6 to 6
- assignment: int32 [96], replicated, may hold values from 0 to 127, as said below
- inverse_rows: bfloat16 [128, 24, 2304], P('dp'), as said below
- gradient: bfloat16 [2304, 3072], P(None, 'group'), may hold values from -6 to 6
Outputs:
- factor_tiles: float32 [128, 24, 2304], P('dp', None, 'group')
- preconditioned: bfloat16 [2304, 3072], P(None, 'group')
Inputs may be any that keep to these rules, and one draw needn't show every extreme that they name: assignment[t] is the slot holding tile t; slot s belongs to the owner at index s // 2 of dp; no two tiles share a slot; some owner holds 2 tiles. `inverse_rows`: slot assignment[t] holds the inverse factor's rows of tile t; slots that no tile names are not read.
All inputs are finite; a program needn't handle non-finite values.
Results may differ from a plain program's by a relative error of at most 0.0004.
Values may be sent and summed in bfloat16 or wider, within the bound.
No kernel may reach another device: no remote copies, remote signals or barrier semaphores. Data moves between devices by JAX's collectives and lax.ppermute only.
A program may use at most 64 MiB of HBM per device.

v0:
```python
import jax
import jax.numpy as jnp
from jax import lax
from jax.sharding import PartitionSpec as P


def body(sampled, assignment, inverse_rows, gradient):
    owners = lax.axis_size("dp")
    myself = lax.axis_index("dp")
    token_count = sampled.shape[0]
    column_width = sampled.shape[1]
    slot_count = inverse_rows.shape[0]
    tile_rows = inverse_rows.shape[1]
    tile_count = assignment.shape[0]
    grad_width = gradient.shape[1]
    partial_value = lax.dot_general(
        lax.all_gather(sampled, "group", axis=1, tiled=True),
        sampled,
        (((0,), (0,)), ((), ())),
        preferred_element_type=jnp.float32,
    )
    partial_value = partial_value * (1.0 / (token_count * owners))
    rows_tiled = partial_value.reshape(tile_count, tile_rows * column_width)
    wanted = myself * slot_count + jnp.arange(slot_count, dtype=jnp.int32)
    slot_hits = (assignment[None, :] == wanted[:, None]).astype(jnp.int32)
    slot_used = jnp.sum(slot_hits, axis=1) > 0
    padded = (
        jnp.zeros((owners * slot_count, tile_rows * column_width), jnp.float32)
        .at[assignment]
        .set(rows_tiled)
    )
    factor = lax.psum_scatter(padded, "dp", scatter_dimension=0, tiled=True)
    factor_tiles = factor.reshape(slot_count, tile_rows, column_width)

    def one_slot(position):

        def compute_rows(unused_arg):
            return jnp.dot(
                inverse_rows[position], gradient, preferred_element_type=jnp.float32
            ).astype(jnp.bfloat16)

        def empty_rows(unused_arg):
            return jnp.zeros((tile_rows, grad_width), jnp.bfloat16)

        return lax.cond(slot_used[position], compute_rows, empty_rows, 0)

    blocks = jnp.stack([one_slot(position) for position in range(slot_count)])
    stacked = lax.all_gather(blocks, "dp", axis=0, tiled=True)
    stacked = stacked.reshape(owners * slot_count, tile_rows * grad_width)
    preconditioned = jnp.take(stacked, assignment, axis=0).reshape(
        tile_count * tile_rows, grad_width
    )
    return (factor_tiles, preconditioned)


def solution(mesh):
    placed = (P("dp", "group"), P(), P("dp", None, None), P(None, "group"))
    return jax.shard_map(
        body,
        mesh=mesh,
        in_specs=placed,
        out_specs=(P("dp", None, "group"), P(None, "group")),
        check_vma=False,
    )
```

profile of v0, /device:TPU:64, one launch (start us, length us, event | category | flops | bytes accessed | tf_op | source)
XLA Modules:
  0.0 1080.1 jit_solution(16584470576240750730)
XLA Ops:
  7.2 0.0 copy-start
  7.2 0.0 copy-start.1
  7.2 0.0 all-gather.3.cloned.1.call-start
  7.2 0.7 all-gather.3.cloned.1.call-update
  7.9 0.0 all-gather.5.cloned.1.call-start
  8.0 0.8 fusion.8
  8.8 0.6 fusion.9
  10.7 1.9 conditional.3
  10.7 1.9 fusion.3
  12.6 1.9 conditional.2
  12.7 1.9 fusion
  14.6 0.6 pad_maximum_fusion
  15.2 0.0 all-gather.5.cloned.1.call-update
  15.2 0.0 all-reduce.3.cloned.1.call-start
  15.3 0.0 copy-done.1
  15.3 56.4 %all-gather.3.cloned.1.call-done = bf16[1024,2304]{0,1:T(8,128)(2,1)} async-done(((bf16[1024,288]{0,1:T(8,128)(2,1)}), bf16[1024,2304]{0,1:T(8,128)(2,1)}) %all-gather.3.cloned.1.call-update) | async-done | bytes 4718608 | tf_op jit(solution)/shard_map/all_gather | solution.py:17
  71.7 0.0 copy-done
  71.7 5.4 convolution_multiply_fusion
  77.1 2.4 copy.8
  79.5 2.2 reshape.47
  81.7 5.2 scatter_custom_fusion
  86.9 0.0 all-reduce.3.cloned.1.call-update
  86.9 0.1 broadcast_in_dim.24
  87.0 0.1 broadcast_in_dim.25
  87.1 1.3 dynamic-slice
  89.1 131.4 %all-gather.5.cloned.1.call-done = bf16[128,24,384]{2,1,0:T(8,128)(2,1)} async-done(((bf16[2,24,384]{2,1,0:T(8,128)(2,1)}), bf16[128,24,384]{2,1,0:T(8,128)(2,1)}) %all-gather.5.cloned.1.call-update) | async-done | bytes 2359312 | tf_op jit(solution)/shard_map/all_gather | solution.py:48
  220.5 2.1 copy.9
  222.6 2.9 gather_fusion
  225.5 2.7 gather.7
  228.2 2.2 broadcast_select_fusion
  230.3 841.6 %all-reduce.3.cloned.1.call-done = f32[128,6912]{1,0:T(8,128)} async-done(((f32[128,6912]{1,0:T(8,128)}), f32[128,6912]{1,0:T(8,128)}) %all-reduce.3.cloned.1.call-update) | async-done | bytes 3538960
  1071.9 1.0 constant_dynamic-slice_fusion
  1072.9 0.7 reshape.31
  (5 shorter events, 0.0 us)
Async XLA Ops:
  7.2 64.5 %copy-start = (bf16[1024,288]{0,1:T(8,128)(2,1)S(1)}, bf16[1024,288]{0,1:T(8,128)(2,1)}, u32[]{:S(2)}) copy-start(bf16[1024,288]{0,1:T(8,128)(2,1)} %param.8) | copy-start | bytes 1769476
  7.2 8.1 copy-start.1
  7.2 64.5 %all-gather.3.cloned.1.call-start = ((), (), s32[]{:S(2)}) async-start(), calls=%async_computation | async-start | bytes 5308416 | tf_op jit(solution)/shard_map/all_gather | solution.py:17
  7.9 212.6 %all-gather.5.cloned.1.call-start = ((), (), s32[]{:S(2)}) async-start(), calls=%async_computation.1 | async-start | bytes 2396160 | tf_op jit(solution)/shard_map/all_gather | solution.py:48
  15.2 1056.7 %all-reduce.3.cloned.1.call-start = ((), (), s32[]{:S(2)}) async-start(), calls=%async_computation.2 | async-start | bytes 7077888
Sparse Core Ops, SparseCore 0:
  10.1 61.5 all-gather.2
  76.7 143.7 all-gather.4
  223.4 848.4 all-reduce.2
where the time goes:
time: 1080 us
  waiting for transfers between devices  1030 us (95%)
  local copies, waits for them, and re-layouts  21.1 us (2%)
  between operations  15.8 us (1%)
    unnamed x4, waiting for transfers between devices  842 us
    all_gather x1, waiting for transfers between devices, body(): stacked = lax.all_gather(blocks, 'dp', axis=0, tiled=True)  131 us
    all_gather x1, waiting for transfers between devices, body(): lax.all_gather(sampled, 'group', axis=1, tiled=True)  56.4 us
  transfers between devices with their start and end apart: 3, of which 3 were waited for; matrix products, arithmetic and copies ran while one was open for 3% of the time, Pallas kernels for 0%

commit v1 on v0

v1 whole, which is shorter than its diff:
```python
import jax
import jax.numpy as jnp
from jax import lax
from jax.experimental import pallas as pl
from jax.experimental.pallas import tpu as pltpu
from jax.sharding import Mesh, PartitionSpec as P

DP = ("zh", "x", "yh", "yl")
GROUP = ("zl", "c")
NEAR = ("x", "yl")
FAR = ("yh", "zh")


def gram_kernel(tile_of, own_ref, all_ref, out_ref, rows_ref):
    tile = all_ref.shape[1]
    slots = out_ref.shape[2] // tile
    dest = pl.program_id(0)
    for pair in range(slots // 2):
        both = []
        for part in range(2):
            t = tile_of[dest * slots + 2 * pair + part]
            rows = all_ref[jnp.maximum(t, 0)].astype(jnp.float32)
            both.append(jnp.where(t >= 0, rows, 0.0))
        rows_ref[2 * tile * pair : 2 * tile * (pair + 1), :] = jnp.concatenate(both).astype(
            jnp.bfloat16
        )
    out_ref[0] = lax.dot_general(
        own_ref[...], rows_ref[...], (((1,), (1,)), ((), ())), preferred_element_type=jnp.float32
    )


def gram(tile_of, own, tiles, dests):
    count, tile, tokens = tiles.shape
    cols = own.shape[0]
    lanes = tile_of.shape[0] // dests * tile
    return pl.pallas_call(
        gram_kernel,
        grid_spec=pltpu.PrefetchScalarGridSpec(
            num_scalar_prefetch=1,
            grid=(dests,),
            in_specs=[
                pl.BlockSpec((cols, tokens), lambda d, t: (0, 0)),
                pl.BlockSpec((count, tile, tokens), lambda d, t: (0, 0, 0)),
            ],
            out_specs=pl.BlockSpec((1, cols, lanes), lambda d, t: (d, 0, 0)),
            scratch_shapes=[pltpu.VMEM((lanes, tokens), jnp.bfloat16)],
        ),
        out_shape=jax.ShapeDtypeStruct((dests, cols, lanes), jnp.float32),
        compiler_params=pltpu.CompilerParams(vmem_limit_bytes=48 * 2**20),
    )(tile_of, own, tiles)


def sum_turn_kernel(parts_ref, out_ref):
    total = parts_ref[0]
    for n in range(1, parts_ref.shape[0]):
        total = total + parts_ref[n]
    out_ref[...] = total.T


def sum_turn(parts):
    n, cols, lanes = parts.shape
    return pl.pallas_call(
        sum_turn_kernel,
        grid=(lanes // 128,),
        in_specs=[pl.BlockSpec((n, cols, 128), lambda i: (0, 0, i))],
        out_specs=pl.BlockSpec((128, cols), lambda i: (i, 0)),
        out_shape=jax.ShapeDtypeStruct((lanes, cols), jnp.float32),
        compiler_params=pltpu.CompilerParams(vmem_limit_bytes=32 * 2**20),
    )(parts)


def place_kernel(slot_of, rows_ref, out_ref):
    tile = rows_ref.shape[1]
    for pair in range(out_ref.shape[0] // (2 * tile)):
        both = [rows_ref[slot_of[2 * pair + n]].astype(jnp.float32) for n in range(2)]
        out_ref[2 * tile * pair : 2 * tile * (pair + 1), :] = jnp.concatenate(both).astype(
            out_ref.dtype
        )


def place(slot_of, rows):
    slots, tile, cols = rows.shape
    tiles = slot_of.shape[0]
    return pl.pallas_call(
        place_kernel,
        grid_spec=pltpu.PrefetchScalarGridSpec(
            num_scalar_prefetch=1,
            grid=(1,),
            in_specs=[pl.BlockSpec((slots, tile, cols), lambda i, s: (0, 0, 0))],
            out_specs=pl.BlockSpec((tiles * tile, cols), lambda i, s: (0, 0)),
        ),
        out_shape=jax.ShapeDtypeStruct((tiles * tile, cols), rows.dtype),
        compiler_params=pltpu.CompilerParams(vmem_limit_bytes=32 * 2**20),
    )(slot_of, rows)


def spread(rows, axis):
    copies = jnp.broadcast_to(rows[None], (lax.axis_size(axis),) + rows.shape)
    return lax.all_to_all(copies, axis, 0, 0)


def body(sampled, assignment, inverse_rows, gradient):
    n_zh, n_x, n_yh, n_yl = (lax.axis_size(name) for name in DP)
    held, tile, order = inverse_rows.shape
    tiles = assignment.shape[0]
    tokens, cols = sampled.shape
    width = gradient.shape[1]
    owners = n_zh * n_x * n_yh * n_yl

    own = sampled.T
    everything = lax.all_gather(own, GROUP, axis=0, tiled=True)

    mine = jnp.dot(
        inverse_rows.reshape(held * tile, order), gradient, preferred_element_type=jnp.float32
    ).astype(jnp.bfloat16)
    other = lax.ppermute(mine, "zh", [(0, 1), (1, 0)])
    first = lax.axis_index("zh") == 0
    rows = jnp.stack([jnp.where(first, mine, other), jnp.where(first, other, mine)])
    rows = spread(rows.reshape(n_zh * held * tile, width), ("yh", "yl"))
    rows = rows.reshape(n_yh * n_yl * n_zh * held * tile, width)
    rows = spread(rows, "x").reshape(owners * held, tile, width)
    place_of = jnp.arange(owners * held, dtype=jnp.int32).reshape(n_x, n_yh * n_yl, n_zh, held)
    slot_place = place_of.transpose(2, 0, 1, 3).reshape(-1)
    preconditioned = place(slot_place[assignment], rows)

    tile_of = (
        jnp.full((owners * held,), -1, jnp.int32)
        .at[assignment]
        .set(jnp.arange(tiles, dtype=jnp.int32))
    )
    tile_of = tile_of.reshape(n_zh, n_x, n_yh, n_yl, held).transpose(1, 3, 2, 0, 4).reshape(-1)
    near, far = n_x * n_yl, n_yh * n_zh
    scale = 1.0 / (tokens * owners)
    terms = gram(tile_of, own, everything.reshape(tiles, tile, tokens), near)
    terms = lax.all_to_all(terms, NEAR, 0, 0)
    terms = sum_turn(terms).reshape(far, held * tile, cols)
    terms = lax.all_to_all(terms, FAR, 0, 0)
    factor_tiles = (jnp.sum(terms, axis=0) * scale).reshape(held, tile, cols)
    return factor_tiles, preconditioned


def solution(mesh):
    split = Mesh(mesh.devices.reshape(2, 4, 4, 2, 4, 2), DP + GROUP)
    placed = (P(DP, GROUP), P(), P(DP, None, None), P(None, GROUP))
    return jax.shard_map(
        body,
        mesh=split,
        in_specs=placed,
        out_specs=(P(DP, None, GROUP), P(None, GROUP)),
        check_vma=False,
    )
```

time: 1080 us -> 206 us (0.19)
  the two profiles are of different devices: /device:TPU:64 before, /device:TPU:1 now
where the time goes in v1:
time: 206 us; the launch traced here: 202 us
  waiting for transfers between devices  79.1 us (38%)
  blocking collectives  44.2 us (21%)
  starting transfers between devices  40.7 us (20%)
  between operations  14.2 us (7%)
  Pallas kernels  12.3 us (6%)
  local copies, waits for them, and re-layouts  9.58 us (5%)
    all_to_all x1, blocking collectives, body(): terms = lax.all_to_all(terms, NEAR, 0, 0)  44.2 us
    all_gather x1, waiting for transfers between devices, body(): everything = lax.all_gather(own, GROUP, axis=0, tiled=True)  43.8 us
    all_to_all x2, waiting for transfers between devices, spread(): return lax.all_to_all(copies, axis, 0, 0)  20.8 us
    all_to_all x1, starting transfers between devices, body(): terms = lax.all_to_all(terms, FAR, 0, 0)  17.9 us
    all_to_all x1, waiting for transfers between devices, body(): terms = lax.all_to_all(terms, FAR, 0, 0)  12.6 us
    ppermute x1, starting transfers between devices, body(): other = lax.ppermute(mine, 'zh', [(0, 1), (1, 0)])  11.5 us
    all_to_all x2, starting transfers between devices, spread(): return lax.all_to_all(copies, axis, 0, 0)  11.3 us
    pallas_call x1, Pallas kernels, gram(): pl.pallas_call(gram_kernel, grid_spec=pltpu.PrefetchScalarGridSpec(num_sc...  6.91 us
  transfers between devices with their start and end apart: 5, of which 4 were waited for; matrix products, arithmetic and copies ran while one was open for 2% of the time, Pallas kernels for 6%

profile of v1, /device:TPU:1, one launch (start us, length us, event | category | flops | bytes accessed | tf_op | source)
XLA Modules:
  0.0 202.1 jit_solution(10213915404019885702)
XLA Ops:
  7.2 0.0 copy-start
  7.2 0.0 all-gather.2.cloned.1.call-start
  7.2 0.0 copy-start.4
  7.2 0.0 copy-start.3
  7.2 0.7 all-gather.2.cloned.1.call-update
  7.9 0.7 copy-done
  8.6 1.3 convolution_convert_fusion
  10.0 11.5 %collective-permute-start = (bf16[48,384]{1,0:T(8,128)(2,1)S(1)}, bf16[48,384]{1,0:T(8,128)(2,1)S(1)}, u32[]{:S(2)}, u32[]{:S(2)}) collective-permute-start(bf16[48,384]{1,0:T(8,128)(2,1)S(1)} %convolution_convert_fusion), channel_id=1, source_target_pairs={{0,256},{256,0},{1,257},{257,1},{2,258},{258,2},{3,259},{259,3},{4... | collective-permute-start | bytes 110600 | tf_op jit(solution)/shard_map/ppermute | solution.py:116
  21.5 1.3 collective-permute-done
  22.8 0.9 broadcast_in_dim.24
  23.7 6.8 %all-to-all-start.2 = ((bf16[8,96,384]{2,1,0:T(8,128)(2,1)}), bf16[8,96,384]{2,1,0:T(8,128)(2,1)S(1)}, u32[]{:S(2)}, u32[]{:S(2)}) async-start(bf16[8,96,384]{2,1,0:T(8,128)(2,1)} %broadcast_in_dim.24), calls=%async_computation.2 | async-start | bytes 1179648 | tf_op jit(solution)/shard_map/all_to_all | solution.py:99
  30.5 0.0 copy-done.4
  30.6 0.9 scatter_custom_fusion
  31.4 0.2 reshape.63
  31.6 0.1 reshape.64.tile_of
  31.8 43.8 %all-gather.2.cloned.1.call-done = bf16[2304,1024]{1,0:T(8,128)(2,1)} async-done(((bf16[288,1024]{1,0:T(8,128)(2,1)}), bf16[2304,1024]{1,0:T(8,128)(2,1)}) %all-gather.2.cloned.1.call-update) | async-done | bytes 4718608 | tf_op jit(solution)/shard_map/all_gather | solution.py:111
  75.6 0.0 copy-done.3
  75.6 6.9 %shard_map.59 = f32[8,288,384]{2,1,0:T(8,128)S(1)} custom-call(s32[128]{0:T(128)S(1)} %reshape.64.tile_of, bf16[288,1024]{1,0:T(8,128)(2,1)S(1)} %bitcast.18, bf16[96,24,1024]{2,1,0:T(8,128)(2,1)} %bitcast.19), custom_call_target="tpu_custom_call" | custom-call | tf_op jit(solution)/shard_map/pallas_call | solution.py:36
  82.5 0.0 copy-start.1
  82.5 1.8 copy-done.1
  84.3 0.0 all-to-all-done.2
  84.3 44.2 %all_to_all.20.parts_ref = f32[8,288,384]{2,1,0:T(8,128)} all-to-all(f32[8,288,384]{2,1,0:T(8,128)} %copy-done.1), channel_id=1, replica_groups=mesh['zh'=2,'x'=4,'yh'=4,'yl'=2,'zl'=4,'c'=2] {'x','yl'}, dimensions={0} | all-to-all | bytes 7077888 | tf_op jit(solution)/shard_map/all_to_all | solution.py:135
  128.4 1.6 broadcast_in_dim.26
  130.0 4.5 %all-to-all-start.3 = ((bf16[4,768,384]{2,1,0:T(8,128)(2,1)}), bf16[4,768,384]{2,1,0:T(8,128)(2,1)}, u32[]{:S(2)}, u32[]{:S(2)}) async-start(bf16[4,768,384]{2,1,0:T(8,128)(2,1)} %broadcast_in_dim.26), calls=%async_computation.3 | async-start | bytes 4718592 | tf_op jit(solution)/shard_map/all_to_all | solution.py:99
  134.5 0.0 copy-start.2
  134.6 2.0 copy-done.2
  136.5 1.8 shard_map.60
  138.4 20.8 %all-to-all-done.3 = bf16[4,768,384]{2,1,0:T(8,128)(2,1)} async-done(((bf16[4,768,384]{2,1,0:T(8,128)(2,1)}), bf16[4,768,384]{2,1,0:T(8,128)(2,1)}, u32[]{:S(2)}, u32[]{:S(2)}) %all-to-all-start.3) | async-done | bytes 2359328 | tf_op jit(solution)/shard_map/all_to_all | solution.py:99
  159.1 17.9 %all-to-all-start.1 = ((f32[8,48,288]{2,1,0:T(8,128)}), f32[8,48,288]{2,1,0:T(8,128)S(1)}, u32[]{:S(2)}, u32[]{:S(2)}) async-start(f32[8,48,288]{2,1,0:T(8,128)} %bitcast.3), calls=%async_computation.1 | async-start | bytes 1179648 | tf_op jit(solution)/shard_map/all_to_all | solution.py:137
  177.0 0.1 reshape.76
  177.2 1.2 gather_fusion
  178.4 3.6 %shard_map.61 = bf16[2304,384]{1,0:T(8,128)(2,1)} custom-call(s32[96]{0:T(128)S(1)} %gather_fusion, bf16[128,24,384]{2,1,0:T(8,128)(2,1)} %bitcast.10.rows_ref), custom_call_target="tpu_custom_call" | custom-call | tf_op jit(solution)/shard_map/pallas_call | solution.py:84
  182.0 12.6 %all-to-all-done.1 = f32[8,48,288]{2,1,0:T(8,128)S(1)} async-done(((f32[8,48,288]{2,1,0:T(8,128)}), f32[8,48,288]{2,1,0:T(8,128)S(1)}, u32[]{:S(2)}, u32[]{:S(2)}) %all-to-all-start.1) | async-done | bytes 442400 | tf_op jit(solution)/shard_map/all_to_all | solution.py:137
  194.7 0.6 broadcast_multiply_fusion
  (8 shorter events, 0.1 us)
Async XLA Ops:
  7.2 1.5 copy-start
  7.2 68.4 %all-gather.2.cloned.1.call-start = ((), (), s32[]{:S(2)}) async-start(), calls=%async_computation.4 | async-start | bytes 5308416 | tf_op jit(solution)/shard_map/all_gather | solution.py:111
  7.2 23.3 %copy-start.4 = (s32[96]{0:T(128)S(1)}, s32[96]{0:T(128)}, u32[]{:S(2)}) copy-start(s32[96]{0:T(128)} %param.5) | copy-start | bytes 1156
  7.2 68.3 %copy-start.3 = (bf16[1024,288]{0,1:T(8,128)(2,1)S(1)}, bf16[1024,288]{0,1:T(8,128)(2,1)}, u32[]{:S(2)}) copy-start(bf16[1024,288]{0,1:T(8,128)(2,1)} %param.4) | copy-start | bytes 1769476
  10.0 12.8 %collective-permute-start = (bf16[48,384]{1,0:T(8,128)(2,1)S(1)}, bf16[48,384]{1,0:T(8,128)(2,1)S(1)}, u32[]{:S(2)}, u32[]{:S(2)}) collective-permute-start(bf16[48,384]{1,0:T(8,128)(2,1)S(1)} %convolution_convert_fusion), channel_id=1, source_target_pairs={{0,256},{256,0},{1,257},{257,1},{2,258},{258,2},{3,259},{259,3},{4... | collective-permute-start | bytes 110600 | tf_op jit(solution)/shard_map/ppermute | solution.py:116
  23.7 60.6 %all-to-all-start.2 = ((bf16[8,96,384]{2,1,0:T(8,128)(2,1)}), bf16[8,96,384]{2,1,0:T(8,128)(2,1)S(1)}, u32[]{:S(2)}, u32[]{:S(2)}) async-start(bf16[8,96,384]{2,1,0:T(8,128)(2,1)} %broadcast_in_dim.24), calls=%async_computation.2 | async-start | bytes 1179648 | tf_op jit(solution)/shard_map/all_to_all | solution.py:99
  82.5 1.8 copy-start.1
  130.0 29.1 %all-to-all-start.3 = ((bf16[4,768,384]{2,1,0:T(8,128)(2,1)}), bf16[4,768,384]{2,1,0:T(8,128)(2,1)}, u32[]{:S(2)}, u32[]{:S(2)}) async-start(bf16[4,768,384]{2,1,0:T(8,128)(2,1)} %broadcast_in_dim.26), calls=%async_computation.3 | async-start | bytes 4718592 | tf_op jit(solution)/shard_map/all_to_all | solution.py:99
  134.5 2.0 copy-start.2
  159.1 35.5 %all-to-all-start.1 = ((f32[8,48,288]{2,1,0:T(8,128)}), f32[8,48,288]{2,1,0:T(8,128)S(1)}, u32[]{:S(2)}, u32[]{:S(2)}) async-start(f32[8,48,288]{2,1,0:T(8,128)} %bitcast.3), calls=%async_computation.1 | async-start | bytes 1179648 | tf_op jit(solution)/shard_map/all_to_all | solution.py:137
Sparse Core Ops, SparseCore 0:
  10.1 65.4 all-gather.1

commit v2 on v1

v2 whole, which is shorter than its diff:
```python
import functools

import jax
import jax.numpy as jnp
from jax import lax
from jax.experimental import pallas as pl
from jax.experimental.pallas import tpu as pltpu
from jax.sharding import Mesh, PartitionSpec as P

DP = ("zh", "x", "yh", "yl")
GROUP = ("zl", "c")
NEAR = ("x", "yl")
FAR = ("yh", "zh")


def gram_kernel(table, all_ref, keep_ref, send_ref, cols_ref, rows_ref):
    runs, _, tile, tokens = all_ref.shape
    half = keep_ref.shape[1]
    slots = keep_ref.shape[2] // tile
    count = pl.num_programs(0) * slots
    dest = pl.program_id(0)

    def fetch(to_ref, pair, places):
        for run in range(runs):
            both = []
            for place in places:
                rows = all_ref[run, jnp.maximum(place, 0)].astype(jnp.float32)
                both.append(jnp.where(place >= 0, rows, 0.0))
            to_ref[2 * tile * pair : 2 * tile * (pair + 1), tokens * run : tokens * (run + 1)] = (
                jnp.concatenate(both).astype(jnp.bfloat16)
            )

    @pl.when(dest == 0)
    def _():
        per = half // tile
        for core in range(2):
            for pair in range(per // 2):
                start = table[count + core] + 2 * pair
                fetch(cols_ref, core * per // 2 + pair, (start, start + 1))

    for pair in range(slots // 2):
        at = dest * slots + 2 * pair
        fetch(rows_ref, pair, (table[at], table[at + 1]))
    terms = lax.dot_general(
        cols_ref[...], rows_ref[...], (((1,), (1,)), ((), ())), preferred_element_type=jnp.float32
    )
    keep_ref[0] = terms[:half]
    send_ref[0] = terms[half:]


def gram(table, everything, dests, slots, half):
    runs, count, tile, tokens = everything.shape
    lanes = slots // dests * tile
    out = jax.ShapeDtypeStruct((dests, half, lanes), jnp.float32)
    return pl.pallas_call(
        gram_kernel,
        grid_spec=pltpu.PrefetchScalarGridSpec(
            num_scalar_prefetch=1,
            grid=(dests,),
            in_specs=[pl.BlockSpec((runs, count, tile, tokens), lambda d, t: (0, 0, 0, 0))],
            out_specs=[pl.BlockSpec((1, half, lanes), lambda d, t: (d, 0, 0))] * 2,
            scratch_shapes=[
                pltpu.VMEM((2 * half, runs * tokens), jnp.bfloat16),
                pltpu.VMEM((lanes, runs * tokens), jnp.bfloat16),
            ],
        ),
        out_shape=[out, out],
        compiler_params=pltpu.CompilerParams(vmem_limit_bytes=48 * 2**20),
    )(table, everything)


def sum_turn_kernel(parts_ref, out_ref):
    total = parts_ref[0]
    for n in range(1, parts_ref.shape[0]):
        total = total + parts_ref[n]
    total = total.T
    dests = out_ref.shape[0]
    rows, cols = total.shape[0] // dests, total.shape[1]
    for dest in range(dests):
        mine = total[rows * dest : rows * (dest + 1)]
        out_ref[dest, :rows] = mine[:, :128]
        rest = [mine[8 * n : 8 * n + 8, 128:] for n in range(rows // 8)]
        rest.append(jnp.zeros((8, 128 - (cols - 128) * (rows // 8)), jnp.float32))
        out_ref[dest, rows:] = jnp.concatenate(rest, axis=1)


def sum_turn(parts, dests):
    n, cols, lanes = parts.shape
    return pl.pallas_call(
        sum_turn_kernel,
        out_shape=jax.ShapeDtypeStruct((dests, lanes // dests + 8, 128), jnp.float32),
        compiler_params=pltpu.CompilerParams(vmem_limit_bytes=32 * 2**20),
    )(parts)


def sum_join_kernel(scale, parts_ref, out_ref):
    held, tile, cols = out_ref.shape
    halves, rows = parts_ref.shape[1], held * tile
    extra = cols // halves - 128
    pieces = []
    for half in range(halves):
        total = parts_ref[0, half]
        for n in range(1, parts_ref.shape[0]):
            total = total + parts_ref[n, half]
        total = total * scale
        pieces.append(total[:rows])
        rest = total[rows:]
        pieces.append(
            jnp.concatenate([rest[:, extra * n : extra * (n + 1)] for n in range(rows // 8)])
        )
    joined = jnp.concatenate(pieces, axis=1)
    for slot in range(held):
        out_ref[slot] = joined[tile * slot : tile * (slot + 1)]


def sum_join(parts, held, tile, cols, scale):
    return pl.pallas_call(
        functools.partial(sum_join_kernel, scale),
        out_shape=jax.ShapeDtypeStruct((held, tile, cols), jnp.float32),
    )(parts)


def place_kernel(slot_of, rows_ref, out_ref):
    tile = rows_ref.shape[1]
    for pair in range(out_ref.shape[0] // (2 * tile)):
        both = [rows_ref[slot_of[2 * pair + n]].astype(jnp.float32) for n in range(2)]
        out_ref[2 * tile * pair : 2 * tile * (pair + 1), :] = jnp.concatenate(both).astype(
            out_ref.dtype
        )


def place(slot_of, rows):
    slots, tile, cols = rows.shape
    tiles = slot_of.shape[0]
    return pl.pallas_call(
        place_kernel,
        grid_spec=pltpu.PrefetchScalarGridSpec(
            num_scalar_prefetch=1,
            grid=(1,),
            in_specs=[pl.BlockSpec((slots, tile, cols), lambda i, s: (0, 0, 0))],
            out_specs=pl.BlockSpec((tiles * tile, cols), lambda i, s: (0, 0)),
        ),
        out_shape=jax.ShapeDtypeStruct((tiles * tile, cols), rows.dtype),
        compiler_params=pltpu.CompilerParams(vmem_limit_bytes=32 * 2**20),
    )(slot_of, rows)


def spread(rows, axis):
    copies = jnp.broadcast_to(rows[None], (lax.axis_size(axis),) + rows.shape)
    return lax.all_to_all(copies, axis, 0, 0)


def body(sampled, assignment, inverse_rows, gradient):
    n_zh, n_x, n_yh, n_yl = (lax.axis_size(name) for name in DP)
    held, tile, order = inverse_rows.shape
    tiles = assignment.shape[0]
    tokens, cols = sampled.shape
    width = gradient.shape[1]
    owners = n_zh * n_x * n_yh * n_yl

    core, run = lax.axis_index("c"), lax.axis_index("zl")
    upper = lax.axis_index("zh")
    own = sampled.T
    kept = lax.dynamic_slice(own, (0, core * (tokens // 2)), (cols, tokens // 2))
    swapped = lax.dynamic_slice(own, (0, (1 - core) * (tokens // 2)), (cols, tokens // 2))
    swapped = lax.ppermute(swapped, "c", [(0, 1), (1, 0)])
    everything = lax.all_gather(jnp.concatenate([kept, swapped]), ("zh", "zl"), axis=0, tiled=True)

    mine = jnp.dot(
        inverse_rows.reshape(held * tile, order), gradient, preferred_element_type=jnp.float32
    ).astype(jnp.bfloat16)
    other = lax.ppermute(mine, "zh", [(0, 1), (1, 0)])
    first = lax.axis_index("zh") == 0
    rows = jnp.stack([jnp.where(first, mine, other), jnp.where(first, other, mine)])
    rows = spread(rows.reshape(n_zh * held * tile, width), ("yh", "yl"))
    rows = rows.reshape(n_yh * n_yl * n_zh * held * tile, width)
    rows = spread(rows, "x").reshape(owners * held, tile, width)
    everything, rows = lax.optimization_barrier((everything, rows))
    place_of = jnp.arange(owners * held, dtype=jnp.int32).reshape(n_x, n_yh * n_yl, n_zh, held)
    slot_place = place_of.transpose(2, 0, 1, 3).reshape(-1)
    preconditioned = place(slot_place[assignment], rows)

    near, far = n_x * n_yl, n_yh * n_zh
    per = cols // tile
    index = jnp.arange(tiles, dtype=jnp.int32)
    place_of = index // (2 * per) * (2 * per) + index % per
    place_of = place_of + jnp.where(index // per % 2 == core, 0, per)
    table = jnp.full((owners * held,), -1, jnp.int32).at[assignment].set(place_of)
    table = table.reshape(n_zh, n_x, n_yh, n_yl, held).transpose(1, 3, 2, 0, 4).reshape(-1)
    start = run * (2 * per) + upper * (per // n_zh)
    table = jnp.concatenate([table, jnp.stack([start, start + per]).astype(jnp.int32)])
    half = cols // n_zh
    keep, send = gram(
        table, everything.reshape(n_zh, tiles, tile, tokens // 2), near, owners * held, half
    )
    terms = keep + lax.ppermute(send, "c", [(0, 1), (1, 0)])
    terms = lax.all_to_all(terms, NEAR, 0, 0)
    terms = lax.all_to_all(sum_turn(terms, far), FAR, 0, 0)
    terms = terms.reshape((n_yh, n_zh) + terms.shape[1:])
    factor_tiles = sum_join(terms, held, tile, cols, 1.0 / (tokens * owners))
    return factor_tiles, preconditioned


def solution(mesh):
    split = Mesh(mesh.devices.reshape(2, 4, 4, 2, 4, 2), DP + GROUP)
    placed = (P(DP, GROUP), P(), P(DP, None, None), P(None, GROUP))
    return jax.shard_map(
        body,
        mesh=split,
        in_specs=placed,
        out_specs=(P(DP, None, GROUP), P(None, GROUP)),
        check_vma=False,
    )
```

time: 206 us -> 156 us (0.76); the launches traced: 202 us -> 154 us
  waiting for transfers between devices: 79.1 us -> 40.1 us
  starting transfers between devices: 40.7 us -> 31.9 us
  local copies, waits for them, and re-layouts: 9.58 us -> 6.23 us
  blocking collectives: 44.2 us -> 46.8 us
    all_gather x1, waiting for transfers between devices: 43.8 us -> 0.01 us  [body(): lax.all_gather(jnp.concatenate([kept, swapped]), ('zh', 'zl'), axis=0, ti...]
    all_to_all x0 -> x1, blocking collectives: none -> 21.5 us  [spread(): return lax.all_to_all(copies, axis, 0, 0)]
    all_to_all x1, blocking collectives: 44.2 us -> 25.3 us  [body(): terms = lax.all_to_all(terms, NEAR, 0, 0)]
    ppermute x0 -> x2, starting transfers between devices: none -> 14.6 us  [the longest x1 8.79 us: body(): swapped = lax.ppermute(swapped, 'c', [(0, 1), (1, 0)])]
    all_to_all x1, starting transfers between devices: 17.9 us -> 7.37 us  [body(): terms = lax.all_to_all(sum_turn(terms, far), FAR, 0, 0)]
    all_to_all x2 -> x1, starting transfers between devices: 11.3 us -> 4.63 us  [spread(): return lax.all_to_all(copies, axis, 0, 0)]
    ppermute x1, starting transfers between devices: 11.5 us -> 5.26 us  [body(): other = lax.ppermute(mine, 'zh', [(0, 1), (1, 0)])]
    all_to_all x1, waiting for transfers between devices: 12.6 us -> 7.35 us  [body(): terms = lax.all_to_all(sum_turn(terms, far), FAR, 0, 0)]
  transfers between devices with their start and end apart: 5 -> 6, of which waited for: 4 -> 5; matrix products, arithmetic and copies ran while one was open for 2% -> 3% of each run, Pallas kernels for 6% -> 2%
where the time goes in v2:
time: 156 us; the launch traced here: 154 us
  blocking collectives  46.8 us (30%)
  waiting for transfers between devices  40.1 us (26%)
  starting transfers between devices  31.9 us (20%)
  between operations  14.2 us (9%)
  Pallas kernels  13.3 us (9%)
  local copies, waits for them, and re-layouts  6.23 us (4%)
    all_to_all x1, blocking collectives, body(): terms = lax.all_to_all(terms, NEAR, 0, 0)  25.3 us
    all_to_all x1, waiting for transfers between devices, spread(): return lax.all_to_all(copies, axis, 0, 0)  24.9 us
    all_to_all x1, blocking collectives, spread(): return lax.all_to_all(copies, axis, 0, 0)  21.5 us
    ppermute x1, starting transfers between devices, body(): swapped = lax.ppermute(swapped, 'c', [(0, 1), (1, 0)])  8.79 us
    all_to_all x1, starting transfers between devices, body(): terms = lax.all_to_all(sum_turn(terms, far), FAR, 0, 0)  7.37 us
    all_to_all x1, waiting for transfers between devices, body(): terms = lax.all_to_all(sum_turn(terms, far), FAR, 0, 0)  7.35 us
    pallas_call x1, Pallas kernels, gram(): pl.pallas_call(gram_kernel, grid_spec=pltpu.PrefetchScalarGridSpec(num_sc...  7.04 us
    ppermute x1, starting transfers between devices, body(): terms = keep + lax.ppermute(send, 'c', [(0, 1), (1, 0)])  5.79 us
  transfers between devices with their start and end apart: 6, of which 5 were waited for; matrix products, arithmetic and copies ran while one was open for 3% of the time, Pallas kernels for 2%

profile of v2, /device:TPU:1, one launch (start us, length us, event | category | flops | bytes accessed | tf_op | source)
XLA Modules:
  0.0 154.3 jit_solution(3103115235425524424)
XLA Ops:
  7.2 0.0 copy-start
  7.2 0.0 copy-start.2
  7.2 0.0 all-gather.2.cloned.1.call-start
  7.2 1.2 dynamic-slice_bitcast_fusion.1
  8.5 8.8 %collective-permute-start = (bf16[288,512]{1,0:T(8,128)(2,1)S(1)}, bf16[288,512]{1,0:T(8,128)(2,1)S(1)}, u32[]{:S(2)}, u32[]{:S(2)}) collective-permute-start(bf16[288,512]{1,0:T(8,128)(2,1)S(1)} %get-tuple-element.11), channel_id=1, source_target_pairs={{0,1},{1,0},{2,3},{3,2},{4,5},{5,4},{6,7},{7,6},{8,9},{9,8},{10,11... | collective-permute-start | bytes 884744 | tf_op jit(solution)/shard_map/ppermute | solution.py:166
  17.3 1.2 collective-permute-done
  18.5 0.9 pad_maximum_fusion
  19.3 0.0 all-gather.2.cloned.1.call-update
  19.3 0.0 copy-done
  19.3 0.0 copy-done.2
  19.3 0.4 convolution_convert_fusion
  19.7 5.3 %collective-permute-start.1 = (bf16[48,384]{1,0:T(8,128)(2,1)S(1)}, bf16[48,384]{1,0:T(8,128)(2,1)S(1)}, u32[]{:S(2)}, u32[]{:S(2)}) collective-permute-start(bf16[48,384]{1,0:T(8,128)(2,1)S(1)} %convolution_convert_fusion), channel_id=1, source_target_pairs={{0,256},{256,0},{1,257},{257,1},{2,258},{258,2},{3,259},{259,3},{4... | collective-permute-start | bytes 110600 | tf_op jit(solution)/shard_map/ppermute | solution.py:172
  25.0 3.3 %collective-permute-done.1 = bf16[48,384]{1,0:T(8,128)(2,1)S(1)} collective-permute-done((bf16[48,384]{1,0:T(8,128)(2,1)S(1)}, bf16[48,384]{1,0:T(8,128)(2,1)S(1)}, u32[]{:S(2)}, u32[]{:S(2)}) %collective-permute-start.1) | collective-permute-done | bytes 36896 | tf_op jit(solution)/shard_map/ppermute | solution.py:172
  28.4 0.1 broadcast_in_dim.28
  28.4 21.5 %all_to_all.20 = bf16[8,96,384]{2,1,0:T(8,128)(2,1)S(1)} all-to-all(bf16[8,96,384]{2,1,0:T(8,128)(2,1)S(1)} %broadcast_in_dim.28), channel_id=1, replica_groups=mesh['zh'=2,'x'=4,'yh'=4,'yl'=2,'zl'=4,'c'=2] {'yh','yl'}, dimensions={0} | all-to-all | bytes 1179648 | tf_op jit(solution)/shard_map/all_to_all | solution.py:150
  50.0 1.7 %broadcast_in_dim.30 = bf16[4,768,384]{2,1,0:T(8,128)(2,1)} broadcast(bf16[768,384]{1,0:T(8,128)(2,1)S(1)} %bitcast.23), dimensions={1,2} | broadcast | bytes 2949120 | tf_op jit(solution)/shard_map/broadcast_in_dim | solution.py:149
  51.7 0.0 copy-start.3
  51.7 4.6 %all-to-all-start.1 = ((bf16[4,768,384]{2,1,0:T(8,128)(2,1)}), bf16[4,768,384]{2,1,0:T(8,128)(2,1)}, u32[]{:S(2)}, u32[]{:S(2)}) async-start(bf16[4,768,384]{2,1,0:T(8,128)(2,1)} %broadcast_in_dim.30), calls=%async_computation.1 | async-start | bytes 4718592 | tf_op jit(solution)/shard_map/all_to_all | solution.py:150
  56.3 0.0 copy-done.3
  56.3 0.9 scatter_custom_fusion
  57.2 0.2 reshape.59
  57.4 0.1 reshape.60
  57.6 0.1 pad_add_fusion.table
  57.7 24.9 %all-to-all-done.1 = bf16[4,768,384]{2,1,0:T(8,128)(2,1)} async-done(((bf16[4,768,384]{2,1,0:T(8,128)(2,1)}), bf16[4,768,384]{2,1,0:T(8,128)(2,1)}, u32[]{:S(2)}, u32[]{:S(2)}) %all-to-all-start.1) | async-done | bytes 2359328 | tf_op jit(solution)/shard_map/all_to_all | solution.py:150
  82.6 0.0 all-gather.2.cloned.1.call-done
  82.6 7.0 %shard_map.59 = (f32[8,144,384]{2,1,0:T(8,128)S(1)}, f32[8,144,384]{2,1,0:T(8,128)S(1)}) custom-call(s32[130]{0:T(256)S(1)} %pad_add_fusion.table, bf16[2,96,24,512]{3,2,1,0:T(8,128)(2,1)} %bitcast.22), custom_call_target="tpu_custom_call" | custom-call | tf_op jit(solution)/shard_map/pallas_call | solution.py:55
  89.6 5.8 %collective-permute-start.2 = (f32[8,144,384]{2,1,0:T(8,128)S(1)}, f32[8,144,384]{2,1,0:T(8,128)S(1)}, u32[]{:S(2)}, u32[]{:S(2)}) collective-permute-start(f32[8,144,384]{2,1,0:T(8,128)S(1)} %get-tuple-element.8), channel_id=1, source_target_pairs={{0,1},{1,0},{2,3},{3,2},{4,5},{5,4},{6,7},{7,6},{8,9},{9,8},{10,11... | collective-permute-start | bytes 5308424 | tf_op jit(solution)/shard_map/ppermute | solution.py:196
  95.4 3.3 %collective-permute-done.2 = f32[8,144,384]{2,1,0:T(8,128)S(1)} collective-permute-done((f32[8,144,384]{2,1,0:T(8,128)S(1)}, f32[8,144,384]{2,1,0:T(8,128)S(1)}, u32[]{:S(2)}, u32[]{:S(2)}) %collective-permute-start.2) | collective-permute-done | bytes 1769504 | tf_op jit(solution)/shard_map/ppermute | solution.py:196
  98.7 0.3 add.58
  99.0 25.3 %all_to_all.21.parts_ref = f32[8,144,384]{2,1,0:T(8,128)S(1)} all-to-all(f32[8,144,384]{2,1,0:T(8,128)S(1)} %add.58), channel_id=1, replica_groups=mesh['zh'=2,'x'=4,'yh'=4,'yl'=2,'zl'=4,'c'=2] {'x','yl'}, dimensions={0} | all-to-all | bytes 3538944 | tf_op jit(solution)/shard_map/all_to_all | solution.py:197
  124.3 1.0 shard_map.60
  125.3 7.4 %all-to-all-start.3 = ((f32[8,56,128]{2,1,0:T(8,128)}), f32[8,56,128]{2,1,0:T(8,128)S(1)}, u32[]{:S(2)}, u32[]{:S(2)}) async-start(f32[8,56,128]{2,1,0:T(8,128)} %shard_map.60), calls=%async_computation.3 | async-start | bytes 458752 | tf_op jit(solution)/shard_map/all_to_all | solution.py:198
  132.7 0.1 reshape.74
  132.8 1.2 gather_fusion
  134.1 3.6 %shard_map.62 = bf16[2304,384]{1,0:T(8,128)(2,1)} custom-call(s32[96]{0:T(128)S(1)} %gather_fusion, bf16[128,24,384]{2,1,0:T(8,128)(2,1)} %bitcast.10.rows_ref), custom_call_target="tpu_custom_call" | custom-call | tf_op jit(solution)/shard_map/pallas_call | solution.py:135
  137.7 7.4 %all-to-all-done.3 = f32[8,56,128]{2,1,0:T(8,128)S(1)} async-done(((f32[8,56,128]{2,1,0:T(8,128)}), f32[8,56,128]{2,1,0:T(8,128)S(1)}, u32[]{:S(2)}, u32[]{:S(2)}) %all-to-all-start.3) | async-done | bytes 229408 | tf_op jit(solution)/shard_map/all_to_all | solution.py:198
  145.0 0.0 copy-start.1
  145.0 0.7 copy-done.1
  145.7 1.7 %shard_map.61 = f32[2,24,288]{2,1,0:T(8,128)} custom-call(f32[4,2,56,128]{3,2,1,0:T(8,128)} %bitcast.24), custom_call_target="tpu_custom_call" | custom-call | tf_op jit(solution)/shard_map/pallas_call | solution.py:117
  (6 shorter events, 0.1 us)
Async XLA Ops:
  7.2 12.2 %copy-start = (bf16[2304,384]{1,0:T(8,128)(2,1)S(1)}, bf16[2304,384]{1,0:T(8,128)(2,1)}, u32[]{:S(2)}) copy-start(bf16[2304,384]{1,0:T(8,128)(2,1)} %param.7) | copy-start | bytes 5308420
  7.2 12.2 %copy-start.2 = (bf16[2,24,2304]{2,1,0:T(8,128)(2,1)S(1)}, bf16[2,24,2304]{2,1,0:T(8,128)(2,1)}, u32[]{:S(2)}) copy-start(bf16[2,24,2304]{2,1,0:T(8,128)(2,1)} %param.6) | copy-start | bytes 663556
  7.2 75.4 %all-gather.2.cloned.1.call-start = ((), (), s32[]{:S(2)}) async-start(), calls=%async_computation.4 | async-start | bytes 5308416 | tf_op jit(solution)/shard_map/all_gather | solution.py:167
  8.5 10.0 %collective-permute-start = (bf16[288,512]{1,0:T(8,128)(2,1)S(1)}, bf16[288,512]{1,0:T(8,128)(2,1)S(1)}, u32[]{:S(2)}, u32[]{:S(2)}) collective-permute-start(bf16[288,512]{1,0:T(8,128)(2,1)S(1)} %get-tuple-element.11), channel_id=1, source_target_pairs={{0,1},{1,0},{2,3},{3,2},{4,5},{5,4},{6,7},{7,6},{8,9},{9,8},{10,11... | collective-permute-start | bytes 884744 | tf_op jit(solution)/shard_map/ppermute | solution.py:166
  19.7 8.6 %collective-permute-start.1 = (bf16[48,384]{1,0:T(8,128)(2,1)S(1)}, bf16[48,384]{1,0:T(8,128)(2,1)S(1)}, u32[]{:S(2)}, u32[]{:S(2)}) collective-permute-start(bf16[48,384]{1,0:T(8,128)(2,1)S(1)} %convolution_convert_fusion), channel_id=1, source_target_pairs={{0,256},{256,0},{1,257},{257,1},{2,258},{258,2},{3,259},{259,3},{4... | collective-permute-start | bytes 110600 | tf_op jit(solution)/shard_map/ppermute | solution.py:172
  51.7 4.6 %copy-start.3 = (s32[96]{0:T(128)S(1)}, s32[96]{0:T(128)}, u32[]{:S(2)}) copy-start(s32[96]{0:T(128)} %param.5) | copy-start | bytes 1156
  51.7 30.9 %all-to-all-start.1 = ((bf16[4,768,384]{2,1,0:T(8,128)(2,1)}), bf16[4,768,384]{2,1,0:T(8,128)(2,1)}, u32[]{:S(2)}, u32[]{:S(2)}) async-start(bf16[4,768,384]{2,1,0:T(8,128)(2,1)} %broadcast_in_dim.30), calls=%async_computation.1 | async-start | bytes 4718592 | tf_op jit(solution)/shard_map/all_to_all | solution.py:150
  89.6 9.1 %collective-permute-start.2 = (f32[8,144,384]{2,1,0:T(8,128)S(1)}, f32[8,144,384]{2,1,0:T(8,128)S(1)}, u32[]{:S(2)}, u32[]{:S(2)}) collective-permute-start(f32[8,144,384]{2,1,0:T(8,128)S(1)} %get-tuple-element.8), channel_id=1, source_target_pairs={{0,1},{1,0},{2,3},{3,2},{4,5},{5,4},{6,7},{7,6},{8,9},{9,8},{10,11... | collective-permute-start | bytes 5308424 | tf_op jit(solution)/shard_map/ppermute | solution.py:196
  125.3 19.7 %all-to-all-start.3 = ((f32[8,56,128]{2,1,0:T(8,128)}), f32[8,56,128]{2,1,0:T(8,128)S(1)}, u32[]{:S(2)}, u32[]{:S(2)}) async-start(f32[8,56,128]{2,1,0:T(8,128)} %shard_map.60), calls=%async_computation.3 | async-start | bytes 458752 | tf_op jit(solution)/shard_map/all_to_all | solution.py:198
  145.0 0.7 copy-start.1
Sparse Core Ops, SparseCore 0:
  19.4 62.1 all-gather.1

commit v3 on v2

v3 whole, which is shorter than its diff:
```python
import functools

import jax
import jax.numpy as jnp
from jax import lax
from jax.experimental import pallas as pl
from jax.experimental.pallas import tpu as pltpu
from jax.sharding import Mesh, PartitionSpec as P

DP = ("zh", "x", "yh", "yl")
GROUP = ("zl", "c")
NEAR = ("x", "yl")
FAR = ("yh", "zh")


def gram_kernel(table, slots, own_ref, twin_ref, far_twin_ref, *refs):
    *others, keep_ref, send_ref, factors_ref, keep_sum, send_sum = refs
    blocks = [own_ref] + others
    far_ref = others[3]
    cols = own_ref.shape[0]
    share = keep_sum.shape[1]
    dest = pl.program_id(0)
    pairs = slots // 2
    tile = 24
    high = keep_ref.shape[1] // pairs
    count = pl.num_programs(0) * slots

    @pl.when(dest == 0)
    def _():
        start = pl.multiple_of(table[count], 16)
        mine = pl.ds(start, share)
        factors_ref[0, 0] = own_ref[mine, :]
        factors_ref[0, 1] = far_ref[mine, :]
        factors_ref[1, 0] = twin_ref[mine, :]
        factors_ref[1, 1] = far_twin_ref[mine, :]
        keep_sum[...] = jnp.zeros_like(keep_sum)
        send_sum[...] = jnp.zeros_like(send_sum)
        for n, block in enumerate(blocks):
            at = pl.ds(pl.multiple_of(table[count + 1 + 2 * n], 8), cols)
            which = table[count + 2 + 2 * n]
            for part, total in enumerate((keep_sum, send_sum)):
                total[at, :] += lax.dot_general(
                    block[...],
                    factors_ref[part, which],
                    (((1,), (1,)), ((), ())),
                    preferred_element_type=jnp.float32,
                )

    for total, out_ref in ((keep_sum, keep_ref), (send_sum, send_ref)):
        for pair in range(pairs):
            both = []
            for n in range(2):
                t = table[dest * slots + 2 * pair + n]
                rows = total[pl.ds(pl.multiple_of(jnp.maximum(t, 0) * tile, 8), tile), :]
                both.append(jnp.where(t >= 0, rows, 0.0))
            out_ref[0, high * pair : high * (pair + 1), :] = pack(jnp.concatenate(both))


def pack(rows):
    n, cols = rows.shape
    rest = [rows[8 * k : 8 * k + 8, 128:] for k in range(n // 8)]
    rest.append(jnp.zeros((8, 128 - (cols - 128) * (n // 8)), rows.dtype))
    return jnp.concatenate([rows[:, :128], jnp.concatenate(rest, axis=1)])


def gram(table, own, twin, far_twin, others, dests, slots, tile, share):
    cols, tokens = own.shape
    order = 8 * cols
    high = 2 * tile + 8
    out = jax.ShapeDtypeStruct((dests, slots // 2 * high, 128), jnp.float32)
    given = [own, twin, far_twin, *others]
    return pl.pallas_call(
        lambda table_ref, *refs: gram_kernel(table_ref, slots, *refs),
        grid_spec=pltpu.PrefetchScalarGridSpec(
            num_scalar_prefetch=1,
            grid=(dests,),
            in_specs=[pl.BlockSpec((cols, tokens), lambda d, t: (0, 0))] * len(given),
            out_specs=[pl.BlockSpec((1,) + out.shape[1:], lambda d, t: (d, 0, 0))] * 2,
            scratch_shapes=[
                pltpu.VMEM((2, 2, share, tokens), jnp.bfloat16),
                pltpu.VMEM((order, share), jnp.float32),
                pltpu.VMEM((order, share), jnp.float32),
            ],
        ),
        out_shape=[out, out],
        compiler_params=pltpu.CompilerParams(vmem_limit_bytes=56 * 2**20),
    )(table, *given)


def sum_join_kernel(scale, parts_ref, out_ref):
    held, tile, cols = out_ref.shape
    halves, rows = parts_ref.shape[1], held * tile
    extra = cols // halves - 128
    pieces = []
    for half in range(halves):
        total = parts_ref[0, half]
        for n in range(1, parts_ref.shape[0]):
            total = total + parts_ref[n, half]
        total = total * scale
        pieces.append(total[:rows])
        rest = total[rows:]
        pieces.append(
            jnp.concatenate([rest[:, extra * n : extra * (n + 1)] for n in range(rows // 8)])
        )
    joined = jnp.concatenate(pieces, axis=1)
    for slot in range(held):
        out_ref[slot] = joined[tile * slot : tile * (slot + 1)]


def sum_join(parts, held, tile, cols, scale):
    return pl.pallas_call(
        functools.partial(sum_join_kernel, scale),
        out_shape=jax.ShapeDtypeStruct((held, tile, cols), jnp.float32),
    )(parts)


def place_kernel(slot_of, rows_ref, out_ref):
    tile = rows_ref.shape[1]
    for pair in range(out_ref.shape[0] // (2 * tile)):
        both = [rows_ref[slot_of[2 * pair + n]].astype(jnp.float32) for n in range(2)]
        out_ref[2 * tile * pair : 2 * tile * (pair + 1), :] = jnp.concatenate(both).astype(
            out_ref.dtype
        )


def place(slot_of, rows):
    slots, tile, cols = rows.shape
    tiles = slot_of.shape[0]
    return pl.pallas_call(
        place_kernel,
        grid_spec=pltpu.PrefetchScalarGridSpec(
            num_scalar_prefetch=1,
            grid=(1,),
            in_specs=[pl.BlockSpec((slots, tile, cols), lambda i, s: (0, 0, 0))],
            out_specs=pl.BlockSpec((tiles * tile, cols), lambda i, s: (0, 0)),
        ),
        out_shape=jax.ShapeDtypeStruct((tiles * tile, cols), rows.dtype),
        compiler_params=pltpu.CompilerParams(vmem_limit_bytes=32 * 2**20),
    )(slot_of, rows)


def spread(rows, axis):
    copies = jnp.broadcast_to(rows[None], (lax.axis_size(axis),) + rows.shape)
    return lax.all_to_all(copies, axis, 0, 0)


def body(sampled, assignment, inverse_rows, gradient):
    n_zh, n_x, n_yh, n_yl = (lax.axis_size(name) for name in DP)
    held, tile, order = inverse_rows.shape
    tiles = assignment.shape[0]
    tokens, cols = sampled.shape
    width = gradient.shape[1]
    owners = n_zh * n_x * n_yh * n_yl

    ring = n_zh * lax.axis_size("zl")
    hops = [(2 * r, 2 * ((r + 1) % ring)) for r in range(ring)]
    hops += [(2 * r + 1, 2 * ((r - 1) % ring) + 1) for r in range(ring)]
    swap = [(0, 1), (1, 0)]

    def hop(block):
        return lax.ppermute(block, ("zh", "zl", "c"), hops)

    own = sampled.T
    twin = lax.ppermute(own, "c", swap)
    same, cross = [own], [twin]
    for step in range(ring // 2):
        same.append(hop(same[-1]))
        if step < ring // 2 - 1:
            cross.append(hop(cross[-1]))
    far_twin = lax.ppermute(same[-1], "c", swap)

    mine = jnp.dot(
        inverse_rows.reshape(held * tile, order), gradient, preferred_element_type=jnp.float32
    ).astype(jnp.bfloat16)
    other = lax.ppermute(mine, "zh", [(0, 1), (1, 0)])
    first = lax.axis_index("zh") == 0
    rows = jnp.stack([jnp.where(first, mine, other), jnp.where(first, other, mine)])
    rows = spread(rows.reshape(n_zh * held * tile, width), ("yh", "yl"))
    rows = rows.reshape(n_yh * n_yl * n_zh * held * tile, width)
    rows = spread(rows, "x").reshape(owners * held, tile, width)
    far_twin, rows = lax.optimization_barrier((far_twin, rows))
    place_of = jnp.arange(owners * held, dtype=jnp.int32).reshape(n_x, n_yh * n_yl, n_zh, held)
    slot_place = place_of.transpose(2, 0, 1, 3).reshape(-1)
    preconditioned = place(slot_place[assignment], rows)

    near, far = n_x * n_yl, n_yh * n_zh
    index = jnp.arange(tiles, dtype=jnp.int32)
    table = jnp.full((owners * held,), -1, jnp.int32).at[assignment].set(index)
    table = table.reshape(n_zh, n_x, n_yh, n_yl, held).transpose(1, 3, 2, 0, 4).reshape(-1)
    core, upper = lax.axis_index("c"), lax.axis_index("zh")
    here = upper * (ring // n_zh) + lax.axis_index("zl")
    share = cols // n_zh
    more = [upper * share]
    for steps, side in [(n, core) for n in range(ring // 2 + 1)] + [
        (n, 1 - core) for n in range(1, ring // 2)
    ]:
        chip = (here + jnp.where(core == 0, ring - steps, steps)) % ring
        row = (chip % (ring // n_zh) * 2 + side) * cols
        more += [row, (chip // (ring // n_zh) != upper).astype(jnp.int32)]
    table = jnp.concatenate([table, jnp.stack(more).astype(jnp.int32)])
    keep, send = gram(
        table, own, twin, far_twin, same[1:] + cross[1:], near, far * held, tile, share
    )
    terms = keep + lax.ppermute(send, "c", swap)
    terms = jnp.sum(lax.all_to_all(terms, NEAR, 0, 0), axis=0)
    terms = lax.all_to_all(terms.reshape(far, -1, terms.shape[1]), FAR, 0, 0)
    terms = terms.reshape((n_yh, n_zh) + terms.shape[1:])
    factor_tiles = sum_join(terms, held, tile, cols, 1.0 / (tokens * owners))
    return factor_tiles, preconditioned


def solution(mesh):
    split = Mesh(mesh.devices.reshape(2, 4, 4, 2, 4, 2), DP + GROUP)
    placed = (P(DP, GROUP), P(), P(DP, None, None), P(None, GROUP))
    return jax.shard_map(
        body,
        mesh=split,
        in_specs=placed,
        out_specs=(P(DP, None, GROUP), P(None, GROUP)),
        check_vma=False,
    )
```

time: 156 us -> 163 us (1.045)
  starting transfers between devices: 31.9 us -> 75.8 us
  blocking collectives: 46.8 us -> 27.6 us
  waiting for transfers between devices: 40.1 us -> 25 us
  between operations: 14.2 us -> 1.11 us
  local copies, waits for them, and re-layouts: 6.23 us -> 10.7 us
  other arithmetic: 1.28 us -> 4.11 us
  Pallas kernels: 13.3 us -> 15.6 us
    ppermute x2 -> x10, starting transfers between devices: 14.6 us -> 45.7 us  [the longest x7 30.5 us: hop(): return lax.ppermute(block, ('zh', 'zl', 'c'), hops)]
    all_to_all x1 -> x2, waiting for transfers between devices: 24.9 us -> 0.01 us  [spread(): return lax.all_to_all(copies, axis, 0, 0)]
    all_to_all x2 -> x1, blocking collectives: 46.8 us -> 27.6 us  [body(): terms = jnp.sum(lax.all_to_all(terms, NEAR, 0, 0), axis=0)]
    ppermute x2 -> x10, waiting for transfers between devices: 4.48 us -> 17.8 us  [the longest x7 14.2 us: hop(): return lax.ppermute(block, ('zh', 'zl', 'c'), hops)]
    all_to_all x1 -> x2, starting transfers between devices: 4.63 us -> 11.4 us  [spread(): return lax.all_to_all(copies, axis, 0, 0)]
    ppermute x1, starting transfers between devices: 5.26 us -> 11.5 us  [body(): other = lax.ppermute(mine, 'zh', [(0, 1), (1, 0)])]
    ppermute x1, waiting for transfers between devices: 3.33 us -> 0.01 us  [body(): other = lax.ppermute(mine, 'zh', [(0, 1), (1, 0)])]
    reduce_sum x0 -> x1, other arithmetic: none -> 2.33 us  [body(): terms = jnp.sum(lax.all_to_all(terms, NEAR, 0, 0), axis=0)]
  transfers between devices with their start and end apart: 6 -> 14, of which waited for: 5 -> 8; matrix products, arithmetic and copies ran while one was open for 3% -> 5% of each run, Pallas kernels for 2% -> 2%
where the time goes in v3:
time: 163 us; the launch traced here: 161 us
  starting transfers between devices  75.8 us (47%)
  blocking collectives  27.6 us (17%)
  waiting for transfers between devices  25 us (15%)
  Pallas kernels  15.6 us (10%)
  local copies, waits for them, and re-layouts  10.7 us (7%)
  other arithmetic  4.11 us (3%)
    ppermute x7, starting transfers between devices, hop(): return lax.ppermute(block, ('zh', 'zl', 'c'), hops)  30.5 us
    all_to_all x1, blocking collectives, body(): terms = jnp.sum(lax.all_to_all(terms, NEAR, 0, 0), axis=0)  27.6 us
    ppermute x7, waiting for transfers between devices, hop(): return lax.ppermute(block, ('zh', 'zl', 'c'), hops)  14.2 us
    ppermute x1, starting transfers between devices, body(): other = lax.ppermute(mine, 'zh', [(0, 1), (1, 0)])  11.5 us
    all_to_all x2, starting transfers between devices, spread(): return lax.all_to_all(copies, axis, 0, 0)  11.4 us
    pallas_call x1, Pallas kernels, gram(): pl.pallas_call(lambda table_ref, *refs: gram_kernel(table_ref, slots, *re...  10.3 us
    ppermute x1, starting transfers between devices, body(): terms = keep + lax.ppermute(send, 'c', swap)  7.25 us
    all_to_all x1, waiting for transfers between devices, body(): terms = lax.all_to_all(terms.reshape(far, -1, terms.shape[1]), FAR, 0, 0)  7.21 us
  transfers between devices with their start and end apart: 14, of which 8 were waited for; matrix products, arithmetic and copies ran while one was open for 5% of the time, Pallas kernels for 2%

profile of v3, /device:TPU:1, one launch (start us, length us, event | category | flops | bytes accessed | tf_op | source)
XLA Modules:
  0.0 161.2 jit_solution(2111544840203249461)
XLA Ops:
  0.6 0.0 copy-start
  0.6 0.0 copy-start.2
  0.7 1.5 copy-done
  2.1 1.3 convolution_convert_fusion
  3.4 11.5 %collective-permute-start.6 = (bf16[48,384]{1,0:T(8,128)(2,1)S(1)}, bf16[48,384]{1,0:T(8,128)(2,1)S(1)}, u32[]{:S(2)}, u32[]{:S(2)}) collective-permute-start(bf16[48,384]{1,0:T(8,128)(2,1)S(1)} %convolution_convert_fusion), channel_id=1, source_target_pairs={{0,256},{256,0},{1,257},{257,1},{2,258},{258,2},{3,259},{259,3},{4... | collective-permute-start | bytes 110600 | tf_op jit(solution)/shard_map/ppermute | solution.py:175
  14.9 0.0 copy-done.2
  14.9 2.0 %collective-permute-start.1 = (bf16[288,1024]{1,0:T(8,128)(2,1)S(1)}, bf16[288,1024]{1,0:T(8,128)(2,1)S(1)}, u32[]{:S(2)}, u32[]{:S(2)}) collective-permute-start(bf16[288,1024]{1,0:T(8,128)(2,1)S(1)} %bitcast.34), channel_id=1, source_target_pairs={{0,2},{2,4},{4,6},{6,256},{256,258},{258,260},{260,262},{262,0},{1... | collective-permute-start | bytes 1769480 | tf_op jit(solution)/shard_map/ppermute | solution.py:161
  16.9 0.0 collective-permute-done.6
  16.9 0.9 broadcast_in_dim.24
  17.8 6.8 %all-to-all-start = ((bf16[8,96,384]{2,1,0:T(8,128)(2,1)}), bf16[8,96,384]{2,1,0:T(8,128)(2,1)S(1)}, u32[]{:S(2)}, u32[]{:S(2)}) async-start(bf16[8,96,384]{2,1,0:T(8,128)(2,1)} %broadcast_in_dim.24), calls=%async_computation | async-start | bytes 1179648 | tf_op jit(solution)/shard_map/all_to_all | solution.py:144
  24.6 1.6 %collective-permute-done.1.refs_3_ = bf16[288,1024]{1,0:T(8,128)(2,1)S(1)} collective-permute-done((bf16[288,1024]{1,0:T(8,128)(2,1)S(1)}, bf16[288,1024]{1,0:T(8,128)(2,1)S(1)}, u32[]{:S(2)}, u32[]{:S(2)}) %collective-permute-start.1) | collective-permute-done | bytes 589856 | tf_op jit(solution)/shard_map/ppermute | solution.py:161
  26.2 0.0 copy-start.3
  26.3 5.1 %collective-permute-start.2 = (bf16[288,1024]{1,0:T(8,128)(2,1)S(1)}, bf16[288,1024]{1,0:T(8,128)(2,1)}, u32[]{:S(2)}, u32[]{:S(2)}) collective-permute-start(bf16[288,1024]{1,0:T(8,128)(2,1)S(1)} %collective-permute-done.1.refs_3_), channel_id=1, source_target_pairs={{0,2},{2,4},{4,6},{6,256},{256,258},{258,260},{260,262},{262,0},{1... | collective-permute-start | bytes 1769480 | tf_op jit(solution)/shard_map/ppermute | solution.py:161
  31.3 1.9 %collective-permute-start = (bf16[288,1024]{1,0:T(8,128)(2,1)S(1)}, bf16[288,1024]{1,0:T(8,128)(2,1)}, u32[]{:S(2)}, u32[]{:S(2)}) collective-permute-start(bf16[288,1024]{1,0:T(8,128)(2,1)S(1)} %bitcast.35), channel_id=1, source_target_pairs={{0,1},{1,0},{2,3},{3,2},{4,5},{5,4},{6,7},{7,6},{8,9},{9,8},{10,11... | collective-permute-start | bytes 1769480 | tf_op jit(solution)/shard_map/ppermute | solution.py:164
  33.3 4.9 %collective-permute-done.2.refs_4_ = bf16[288,1024]{1,0:T(8,128)(2,1)} collective-permute-done((bf16[288,1024]{1,0:T(8,128)(2,1)S(1)}, bf16[288,1024]{1,0:T(8,128)(2,1)}, u32[]{:S(2)}, u32[]{:S(2)}) %collective-permute-start.2) | collective-permute-done | bytes 589856 | tf_op jit(solution)/shard_map/ppermute | solution.py:161
  38.1 5.3 %collective-permute-start.3 = (bf16[288,1024]{1,0:T(8,128)(2,1)}, bf16[288,1024]{1,0:T(8,128)(2,1)}, u32[]{:S(2)}, u32[]{:S(2)}) collective-permute-start(bf16[288,1024]{1,0:T(8,128)(2,1)} %collective-permute-done.2.refs_4_), channel_id=1, source_target_pairs={{0,2},{2,4},{4,6},{6,256},{256,258},{258,260},{260,262},{262,0},{1... | collective-permute-start | bytes 1769480 | tf_op jit(solution)/shard_map/ppermute | solution.py:161
  43.5 0.0 all-to-all-done
  43.5 1.6 %broadcast_in_dim.26 = bf16[4,768,384]{2,1,0:T(8,128)(2,1)} broadcast(bf16[768,384]{1,0:T(8,128)(2,1)S(1)} %bitcast.31), dimensions={1,2} | broadcast | bytes 2949120 | tf_op jit(solution)/shard_map/broadcast_in_dim | solution.py:143
  45.1 0.0 copy-start.7
  45.1 0.0 copy-done.3
  45.1 4.6 %all-to-all-start.1 = ((bf16[4,768,384]{2,1,0:T(8,128)(2,1)}), bf16[4,768,384]{2,1,0:T(8,128)(2,1)}, u32[]{:S(2)}, u32[]{:S(2)}) async-start(bf16[4,768,384]{2,1,0:T(8,128)(2,1)} %broadcast_in_dim.26), calls=%async_computation.1 | async-start | bytes 4718592 | tf_op jit(solution)/shard_map/all_to_all | solution.py:144
  49.8 0.0 collective-permute-done.refs_1_
  49.8 4.9 %collective-permute-start.7 = (bf16[288,1024]{1,0:T(8,128)(2,1)}, bf16[288,1024]{1,0:T(8,128)(2,1)S(1)}, u32[]{:S(2)}, u32[]{:S(2)}) collective-permute-start(bf16[288,1024]{1,0:T(8,128)(2,1)} %collective-permute-done.refs_1_), channel_id=1, source_target_pairs={{0,2},{2,4},{4,6},{6,256},{256,258},{258,260},{260,262},{262,0},{1... | collective-permute-start | bytes 1769480 | tf_op jit(solution)/shard_map/ppermute | solution.py:161
  54.6 0.0 collective-permute-done.3.refs_5_
  54.7 2.6 %collective-permute-start.4 = (bf16[288,1024]{1,0:T(8,128)(2,1)}, bf16[288,1024]{1,0:T(8,128)(2,1)S(1)}, u32[]{:S(2)}, u32[]{:S(2)}) collective-permute-start(bf16[288,1024]{1,0:T(8,128)(2,1)} %collective-permute-done.3.refs_5_), channel_id=1, source_target_pairs={{0,2},{2,4},{4,6},{6,256},{256,258},{258,260},{260,262},{262,0},{1... | collective-permute-start | bytes 1769480 | tf_op jit(solution)/shard_map/ppermute | solution.py:161
  57.3 4.5 %collective-permute-done.7.refs_7_ = bf16[288,1024]{1,0:T(8,128)(2,1)S(1)} collective-permute-done((bf16[288,1024]{1,0:T(8,128)(2,1)}, bf16[288,1024]{1,0:T(8,128)(2,1)S(1)}, u32[]{:S(2)}, u32[]{:S(2)}) %collective-permute-start.7) | collective-permute-done | bytes 589856 | tf_op jit(solution)/shard_map/ppermute | solution.py:161
  61.8 0.0 copy-start.4
  61.8 5.3 %collective-permute-start.8 = (bf16[288,1024]{1,0:T(8,128)(2,1)S(1)}, bf16[288,1024]{1,0:T(8,128)(2,1)S(1)}, u32[]{:S(2)}, u32[]{:S(2)}) collective-permute-start(bf16[288,1024]{1,0:T(8,128)(2,1)S(1)} %collective-permute-done.7.refs_7_), channel_id=1, source_target_pairs={{0,2},{2,4},{4,6},{6,256},{256,258},{258,260},{260,262},{262,0},{1... | collective-permute-start | bytes 1769480 | tf_op jit(solution)/shard_map/ppermute | solution.py:161
  67.1 1.0 collective-permute-done.4.refs_6_
  68.1 0.0 copy-start.5
  68.1 5.9 %collective-permute-start.5 = (bf16[288,1024]{1,0:T(8,128)(2,1)S(1)}, bf16[288,1024]{1,0:T(8,128)(2,1)}, u32[]{:S(2)}, u32[]{:S(2)}) collective-permute-start(bf16[288,1024]{1,0:T(8,128)(2,1)S(1)} %collective-permute-done.4.refs_6_), channel_id=1, source_target_pairs={{0,1},{1,0},{2,3},{3,2},{4,5},{5,4},{6,7},{7,6},{8,9},{9,8},{10,11... | collective-permute-start | bytes 1769480 | tf_op jit(solution)/shard_map/ppermute | solution.py:170
  74.0 0.3 collective-permute-done.8.refs_8_
  74.3 0.0 copy-start.6
  74.3 5.4 %collective-permute-start.9 = (bf16[288,1024]{1,0:T(8,128)(2,1)S(1)}, bf16[288,1024]{1,0:T(8,128)(2,1)}, u32[]{:S(2)}, u32[]{:S(2)}) collective-permute-start(bf16[288,1024]{1,0:T(8,128)(2,1)S(1)} %collective-permute-done.8.refs_8_), channel_id=1, source_target_pairs={{0,2},{2,4},{4,6},{6,256},{256,258},{258,260},{260,262},{262,0},{1... | collective-permute-start | bytes 1769480 | tf_op jit(solution)/shard_map/ppermute | solution.py:161
  79.9 0.0 copy-done.7
  80.0 0.9 scatter_custom_fusion
  80.9 0.8 reshape.59
  81.6 1.4 copy.7
  83.0 0.9 reshape.60
  83.9 0.7 concatenate.3.table_ref
  84.6 0.0 all-to-all-done.1
  84.6 0.0 collective-permute-done.5.refs_2_
  84.6 1.9 %collective-permute-done.9.refs_9_ = bf16[288,1024]{1,0:T(8,128)(2,1)} collective-permute-done((bf16[288,1024]{1,0:T(8,128)(2,1)S(1)}, bf16[288,1024]{1,0:T(8,128)(2,1)}, u32[]{:S(2)}, u32[]{:S(2)}) %collective-permute-start.9) | collective-permute-done | bytes 589856 | tf_op jit(solution)/shard_map/ppermute | solution.py:161
  86.5 0.0 copy-done.4
  86.5 0.0 copy-done.5
  86.5 0.0 copy-done.6
  86.5 10.3 %shard_map.59 = (f32[8,448,128]{2,1,0:T(8,128)}, f32[8,448,128]{2,1,0:T(8,128)}) custom-call(s32[145]{0:T(256)} %concatenate.3.table_ref, bf16[288,1024]{1,0:T(8,128)(2,1)} %bitcast.33, bf16[288,1024]{1,0:T(8,128)(2,1)} %collective-permute-done.refs_1_, bf16[288,1024]{1,0:T(8,128)(2,1)} %collective-permute-done.5.refs_2_, bf16[288,1024]{1,0:T(8,128)(2,1)} %copy-done.3, ...), custom_call_target="tpu_custom_call" | custom-call | tf_op jit(solution)/shard_map/pallas_call | solution.py:72
  96.8 7.3 %collective-permute-start.10 = (f32[8,448,128]{2,1,0:T(8,128)}, f32[8,448,128]{2,1,0:T(8,128)S(1)}, u32[]{:S(2)}, u32[]{:S(2)}) collective-permute-start(f32[8,448,128]{2,1,0:T(8,128)} %get-tuple-element.8), channel_id=1, source_target_pairs={{0,1},{1,0},{2,3},{3,2},{4,5},{5,4},{6,7},{7,6},{8,9},{9,8},{10,11... | collective-permute-start | bytes 5505032 | tf_op jit(solution)/shard_map/ppermute | solution.py:204
  104.1 3.6 %collective-permute-done.10 = f32[8,448,128]{2,1,0:T(8,128)S(1)} collective-permute-done((f32[8,448,128]{2,1,0:T(8,128)}, f32[8,448,128]{2,1,0:T(8,128)S(1)}, u32[]{:S(2)}, u32[]{:S(2)}) %collective-permute-start.10) | collective-permute-done | bytes 1835040 | tf_op jit(solution)/shard_map/ppermute | solution.py:204
  107.7 1.7 %add.131 = f32[8,448,128]{2,1,0:T(8,128)S(1)} add(f32[8,448,128]{2,1,0:T(8,128)} %get-tuple-element.7, f32[8,448,128]{2,1,0:T(8,128)S(1)} %collective-permute-done.10) | non-fusion elementwise | flops 458752 | bytes 5505024 | tf_op jit(solution)/shard_map/add | solution.py:204
  109.4 27.6 %all_to_all.20 = f32[8,448,128]{2,1,0:T(8,128)} all-to-all(f32[8,448,128]{2,1,0:T(8,128)S(1)} %add.131), channel_id=1, replica_groups=mesh['zh'=2,'x'=4,'yh'=4,'yl'=2,'zl'=4,'c'=2] {'x','yl'}, dimensions={0} | all-to-all | bytes 3670016 | tf_op jit(solution)/shard_map/all_to_all | solution.py:205
  137.0 2.3 %reduce_sum.9 = f32[448,128]{1,0:T(8,128)} reduce(f32[8,448,128]{2,1,0:T(8,128)} %all_to_all.20, f32[]{:T(128)} %constant.147.clone.1), dimensions={0}, to_apply=%region_1.2 | reduce | flops 401408 | bytes 2064388 | tf_op jit(solution)/shard_map/reduce_sum | solution.py:205
  139.4 7.2 %all-to-all-start.3 = ((f32[8,56,128]{2,1,0:T(8,128)}), f32[8,56,128]{2,1,0:T(8,128)S(1)}, u32[]{:S(2)}, u32[]{:S(2)}) async-start(f32[8,56,128]{2,1,0:T(8,128)} %bitcast.22), calls=%async_computation.3 | async-start | bytes 458752 | tf_op jit(solution)/shard_map/all_to_all | solution.py:206
  146.6 0.1 reshape.74
  146.7 1.2 gather_fusion
  147.9 3.6 %shard_map.61 = bf16[2304,384]{1,0:T(8,128)(2,1)} custom-call(s32[96]{0:T(128)S(1)} %gather_fusion, bf16[128,24,384]{2,1,0:T(8,128)(2,1)} %bitcast.21.rows_ref), custom_call_target="tpu_custom_call" | custom-call | tf_op jit(solution)/shard_map/pallas_call | solution.py:129
  151.6 7.2 %all-to-all-done.3 = f32[8,56,128]{2,1,0:T(8,128)S(1)} async-done(((f32[8,56,128]{2,1,0:T(8,128)}), f32[8,56,128]{2,1,0:T(8,128)S(1)}, u32[]{:S(2)}, u32[]{:S(2)}) %all-to-all-start.3) | async-done | bytes 229408 | tf_op jit(solution)/shard_map/all_to_all | solution.py:206
  158.8 0.0 copy-start.1
  158.8 0.7 copy-done.1
  159.5 1.7 %shard_map.60 = f32[2,24,288]{2,1,0:T(8,128)} custom-call(f32[4,2,56,128]{3,2,1,0:T(8,128)} %bitcast.32), custom_call_target="tpu_custom_call" | custom-call | tf_op jit(solution)/shard_map/pallas_call | solution.py:111
  (6 shorter events, 0.0 us)
Async XLA Ops:
  0.6 1.5 copy-start
  0.6 14.3 %copy-start.2 = (bf16[1024,288]{0,1:T(8,128)(2,1)S(1)}, bf16[1024,288]{0,1:T(8,128)(2,1)}, u32[]{:S(2)}) copy-start(bf16[1024,288]{0,1:T(8,128)(2,1)} %param.4) | copy-start | bytes 1769476
  3.4 13.5 %collective-permute-start.6 = (bf16[48,384]{1,0:T(8,128)(2,1)S(1)}, bf16[48,384]{1,0:T(8,128)(2,1)S(1)}, u32[]{:S(2)}, u32[]{:S(2)}) collective-permute-start(bf16[48,384]{1,0:T(8,128)(2,1)S(1)} %convolution_convert_fusion), channel_id=1, source_target_pairs={{0,256},{256,0},{1,257},{257,1},{2,258},{258,2},{3,259},{259,3},{4... | collective-permute-start | bytes 110600 | tf_op jit(solution)/shard_map/ppermute | solution.py:175
  14.9 11.3 %collective-permute-start.1 = (bf16[288,1024]{1,0:T(8,128)(2,1)S(1)}, bf16[288,1024]{1,0:T(8,128)(2,1)S(1)}, u32[]{:S(2)}, u32[]{:S(2)}) collective-permute-start(bf16[288,1024]{1,0:T(8,128)(2,1)S(1)} %bitcast.34), channel_id=1, source_target_pairs={{0,2},{2,4},{4,6},{6,256},{256,258},{258,260},{260,262},{262,0},{1... | collective-permute-start | bytes 1769480 | tf_op jit(solution)/shard_map/ppermute | solution.py:161
  17.8 25.7 %all-to-all-start = ((bf16[8,96,384]{2,1,0:T(8,128)(2,1)}), bf16[8,96,384]{2,1,0:T(8,128)(2,1)S(1)}, u32[]{:S(2)}, u32[]{:S(2)}) async-start(bf16[8,96,384]{2,1,0:T(8,128)(2,1)} %broadcast_in_dim.24), calls=%async_computation | async-start | bytes 1179648 | tf_op jit(solution)/shard_map/all_to_all | solution.py:144
  26.2 18.9 %copy-start.3 = (bf16[288,1024]{1,0:T(8,128)(2,1)}, bf16[288,1024]{1,0:T(8,128)(2,1)S(1)}, u32[]{:S(2)}) copy-start(bf16[288,1024]{1,0:T(8,128)(2,1)S(1)} %collective-permute-done.1.refs_3_) | copy-start | bytes 1769476
  26.3 11.9 %collective-permute-start.2 = (bf16[288,1024]{1,0:T(8,128)(2,1)S(1)}, bf16[288,1024]{1,0:T(8,128)(2,1)}, u32[]{:S(2)}, u32[]{:S(2)}) collective-permute-start(bf16[288,1024]{1,0:T(8,128)(2,1)S(1)} %collective-permute-done.1.refs_3_), channel_id=1, source_target_pairs={{0,2},{2,4},{4,6},{6,256},{256,258},{258,260},{260,262},{262,0},{1... | collective-permute-start | bytes 1769480 | tf_op jit(solution)/shard_map/ppermute | solution.py:161
  31.3 18.4 %collective-permute-start = (bf16[288,1024]{1,0:T(8,128)(2,1)S(1)}, bf16[288,1024]{1,0:T(8,128)(2,1)}, u32[]{:S(2)}, u32[]{:S(2)}) collective-permute-start(bf16[288,1024]{1,0:T(8,128)(2,1)S(1)} %bitcast.35), channel_id=1, source_target_pairs={{0,1},{1,0},{2,3},{3,2},{4,5},{5,4},{6,7},{7,6},{8,9},{9,8},{10,11... | collective-permute-start | bytes 1769480 | tf_op jit(solution)/shard_map/ppermute | solution.py:164
  38.1 16.5 %collective-permute-start.3 = (bf16[288,1024]{1,0:T(8,128)(2,1)}, bf16[288,1024]{1,0:T(8,128)(2,1)}, u32[]{:S(2)}, u32[]{:S(2)}) collective-permute-start(bf16[288,1024]{1,0:T(8,128)(2,1)} %collective-permute-done.2.refs_4_), channel_id=1, source_target_pairs={{0,2},{2,4},{4,6},{6,256},{256,258},{258,260},{260,262},{262,0},{1... | collective-permute-start | bytes 1769480 | tf_op jit(solution)/shard_map/ppermute | solution.py:161
  45.1 34.8 %copy-start.7 = (s32[96]{0:T(128)S(1)}, s32[96]{0:T(128)}, u32[]{:S(2)}) copy-start(s32[96]{0:T(128)} %param.5) | copy-start | bytes 1156
  45.1 39.5 %all-to-all-start.1 = ((bf16[4,768,384]{2,1,0:T(8,128)(2,1)}), bf16[4,768,384]{2,1,0:T(8,128)(2,1)}, u32[]{:S(2)}, u32[]{:S(2)}) async-start(bf16[4,768,384]{2,1,0:T(8,128)(2,1)} %broadcast_in_dim.26), calls=%async_computation.1 | async-start | bytes 4718592 | tf_op jit(solution)/shard_map/all_to_all | solution.py:144
  49.8 12.0 %collective-permute-start.7 = (bf16[288,1024]{1,0:T(8,128)(2,1)}, bf16[288,1024]{1,0:T(8,128)(2,1)S(1)}, u32[]{:S(2)}, u32[]{:S(2)}) collective-permute-start(bf16[288,1024]{1,0:T(8,128)(2,1)} %collective-permute-done.refs_1_), channel_id=1, source_target_pairs={{0,2},{2,4},{4,6},{6,256},{256,258},{258,260},{260,262},{262,0},{1... | collective-permute-start | bytes 1769480 | tf_op jit(solution)/shard_map/ppermute | solution.py:161
  54.7 13.4 %collective-permute-start.4 = (bf16[288,1024]{1,0:T(8,128)(2,1)}, bf16[288,1024]{1,0:T(8,128)(2,1)S(1)}, u32[]{:S(2)}, u32[]{:S(2)}) collective-permute-start(bf16[288,1024]{1,0:T(8,128)(2,1)} %collective-permute-done.3.refs_5_), channel_id=1, source_target_pairs={{0,2},{2,4},{4,6},{6,256},{256,258},{258,260},{260,262},{262,0},{1... | collective-permute-start | bytes 1769480 | tf_op jit(solution)/shard_map/ppermute | solution.py:161
  61.8 24.8 %copy-start.4 = (bf16[288,1024]{1,0:T(8,128)(2,1)}, bf16[288,1024]{1,0:T(8,128)(2,1)S(1)}, u32[]{:S(2)}) copy-start(bf16[288,1024]{1,0:T(8,128)(2,1)S(1)} %collective-permute-done.7.refs_7_) | copy-start | bytes 1769476
  61.8 12.5 %collective-permute-start.8 = (bf16[288,1024]{1,0:T(8,128)(2,1)S(1)}, bf16[288,1024]{1,0:T(8,128)(2,1)S(1)}, u32[]{:S(2)}, u32[]{:S(2)}) collective-permute-start(bf16[288,1024]{1,0:T(8,128)(2,1)S(1)} %collective-permute-done.7.refs_7_), channel_id=1, source_target_pairs={{0,2},{2,4},{4,6},{6,256},{256,258},{258,260},{260,262},{262,0},{1... | collective-permute-start | bytes 1769480 | tf_op jit(solution)/shard_map/ppermute | solution.py:161
  68.1 18.4 %copy-start.5 = (bf16[288,1024]{1,0:T(8,128)(2,1)}, bf16[288,1024]{1,0:T(8,128)(2,1)S(1)}, u32[]{:S(2)}) copy-start(bf16[288,1024]{1,0:T(8,128)(2,1)S(1)} %collective-permute-done.4.refs_6_) | copy-start | bytes 1769476
  68.1 16.5 %collective-permute-start.5 = (bf16[288,1024]{1,0:T(8,128)(2,1)S(1)}, bf16[288,1024]{1,0:T(8,128)(2,1)}, u32[]{:S(2)}, u32[]{:S(2)}) collective-permute-start(bf16[288,1024]{1,0:T(8,128)(2,1)S(1)} %collective-permute-done.4.refs_6_), channel_id=1, source_target_pairs={{0,1},{1,0},{2,3},{3,2},{4,5},{5,4},{6,7},{7,6},{8,9},{9,8},{10,11... | collective-permute-start | bytes 1769480 | tf_op jit(solution)/shard_map/ppermute | solution.py:170
  74.3 12.2 %copy-start.6 = (bf16[288,1024]{1,0:T(8,128)(2,1)}, bf16[288,1024]{1,0:T(8,128)(2,1)S(1)}, u32[]{:S(2)}) copy-start(bf16[288,1024]{1,0:T(8,128)(2,1)S(1)} %collective-permute-done.8.refs_8_) | copy-start | bytes 1769476
  74.3 12.2 %collective-permute-start.9 = (bf16[288,1024]{1,0:T(8,128)(2,1)S(1)}, bf16[288,1024]{1,0:T(8,128)(2,1)}, u32[]{:S(2)}, u32[]{:S(2)}) collective-permute-start(bf16[288,1024]{1,0:T(8,128)(2,1)S(1)} %collective-permute-done.8.refs_8_), channel_id=1, source_target_pairs={{0,2},{2,4},{4,6},{6,256},{256,258},{258,260},{260,262},{262,0},{1... | collective-permute-start | bytes 1769480 | tf_op jit(solution)/shard_map/ppermute | solution.py:161
  96.8 10.9 %collective-permute-start.10 = (f32[8,448,128]{2,1,0:T(8,128)}, f32[8,448,128]{2,1,0:T(8,128)S(1)}, u32[]{:S(2)}, u32[]{:S(2)}) collective-permute-start(f32[8,448,128]{2,1,0:T(8,128)} %get-tuple-element.8), channel_id=1, source_target_pairs={{0,1},{1,0},{2,3},{3,2},{4,5},{5,4},{6,7},{7,6},{8,9},{9,8},{10,11... | collective-permute-start | bytes 5505032 | tf_op jit(solution)/shard_map/ppermute | solution.py:204
  139.4 19.4 %all-to-all-start.3 = ((f32[8,56,128]{2,1,0:T(8,128)}), f32[8,56,128]{2,1,0:T(8,128)S(1)}, u32[]{:S(2)}, u32[]{:S(2)}) async-start(f32[8,56,128]{2,1,0:T(8,128)} %bitcast.22), calls=%async_computation.3 | async-start | bytes 458752 | tf_op jit(solution)/shard_map/all_to_all | solution.py:206
  158.8 0.7 copy-start.1

commit v4 on v3

--- a/solution.py
+++ b/solution.py
@@ -9,51 +9,38 @@
 
 DP = ("zh", "x", "yh", "yl")
 GROUP = ("zl", "c")
-NEAR = ("x", "yl")
-FAR = ("yh", "zh")
-
-
-def gram_kernel(table, slots, own_ref, twin_ref, far_twin_ref, *refs):
-    *others, keep_ref, send_ref, factors_ref, keep_sum, send_sum = refs
-    blocks = [own_ref] + others
-    far_ref = others[3]
-    cols = own_ref.shape[0]
-    share = keep_sum.shape[1]
+Y = ("yh", "yl")
+
+
+def gram_kernel(table, slots, near_ref, far_ref, *refs):
+    *blocks, out_ref, total = refs
+    cols = near_ref.shape[0]
+    share = total.shape[1]
     dest = pl.program_id(0)
     pairs = slots // 2
-    tile = 24
-    high = keep_ref.shape[1] // pairs
+    high = out_ref.shape[1] // pairs
+    tile = (high - 8) // 2
     count = pl.num_programs(0) * slots
 
     @pl.when(dest == 0)
     def _():
-        start = pl.multiple_of(table[count], 16)
-        mine = pl.ds(start, share)
-        factors_ref[0, 0] = own_ref[mine, :]
-        factors_ref[0, 1] = far_ref[mine, :]
-        factors_ref[1, 0] = twin_ref[mine, :]
-        factors_ref[1, 1] = far_twin_ref[mine, :]
-        keep_sum[...] = jnp.zeros_like(keep_sum)
-        send_sum[...] = jnp.zeros_like(send_sum)
+        mine = pl.ds(pl.multiple_of(table[count], 16), share)
+        total[...] = jnp.zeros_like(total)
         for n, block in enumerate(blocks):
             at = pl.ds(pl.multiple_of(table[count + 1 + 2 * n], 8), cols)
-            which = table[count + 2 + 2 * n]
-            for part, total in enumerate((keep_sum, send_sum)):
-                total[at, :] += lax.dot_general(
-                    block[...],
-                    factors_ref[part, which],
-                    (((1,), (1,)), ((), ())),
-                    preferred_element_type=jnp.float32,
-                )
-
-    for total, out_ref in ((keep_sum, keep_ref), (send_sum, send_ref)):
-        for pair in range(pairs):
-            both = []
-            for n in range(2):
-                t = table[dest * slots + 2 * pair + n]
-                rows = total[pl.ds(pl.multiple_of(jnp.maximum(t, 0) * tile, 8), tile), :]
-                both.append(jnp.where(t >= 0, rows, 0.0))
-            out_ref[0, high * pair : high * (pair + 1), :] = pack(jnp.concatenate(both))
+            near = table[count + 2 + 2 * n] == 0
+            factor = jnp.where(near, near_ref[mine, :], far_ref[mine, :])
+            total[at, :] += lax.dot_general(
+                block[...], factor, (((1,), (1,)), ((), ())), preferred_element_type=jnp.float32
+            )
+
+    for pair in range(pairs):
+        both = []
+        for n in range(2):
+            t = table[dest * slots + 2 * pair + n]
+            rows = total[pl.ds(pl.multiple_of(jnp.maximum(t, 0) * tile, 8), tile), :]
+            both.append(jnp.where(t >= 0, rows, 0.0))
+        out_ref[0, high * pair : high * (pair + 1), :] = pack(jnp.concatenate(both))
 
 
 def pack(rows):
@@ -63,39 +50,34 @@
     return jnp.concatenate([rows[:, :128], jnp.concatenate(rest, axis=1)])
 
 
-def gram(table, own, twin, far_twin, others, dests, slots, tile, share):
-    cols, tokens = own.shape
-    order = 8 * cols
+def gram(table, near, far, blocks, dests, slots, tile, share):
+    cols, tokens = near.shape
     high = 2 * tile + 8
     out = jax.ShapeDtypeStruct((dests, slots // 2 * high, 128), jnp.float32)
-    given = [own, twin, far_twin, *others]
+    given = [near, far, *blocks]
     return pl.pallas_call(
         lambda table_ref, *refs: gram_kernel(table_ref, slots, *refs),
         grid_spec=pltpu.PrefetchScalarGridSpec(
             num_scalar_prefetch=1,
             grid=(dests,),
             in_specs=[pl.BlockSpec((cols, tokens), lambda d, t: (0, 0))] * len(given),
-            out_specs=[pl.BlockSpec((1,) + out.shape[1:], lambda d, t: (d, 0, 0))] * 2,
-            scratch_shapes=[
-                pltpu.VMEM((2, 2, share, tokens), jnp.bfloat16),
-                pltpu.VMEM((order, share), jnp.float32),
-                pltpu.VMEM((order, share), jnp.float32),
-            ],
+            out_specs=pl.BlockSpec((1,) + out.shape[1:], lambda d, t: (d, 0, 0)),
+            scratch_shapes=[pltpu.VMEM((len(blocks) * cols, share), jnp.float32)],
         ),
-        out_shape=[out, out],
-        compiler_params=pltpu.CompilerParams(vmem_limit_bytes=56 * 2**20),
+        out_shape=out,
+        compiler_params=pltpu.CompilerParams(vmem_limit_bytes=48 * 2**20),
     )(table, *given)
 
 
 def sum_join_kernel(scale, parts_ref, out_ref):
     held, tile, cols = out_ref.shape
-    halves, rows = parts_ref.shape[1], held * tile
+    halves, rows = parts_ref.shape[0], held * tile
     extra = cols // halves - 128
     pieces = []
     for half in range(halves):
-        total = parts_ref[0, half]
-        for n in range(1, parts_ref.shape[0]):
-            total = total + parts_ref[n, half]
+        total = parts_ref[half, 0]
+        for n in range(1, parts_ref.shape[1]):
+            total = total + parts_ref[half, n]
         total = total * scale
         pieces.append(total[:rows])
         rest = total[rows:]
@@ -175,18 +157,19 @@
     other = lax.ppermute(mine, "zh", [(0, 1), (1, 0)])
     first = lax.axis_index("zh") == 0
     rows = jnp.stack([jnp.where(first, mine, other), jnp.where(first, other, mine)])
-    rows = spread(rows.reshape(n_zh * held * tile, width), ("yh", "yl"))
+    rows = spread(rows.reshape(n_zh * held * tile, width), Y)
     rows = rows.reshape(n_yh * n_yl * n_zh * held * tile, width)
+    rows, cross[2] = lax.optimization_barrier((rows, cross[2]))
     rows = spread(rows, "x").reshape(owners * held, tile, width)
     far_twin, rows = lax.optimization_barrier((far_twin, rows))
     place_of = jnp.arange(owners * held, dtype=jnp.int32).reshape(n_x, n_yh * n_yl, n_zh, held)
     slot_place = place_of.transpose(2, 0, 1, 3).reshape(-1)
     preconditioned = place(slot_place[assignment], rows)
 
-    near, far = n_x * n_yl, n_yh * n_zh
+    n_y = n_yh * n_yl
     index = jnp.arange(tiles, dtype=jnp.int32)
     table = jnp.full((owners * held,), -1, jnp.int32).at[assignment].set(index)
-    table = table.reshape(n_zh, n_x, n_yh, n_yl, held).transpose(1, 3, 2, 0, 4).reshape(-1)
+    table = table.reshape(n_zh, n_x, n_y, held).transpose(1, 0, 2, 3).reshape(-1)
     core, upper = lax.axis_index("c"), lax.axis_index("zh")
     here = upper * (ring // n_zh) + lax.axis_index("zl")
     share = cols // n_zh
@@ -198,13 +181,14 @@
         row = (chip % (ring // n_zh) * 2 + side) * cols
         more += [row, (chip // (ring // n_zh) != upper).astype(jnp.int32)]
     table = jnp.concatenate([table, jnp.stack(more).astype(jnp.int32)])
-    keep, send = gram(
-        table, own, twin, far_twin, same[1:] + cross[1:], near, far * held, tile, share
-    )
-    terms = keep + lax.ppermute(send, "c", swap)
-    terms = jnp.sum(lax.all_to_all(terms, NEAR, 0, 0), axis=0)
-    terms = lax.all_to_all(terms.reshape(far, -1, terms.shape[1]), FAR, 0, 0)
-    terms = terms.reshape((n_yh, n_zh) + terms.shape[1:])
+    blocks = same + cross[1:]
+    sizes = (n_x, n_zh * n_y * held, tile, share)
+    send = gram(table, twin, far_twin, blocks, *sizes)
+    received = lax.ppermute(send, "c", swap)
+    terms = gram(table, own, same[-1], blocks, *sizes) + received
+    terms = jnp.sum(lax.all_to_all(terms, "x", 0, 0), axis=0)
+    terms = lax.all_to_all(terms.reshape(n_zh * n_y, -1, terms.shape[1]), ("zh",) + Y, 0, 0)
+    terms = terms.reshape((n_zh, n_y) + terms.shape[1:])
     factor_tiles = sum_join(terms, held, tile, cols, 1.0 / (tokens * owners))
     return factor_tiles, preconditioned
 

time: 163 us -> 164 us (level)
  starting transfers between devices: 75.8 us -> 70.1 us
  waiting for transfers between devices: 25 us -> 27.5 us
  Pallas kernels: 15.6 us -> 17.6 us
    ppermute x1, starting transfers between devices: 1.92 us -> 8.92 us  [body(): twin = lax.ppermute(own, 'c', swap)]
    ppermute x1, starting transfers between devices: 11.5 us -> 5.25 us  [body(): other = lax.ppermute(mine, 'zh', [(0, 1), (1, 0)])]
    ppermute x7, starting transfers between devices: 30.5 us -> 24.7 us  [hop(): return lax.ppermute(block, ('zh', 'zl', 'c'), hops)]
    ppermute x1, waiting for transfers between devices: 3.6 us -> 0.01 us  [body(): received = lax.ppermute(send, 'c', swap)]
    all_to_all x1, waiting for transfers between devices: 7.21 us -> 10.7 us  [body(): lax.all_to_all(terms.reshape(n_zh * n_y, -1, terms.shape[1]), ('zh',) + Y...]
    ppermute x1, starting transfers between devices: 7.25 us -> 3.97 us  [body(): received = lax.ppermute(send, 'c', swap)]
    ppermute x7, waiting for transfers between devices: 14.2 us -> 16.8 us  [hop(): return lax.ppermute(block, ('zh', 'zl', 'c'), hops)]
    pallas_call x1 -> x2, Pallas kernels: 10.3 us -> 12.2 us  [gram(): pl.pallas_call(lambda table_ref, *refs: gram_kernel(table_ref, slots, *re...]
  transfers between devices with their start and end apart: 14 -> 14, of which waited for: 8 -> 6; matrix products, arithmetic and copies ran while one was open for 5% -> 7% of each run, Pallas kernels for 2% -> 6%
where the time goes in v4:
time: 164 us; the launch traced here: 162 us
  starting transfers between devices  70.1 us (43%)
  blocking collectives  27.7 us (17%)
  waiting for transfers between devices  27.5 us (17%)
  Pallas kernels  17.6 us (11%)
  local copies, waits for them, and re-layouts  10.8 us (7%)
  other arithmetic  4.93 us (3%)
  matrix products  1.94 us (1%)
    all_to_all x1, blocking collectives, body(): terms = jnp.sum(lax.all_to_all(terms, 'x', 0, 0), axis=0)  27.7 us
    ppermute x7, starting transfers between devices, hop(): return lax.ppermute(block, ('zh', 'zl', 'c'), hops)  24.7 us
    ppermute x7, waiting for transfers between devices, hop(): return lax.ppermute(block, ('zh', 'zl', 'c'), hops)  16.8 us
    pallas_call x2, Pallas kernels, gram(): pl.pallas_call(lambda table_ref, *refs: gram_kernel(table_ref, slots, *re...  12.2 us
    all_to_all x2, starting transfers between devices, spread(): return lax.all_to_all(copies, axis, 0, 0)  11.5 us
    all_to_all x1, waiting for transfers between devices, body(): lax.all_to_all(terms.reshape(n_zh * n_y, -1, terms.shape[1]), ('zh',) + Y...  10.7 us
    ppermute x1, starting transfers between devices, body(): twin = lax.ppermute(own, 'c', swap)  8.92 us
    all_to_all x1, starting transfers between devices, body(): lax.all_to_all(terms.reshape(n_zh * n_y, -1, terms.shape[1]), ('zh',) + Y...  8.51 us
  transfers between devices with their start and end apart: 14, of which 6 were waited for; matrix products, arithmetic and copies ran while one was open for 7% of the time, Pallas kernels for 6%

profile of v4, /device:TPU:1, one launch (start us, length us, event | category | flops | bytes accessed | tf_op | source)
XLA Modules:
  0.0 161.7 jit_solution(2331023405391483546)
XLA Ops:
  0.6 0.0 copy-start
  0.6 0.0 copy-start.1
  0.7 8.9 %collective-permute-start.4 = (bf16[288,1024]{1,0:T(8,128)(2,1)}, bf16[288,1024]{1,0:T(8,128)(2,1)}, u32[]{:S(2)}, u32[]{:S(2)}) collective-permute-start(bf16[288,1024]{1,0:T(8,128)(2,1)} %bitcast.33), channel_id=1, source_target_pairs={{0,1},{1,0},{2,3},{3,2},{4,5},{5,4},{6,7},{7,6},{8,9},{9,8},{10,11... | collective-permute-start | bytes 1769480 | tf_op jit(solution)/shard_map/ppermute | solution.py:146
  9.6 0.0 copy-done
  9.6 1.9 %convolution_convert_fusion = bf16[48,384]{1,0:T(8,128)(2,1)} fusion(bf16[48,2304]{1,0:T(8,128)(2,1)} %bitcast.40, bf16[2304,384]{1,0:T(8,128)(2,1)S(1)} %copy-done), kind=kOutput, calls=%fused_computation.2 | convolution fusion | flops 84953088 | bytes 2027520 | tf_op jit(solution)/shard_map/dot_general | solution.py:154
  11.5 5.3 %collective-permute-start.6 = (bf16[48,384]{1,0:T(8,128)(2,1)}, bf16[48,384]{1,0:T(8,128)(2,1)}, u32[]{:S(2)}, u32[]{:S(2)}) collective-permute-start(bf16[48,384]{1,0:T(8,128)(2,1)} %convolution_convert_fusion), channel_id=1, source_target_pairs={{0,256},{256,0},{1,257},{257,1},{2,258},{258,2},{3,259},{259,3},{4... | collective-permute-start | bytes 110600 | tf_op jit(solution)/shard_map/ppermute | solution.py:157
  16.8 0.0 copy-done.1
  16.8 2.0 %collective-permute-start = (bf16[288,1024]{1,0:T(8,128)(2,1)S(1)}, bf16[288,1024]{1,0:T(8,128)(2,1)S(1)}, u32[]{:S(2)}, u32[]{:S(2)}) collective-permute-start(bf16[288,1024]{1,0:T(8,128)(2,1)S(1)} %bitcast.34), channel_id=1, source_target_pairs={{0,2},{2,4},{4,6},{6,256},{256,258},{258,260},{260,262},{262,0},{1... | collective-permute-start | bytes 1769480 | tf_op jit(solution)/shard_map/ppermute | solution.py:143
  18.8 0.0 collective-permute-done.4.refs_0_
  18.8 2.2 %collective-permute-start.5 = (bf16[288,1024]{1,0:T(8,128)(2,1)}, bf16[288,1024]{1,0:T(8,128)(2,1)S(1)}, u32[]{:S(2)}, u32[]{:S(2)}) collective-permute-start(bf16[288,1024]{1,0:T(8,128)(2,1)} %collective-permute-done.4.refs_0_), channel_id=1, source_target_pairs={{0,2},{2,4},{4,6},{6,256},{256,258},{258,260},{260,262},{262,0},{1... | collective-permute-start | bytes 1769480 | tf_op jit(solution)/shard_map/ppermute | solution.py:143
  21.0 0.0 collective-permute-done.6
  21.0 0.8 select_bitcast_fusion.1
  21.8 0.9 broadcast_in_dim.23
  22.7 6.8 %all-to-all-start = ((bf16[8,96,384]{2,1,0:T(8,128)(2,1)}), bf16[8,96,384]{2,1,0:T(8,128)(2,1)}, u32[]{:S(2)}, u32[]{:S(2)}) async-start(bf16[8,96,384]{2,1,0:T(8,128)(2,1)} %broadcast_in_dim.23), calls=%async_computation | async-start | bytes 1179648 | tf_op jit(solution)/shard_map/all_to_all | solution.py:126
  29.5 0.0 collective-permute-done.refs_3_
  29.5 4.8 %collective-permute-start.1 = (bf16[288,1024]{1,0:T(8,128)(2,1)S(1)}, bf16[288,1024]{1,0:T(8,128)(2,1)}, u32[]{:S(2)}, u32[]{:S(2)}) collective-permute-start(bf16[288,1024]{1,0:T(8,128)(2,1)S(1)} %collective-permute-done.refs_3_), channel_id=1, source_target_pairs={{0,2},{2,4},{4,6},{6,256},{256,258},{258,260},{260,262},{262,0},{1... | collective-permute-start | bytes 1769480 | tf_op jit(solution)/shard_map/ppermute | solution.py:143
  34.3 0.3 collective-permute-done.5.refs_7_
  34.7 0.0 copy-start.2
  34.7 3.0 %collective-permute-start.7 = (bf16[288,1024]{1,0:T(8,128)(2,1)S(1)}, bf16[288,1024]{1,0:T(8,128)(2,1)}, u32[]{:S(2)}, u32[]{:S(2)}) collective-permute-start(bf16[288,1024]{1,0:T(8,128)(2,1)S(1)} %collective-permute-done.5.refs_7_), channel_id=1, source_target_pairs={{0,2},{2,4},{4,6},{6,256},{256,258},{258,260},{260,262},{262,0},{1... | collective-permute-start | bytes 1769480 | tf_op jit(solution)/shard_map/ppermute | solution.py:143
  37.7 3.4 %collective-permute-done.1.refs_4_ = bf16[288,1024]{1,0:T(8,128)(2,1)} collective-permute-done((bf16[288,1024]{1,0:T(8,128)(2,1)S(1)}, bf16[288,1024]{1,0:T(8,128)(2,1)}, u32[]{:S(2)}, u32[]{:S(2)}) %collective-permute-start.1) | collective-permute-done | bytes 589856 | tf_op jit(solution)/shard_map/ppermute | solution.py:143
  41.1 5.4 %collective-permute-start.2 = (bf16[288,1024]{1,0:T(8,128)(2,1)}, bf16[288,1024]{1,0:T(8,128)(2,1)}, u32[]{:S(2)}, u32[]{:S(2)}) collective-permute-start(bf16[288,1024]{1,0:T(8,128)(2,1)} %collective-permute-done.1.refs_4_), channel_id=1, source_target_pairs={{0,2},{2,4},{4,6},{6,256},{256,258},{258,260},{260,262},{262,0},{1... | collective-permute-start | bytes 1769480 | tf_op jit(solution)/shard_map/ppermute | solution.py:143
  46.5 0.0 all-to-all-done
  46.6 0.9 collective-permute-done.7.refs_8_
  47.4 2.7 %broadcast_in_dim.24 = bf16[4,768,384]{2,1,0:T(8,128)(2,1)} broadcast(bf16[768,384]{1,0:T(8,128)(2,1)} %bitcast.20), dimensions={1,2} | broadcast | bytes 2949120 | tf_op jit(solution)/shard_map/broadcast_in_dim | solution.py:125
  50.1 0.0 copy-start.5
  50.1 0.0 copy-done.2
  50.1 4.6 %all-to-all-start.1 = ((bf16[4,768,384]{2,1,0:T(8,128)(2,1)}), bf16[4,768,384]{2,1,0:T(8,128)(2,1)}, u32[]{:S(2)}, u32[]{:S(2)}) async-start(bf16[4,768,384]{2,1,0:T(8,128)(2,1)} %broadcast_in_dim.24), calls=%async_computation.1 | async-start | bytes 4718592 | tf_op jit(solution)/shard_map/all_to_all | solution.py:126
  54.8 0.0 collective-permute-done.2.refs_5_
  54.8 5.4 %collective-permute-start.3 = (bf16[288,1024]{1,0:T(8,128)(2,1)}, bf16[288,1024]{1,0:T(8,128)(2,1)S(1)}, u32[]{:S(2)}, u32[]{:S(2)}) collective-permute-start(bf16[288,1024]{1,0:T(8,128)(2,1)} %collective-permute-done.2.refs_5_), channel_id=1, source_target_pairs={{0,2},{2,4},{4,6},{6,256},{256,258},{258,260},{260,262},{262,0},{1... | collective-permute-start | bytes 1769480 | tf_op jit(solution)/shard_map/ppermute | solution.py:143
  60.2 7.1 %collective-permute-done.3.refs_1_.refs_6_ = bf16[288,1024]{1,0:T(8,128)(2,1)S(1)} collective-permute-done((bf16[288,1024]{1,0:T(8,128)(2,1)}, bf16[288,1024]{1,0:T(8,128)(2,1)S(1)}, u32[]{:S(2)}, u32[]{:S(2)}) %collective-permute-start.3) | collective-permute-done | bytes 589856 | tf_op jit(solution)/shard_map/ppermute | solution.py:143
  67.3 7.2 %collective-permute-start.9 = (bf16[288,1024]{1,0:T(8,128)(2,1)S(1)}, bf16[288,1024]{1,0:T(8,128)(2,1)}, u32[]{:S(2)}, u32[]{:S(2)}) collective-permute-start(bf16[288,1024]{1,0:T(8,128)(2,1)S(1)} %collective-permute-done.3.refs_1_.refs_6_), channel_id=1, source_target_pairs={{0,1},{1,0},{2,3},{3,2},{4,5},{5,4},{6,7},{7,6},{8,9},{9,8},{10,11... | collective-permute-start | bytes 1769480 | tf_op jit(solution)/shard_map/ppermute | solution.py:152
  74.6 1.9 %collective-permute-start.8 = (bf16[288,1024]{1,0:T(8,128)(2,1)}, bf16[288,1024]{1,0:T(8,128)(2,1)}, u32[]{:S(2)}, u32[]{:S(2)}) collective-permute-start(bf16[288,1024]{1,0:T(8,128)(2,1)} %collective-permute-done.7.refs_8_), channel_id=1, source_target_pairs={{0,2},{2,4},{4,6},{6,256},{256,258},{258,260},{260,262},{262,0},{1... | collective-permute-start | bytes 1769480 | tf_op jit(solution)/shard_map/ppermute | solution.py:143
  76.7 0.0 copy-done.5
  76.8 0.9 scatter_custom_fusion
  77.6 0.8 reshape.62
  78.4 1.4 copy.7
  79.7 0.9 reshape.63
  80.6 0.1 concatenate.3.table_ref
  80.7 0.0 collective-permute-done.9.refs_1_
  80.8 0.0 all-to-all-done.1
  80.8 5.0 %collective-permute-done.8.refs_9_ = bf16[288,1024]{1,0:T(8,128)(2,1)} collective-permute-done((bf16[288,1024]{1,0:T(8,128)(2,1)}, bf16[288,1024]{1,0:T(8,128)(2,1)}, u32[]{:S(2)}, u32[]{:S(2)}) %collective-permute-start.8) | collective-permute-done | bytes 589856 | tf_op jit(solution)/shard_map/ppermute | solution.py:143
  85.8 0.0 copy-start.3
  85.8 1.1 copy-done.3
  86.9 6.3 %shard_map.60 = f32[4,896,128]{2,1,0:T(8,128)} custom-call(s32[145]{0:T(256)S(1)} %concatenate.3.table_ref, bf16[288,1024]{1,0:T(8,128)(2,1)} %collective-permute-done.4.refs_0_, bf16[288,1024]{1,0:T(8,128)(2,1)} %collective-permute-done.9.refs_1_, bf16[288,1024]{1,0:T(8,128)(2,1)S(1)} %bitcast.35, bf16[288,1024]{1,0:T(8,128)(2,1)S(1)} %collective-permute-done.refs_3_, ...), custom_call_target="tpu_custom_call" | custom-call | tf_op jit(solution)/shard_map/pallas_call | solution.py:58
  93.1 4.0 %collective-permute-start.10 = (f32[4,896,128]{2,1,0:T(8,128)}, f32[4,896,128]{2,1,0:T(8,128)S(1)}, u32[]{:S(2)}, u32[]{:S(2)}) collective-permute-start(f32[4,896,128]{2,1,0:T(8,128)} %shard_map.60), channel_id=1, source_target_pairs={{0,1},{1,0},{2,3},{3,2},{4,5},{5,4},{6,7},{7,6},{8,9},{9,8},{10,11... | collective-permute-start | bytes 5505032 | tf_op jit(solution)/shard_map/ppermute | solution.py:187
  97.1 5.9 %shard_map.59 = f32[4,896,128]{2,1,0:T(8,128)} custom-call(s32[145]{0:T(256)S(1)} %concatenate.3.table_ref, bf16[288,1024]{1,0:T(8,128)(2,1)S(1)} %bitcast.36, bf16[288,1024]{1,0:T(8,128)(2,1)S(1)} %collective-permute-done.3.refs_1_.refs_6_, bf16[288,1024]{1,0:T(8,128)(2,1)S(1)} %bitcast.37, bf16[288,1024]{1,0:T(8,128)(2,1)S(1)} %collective-permute-done.refs_3_, ...), custom_call_target="tpu_custom_call" | custom-call | tf_op jit(solution)/shard_map/pallas_call | solution.py:58
  103.0 0.0 collective-permute-done.10
  103.0 1.7 %add.131 = f32[4,896,128]{2,1,0:T(8,128)S(1)} add(f32[4,896,128]{2,1,0:T(8,128)} %shard_map.59, f32[4,896,128]{2,1,0:T(8,128)S(1)} %collective-permute-done.10) | non-fusion elementwise | flops 458752 | bytes 5505024 | tf_op jit(solution)/shard_map/add | solution.py:188
  104.7 27.7 %all_to_all.20 = f32[4,896,128]{2,1,0:T(8,128)} all-to-all(f32[4,896,128]{2,1,0:T(8,128)S(1)} %add.131), channel_id=1, replica_groups=mesh['zh'=2,'x'=4,'yh'=4,'yl'=2,'zl'=4,'c'=2] {'x'}, dimensions={0} | all-to-all | bytes 3670016 | tf_op jit(solution)/shard_map/all_to_all | solution.py:189
  132.5 2.4 %reduce_sum.9 = f32[896,128]{1,0:T(8,128)} reduce(f32[4,896,128]{2,1,0:T(8,128)} %all_to_all.20, f32[]{:T(128)} %constant.147.clone.1), dimensions={0}, to_apply=%region_1.2 | reduce | flops 344064 | bytes 2293764 | tf_op jit(solution)/shard_map/reduce_sum | solution.py:189
  134.9 8.5 %all-to-all-start.3 = ((f32[16,56,128]{2,1,0:T(8,128)}), f32[16,56,128]{2,1,0:T(8,128)S(1)}, u32[]{:S(2)}, u32[]{:S(2)}) async-start(f32[16,56,128]{2,1,0:T(8,128)} %bitcast.22), calls=%async_computation.3 | async-start | bytes 917504 | tf_op jit(solution)/shard_map/all_to_all | solution.py:190
  143.4 0.1 reshape.78
  143.6 1.2 gather_fusion
  144.8 3.6 %shard_map.62 = bf16[2304,384]{1,0:T(8,128)(2,1)} custom-call(s32[96]{0:T(128)S(1)} %gather_fusion, bf16[128,24,384]{2,1,0:T(8,128)(2,1)} %bitcast.21.rows_ref), custom_call_target="tpu_custom_call" | custom-call | tf_op jit(solution)/shard_map/pallas_call | solution.py:111
  148.4 10.7 %all-to-all-done.3 = f32[16,56,128]{2,1,0:T(8,128)S(1)} async-done(((f32[16,56,128]{2,1,0:T(8,128)}), f32[16,56,128]{2,1,0:T(8,128)S(1)}, u32[]{:S(2)}, u32[]{:S(2)}) %all-to-all-start.3) | async-done | bytes 458784 | tf_op jit(solution)/shard_map/all_to_all | solution.py:190
  159.1 0.0 copy-start.4
  159.1 0.8 copy-done.4
  159.9 1.8 %shard_map.61 = f32[2,24,288]{2,1,0:T(8,128)} custom-call(f32[2,8,56,128]{3,2,1,0:T(8,128)} %bitcast.38), custom_call_target="tpu_custom_call" | custom-call | tf_op jit(solution)/shard_map/pallas_call | solution.py:93
  (5 shorter events, 0.0 us)
Async XLA Ops:
  0.6 9.0 %copy-start = (bf16[2304,384]{1,0:T(8,128)(2,1)S(1)}, bf16[2304,384]{1,0:T(8,128)(2,1)}, u32[]{:S(2)}) copy-start(bf16[2304,384]{1,0:T(8,128)(2,1)} %param.7) | copy-start | bytes 5308420
  0.6 16.1 %copy-start.1 = (bf16[1024,288]{0,1:T(8,128)(2,1)S(1)}, bf16[1024,288]{0,1:T(8,128)(2,1)}, u32[]{:S(2)}) copy-start(bf16[1024,288]{0,1:T(8,128)(2,1)} %param.4) | copy-start | bytes 1769476
  0.7 18.1 %collective-permute-start.4 = (bf16[288,1024]{1,0:T(8,128)(2,1)}, bf16[288,1024]{1,0:T(8,128)(2,1)}, u32[]{:S(2)}, u32[]{:S(2)}) collective-permute-start(bf16[288,1024]{1,0:T(8,128)(2,1)} %bitcast.33), channel_id=1, source_target_pairs={{0,1},{1,0},{2,3},{3,2},{4,5},{5,4},{6,7},{7,6},{8,9},{9,8},{10,11... | collective-permute-start | bytes 1769480 | tf_op jit(solution)/shard_map/ppermute | solution.py:146
  11.5 9.4 %collective-permute-start.6 = (bf16[48,384]{1,0:T(8,128)(2,1)}, bf16[48,384]{1,0:T(8,128)(2,1)}, u32[]{:S(2)}, u32[]{:S(2)}) collective-permute-start(bf16[48,384]{1,0:T(8,128)(2,1)} %convolution_convert_fusion), channel_id=1, source_target_pairs={{0,256},{256,0},{1,257},{257,1},{2,258},{258,2},{3,259},{259,3},{4... | collective-permute-start | bytes 110600 | tf_op jit(solution)/shard_map/ppermute | solution.py:157
  16.8 12.7 %collective-permute-start = (bf16[288,1024]{1,0:T(8,128)(2,1)S(1)}, bf16[288,1024]{1,0:T(8,128)(2,1)S(1)}, u32[]{:S(2)}, u32[]{:S(2)}) collective-permute-start(bf16[288,1024]{1,0:T(8,128)(2,1)S(1)} %bitcast.34), channel_id=1, source_target_pairs={{0,2},{2,4},{4,6},{6,256},{256,258},{258,260},{260,262},{262,0},{1... | collective-permute-start | bytes 1769480 | tf_op jit(solution)/shard_map/ppermute | solution.py:143
  18.8 15.9 %collective-permute-start.5 = (bf16[288,1024]{1,0:T(8,128)(2,1)}, bf16[288,1024]{1,0:T(8,128)(2,1)S(1)}, u32[]{:S(2)}, u32[]{:S(2)}) collective-permute-start(bf16[288,1024]{1,0:T(8,128)(2,1)} %collective-permute-done.4.refs_0_), channel_id=1, source_target_pairs={{0,2},{2,4},{4,6},{6,256},{256,258},{258,260},{260,262},{262,0},{1... | collective-permute-start | bytes 1769480 | tf_op jit(solution)/shard_map/ppermute | solution.py:143
  22.7 23.9 %all-to-all-start = ((bf16[8,96,384]{2,1,0:T(8,128)(2,1)}), bf16[8,96,384]{2,1,0:T(8,128)(2,1)}, u32[]{:S(2)}, u32[]{:S(2)}) async-start(bf16[8,96,384]{2,1,0:T(8,128)(2,1)} %broadcast_in_dim.23), calls=%async_computation | async-start | bytes 1179648 | tf_op jit(solution)/shard_map/all_to_all | solution.py:126
  29.5 11.6 %collective-permute-start.1 = (bf16[288,1024]{1,0:T(8,128)(2,1)S(1)}, bf16[288,1024]{1,0:T(8,128)(2,1)}, u32[]{:S(2)}, u32[]{:S(2)}) collective-permute-start(bf16[288,1024]{1,0:T(8,128)(2,1)S(1)} %collective-permute-done.refs_3_), channel_id=1, source_target_pairs={{0,2},{2,4},{4,6},{6,256},{256,258},{258,260},{260,262},{262,0},{1... | collective-permute-start | bytes 1769480 | tf_op jit(solution)/shard_map/ppermute | solution.py:143
  34.7 15.5 %copy-start.2 = (bf16[288,1024]{1,0:T(8,128)(2,1)}, bf16[288,1024]{1,0:T(8,128)(2,1)S(1)}, u32[]{:S(2)}) copy-start(bf16[288,1024]{1,0:T(8,128)(2,1)S(1)} %collective-permute-done.5.refs_7_) | copy-start | bytes 1769476
  34.7 12.8 %collective-permute-start.7 = (bf16[288,1024]{1,0:T(8,128)(2,1)S(1)}, bf16[288,1024]{1,0:T(8,128)(2,1)}, u32[]{:S(2)}, u32[]{:S(2)}) collective-permute-start(bf16[288,1024]{1,0:T(8,128)(2,1)S(1)} %collective-permute-done.5.refs_7_), channel_id=1, source_target_pairs={{0,2},{2,4},{4,6},{6,256},{256,258},{258,260},{260,262},{262,0},{1... | collective-permute-start | bytes 1769480 | tf_op jit(solution)/shard_map/ppermute | solution.py:143
  41.1 13.7 %collective-permute-start.2 = (bf16[288,1024]{1,0:T(8,128)(2,1)}, bf16[288,1024]{1,0:T(8,128)(2,1)}, u32[]{:S(2)}, u32[]{:S(2)}) collective-permute-start(bf16[288,1024]{1,0:T(8,128)(2,1)} %collective-permute-done.1.refs_4_), channel_id=1, source_target_pairs={{0,2},{2,4},{4,6},{6,256},{256,258},{258,260},{260,262},{262,0},{1... | collective-permute-start | bytes 1769480 | tf_op jit(solution)/shard_map/ppermute | solution.py:143
  50.1 26.6 %copy-start.5 = (s32[96]{0:T(128)S(1)}, s32[96]{0:T(128)}, u32[]{:S(2)}) copy-start(s32[96]{0:T(128)} %param.5) | copy-start | bytes 1156
  50.1 30.6 %all-to-all-start.1 = ((bf16[4,768,384]{2,1,0:T(8,128)(2,1)}), bf16[4,768,384]{2,1,0:T(8,128)(2,1)}, u32[]{:S(2)}, u32[]{:S(2)}) async-start(bf16[4,768,384]{2,1,0:T(8,128)(2,1)} %broadcast_in_dim.24), calls=%async_computation.1 | async-start | bytes 4718592 | tf_op jit(solution)/shard_map/all_to_all | solution.py:126
  54.8 12.6 %collective-permute-start.3 = (bf16[288,1024]{1,0:T(8,128)(2,1)}, bf16[288,1024]{1,0:T(8,128)(2,1)S(1)}, u32[]{:S(2)}, u32[]{:S(2)}) collective-permute-start(bf16[288,1024]{1,0:T(8,128)(2,1)} %collective-permute-done.2.refs_5_), channel_id=1, source_target_pairs={{0,2},{2,4},{4,6},{6,256},{256,258},{258,260},{260,262},{262,0},{1... | collective-permute-start | bytes 1769480 | tf_op jit(solution)/shard_map/ppermute | solution.py:143
  67.3 13.4 %collective-permute-start.9 = (bf16[288,1024]{1,0:T(8,128)(2,1)S(1)}, bf16[288,1024]{1,0:T(8,128)(2,1)}, u32[]{:S(2)}, u32[]{:S(2)}) collective-permute-start(bf16[288,1024]{1,0:T(8,128)(2,1)S(1)} %collective-permute-done.3.refs_1_.refs_6_), channel_id=1, source_target_pairs={{0,1},{1,0},{2,3},{3,2},{4,5},{5,4},{6,7},{7,6},{8,9},{9,8},{10,11... | collective-permute-start | bytes 1769480 | tf_op jit(solution)/shard_map/ppermute | solution.py:152
  74.6 11.2 %collective-permute-start.8 = (bf16[288,1024]{1,0:T(8,128)(2,1)}, bf16[288,1024]{1,0:T(8,128)(2,1)}, u32[]{:S(2)}, u32[]{:S(2)}) collective-permute-start(bf16[288,1024]{1,0:T(8,128)(2,1)} %collective-permute-done.7.refs_8_), channel_id=1, source_target_pairs={{0,2},{2,4},{4,6},{6,256},{256,258},{258,260},{260,262},{262,0},{1... | collective-permute-start | bytes 1769480 | tf_op jit(solution)/shard_map/ppermute | solution.py:143
  85.8 1.1 copy-start.3
  93.1 9.9 %collective-permute-start.10 = (f32[4,896,128]{2,1,0:T(8,128)}, f32[4,896,128]{2,1,0:T(8,128)S(1)}, u32[]{:S(2)}, u32[]{:S(2)}) collective-permute-start(f32[4,896,128]{2,1,0:T(8,128)} %shard_map.60), channel_id=1, source_target_pairs={{0,1},{1,0},{2,3},{3,2},{4,5},{5,4},{6,7},{7,6},{8,9},{9,8},{10,11... | collective-permute-start | bytes 5505032 | tf_op jit(solution)/shard_map/ppermute | solution.py:187
  134.9 24.2 %all-to-all-start.3 = ((f32[16,56,128]{2,1,0:T(8,128)}), f32[16,56,128]{2,1,0:T(8,128)S(1)}, u32[]{:S(2)}, u32[]{:S(2)}) async-start(f32[16,56,128]{2,1,0:T(8,128)} %bitcast.22), calls=%async_computation.3 | async-start | bytes 917504 | tf_op jit(solution)/shard_map/all_to_all | solution.py:190
  159.1 0.8 copy-start.4

commit v5 on v4

--- a/solution.py
+++ b/solution.py
@@ -10,6 +10,8 @@
 DP = ("zh", "x", "yh", "yl")
 GROUP = ("zl", "c")
 Y = ("yh", "yl")
+NEAR = ("x", "yl")
+FAR = ("yh", "zh")
 
 
 def gram_kernel(table, slots, near_ref, far_ref, *refs):
@@ -65,19 +67,19 @@
             scratch_shapes=[pltpu.VMEM((len(blocks) * cols, share), jnp.float32)],
         ),
         out_shape=out,
-        compiler_params=pltpu.CompilerParams(vmem_limit_bytes=48 * 2**20),
+        compiler_params=pltpu.CompilerParams(vmem_limit_bytes=24 * 2**20),
     )(table, *given)
 
 
 def sum_join_kernel(scale, parts_ref, out_ref):
     held, tile, cols = out_ref.shape
-    halves, rows = parts_ref.shape[0], held * tile
+    halves, rows = parts_ref.shape[1], held * tile
     extra = cols // halves - 128
     pieces = []
     for half in range(halves):
-        total = parts_ref[half, 0]
-        for n in range(1, parts_ref.shape[1]):
-            total = total + parts_ref[half, n]
+        total = parts_ref[0, half]
+        for n in range(1, parts_ref.shape[0]):
+            total = total + parts_ref[n, half]
         total = total * scale
         pieces.append(total[:rows])
         rest = total[rows:]
@@ -96,29 +98,42 @@
     )(parts)
 
 
-def place_kernel(slot_of, rows_ref, out_ref):
+def place_kernel(place_of, rows_ref, late_ref, out_ref):
     tile = rows_ref.shape[1]
-    for pair in range(out_ref.shape[0] // (2 * tile)):
-        both = [rows_ref[slot_of[2 * pair + n]].astype(jnp.float32) for n in range(2)]
+    cols = out_ref.shape[1]
+    tiles = out_ref.shape[0] // tile
+    for pair in range(tiles // 2):
+        both = []
+        for n in range(2):
+            at, theirs = place_of[2 * pair + n], place_of[tiles + 2 * pair + n]
+            rows = rows_ref[at].astype(jnp.float32)
+            other = jnp.concatenate(
+                [rows[:, cols:], late_ref[at].astype(jnp.float32)], axis=1
+            )
+            both.append(jnp.where(theirs > 0, other, rows[:, :cols]))
         out_ref[2 * tile * pair : 2 * tile * (pair + 1), :] = jnp.concatenate(both).astype(
             out_ref.dtype
         )
 
 
-def place(slot_of, rows):
-    slots, tile, cols = rows.shape
-    tiles = slot_of.shape[0]
+def place(place_of, rows, late):
+    tile = rows.shape[1]
+    cols = (rows.shape[2] + late.shape[2]) // 2
+    tiles = place_of.shape[0] // 2
     return pl.pallas_call(
         place_kernel,
         grid_spec=pltpu.PrefetchScalarGridSpec(
             num_scalar_prefetch=1,
             grid=(1,),
-            in_specs=[pl.BlockSpec((slots, tile, cols), lambda i, s: (0, 0, 0))],
+            in_specs=[
+                pl.BlockSpec(rows.shape, lambda i, s: (0, 0, 0)),
+                pl.BlockSpec(late.shape, lambda i, s: (0, 0, 0)),
+            ],
             out_specs=pl.BlockSpec((tiles * tile, cols), lambda i, s: (0, 0)),
         ),
         out_shape=jax.ShapeDtypeStruct((tiles * tile, cols), rows.dtype),
-        compiler_params=pltpu.CompilerParams(vmem_limit_bytes=32 * 2**20),
-    )(slot_of, rows)
+        compiler_params=pltpu.CompilerParams(vmem_limit_bytes=24 * 2**20),
+    )(place_of, rows, late)
 
 
 def spread(rows, axis):
@@ -142,34 +157,10 @@
     def hop(block):
         return lax.ppermute(block, ("zh", "zl", "c"), hops)
 
-    own = sampled.T
-    twin = lax.ppermute(own, "c", swap)
-    same, cross = [own], [twin]
-    for step in range(ring // 2):
-        same.append(hop(same[-1]))
-        if step < ring // 2 - 1:
-            cross.append(hop(cross[-1]))
-    far_twin = lax.ppermute(same[-1], "c", swap)
-
-    mine = jnp.dot(
-        inverse_rows.reshape(held * tile, order), gradient, preferred_element_type=jnp.float32
-    ).astype(jnp.bfloat16)
-    other = lax.ppermute(mine, "zh", [(0, 1), (1, 0)])
-    first = lax.axis_index("zh") == 0
-    rows = jnp.stack([jnp.where(first, mine, other), jnp.where(first, other, mine)])
-    rows = spread(rows.reshape(n_zh * held * tile, width), Y)
-    rows = rows.reshape(n_yh * n_yl * n_zh * held * tile, width)
-    rows, cross[2] = lax.optimization_barrier((rows, cross[2]))
-    rows = spread(rows, "x").reshape(owners * held, tile, width)
-    far_twin, rows = lax.optimization_barrier((far_twin, rows))
-    place_of = jnp.arange(owners * held, dtype=jnp.int32).reshape(n_x, n_yh * n_yl, n_zh, held)
-    slot_place = place_of.transpose(2, 0, 1, 3).reshape(-1)
-    preconditioned = place(slot_place[assignment], rows)
-
-    n_y = n_yh * n_yl
+    owner_slots = owners * held
     index = jnp.arange(tiles, dtype=jnp.int32)
-    table = jnp.full((owners * held,), -1, jnp.int32).at[assignment].set(index)
-    table = table.reshape(n_zh, n_x, n_y, held).transpose(1, 0, 2, 3).reshape(-1)
+    table = jnp.full((owner_slots,), -1, jnp.int32).at[assignment].set(index)
+    table = table.reshape(n_zh, n_x, n_yh, n_yl, held).transpose(1, 3, 2, 0, 4).reshape(-1)
     core, upper = lax.axis_index("c"), lax.axis_index("zh")
     here = upper * (ring // n_zh) + lax.axis_index("zl")
     share = cols // n_zh
@@ -181,15 +172,47 @@
         row = (chip % (ring // n_zh) * 2 + side) * cols
         more += [row, (chip // (ring // n_zh) != upper).astype(jnp.int32)]
     table = jnp.concatenate([table, jnp.stack(more).astype(jnp.int32)])
+
+    own = sampled.T
+    twin = lax.ppermute(own, "c", swap)
+    same, cross = [own, hop(own)], [twin, hop(twin)]
+
+    inverse_rows, twin = lax.optimization_barrier((inverse_rows, twin))
+    rows = jnp.dot(
+        inverse_rows.reshape(held * tile, order), gradient, preferred_element_type=jnp.float32
+    ).astype(jnp.bfloat16)
+    early = width * 2 // 3 // 128 * 128
+    other = lax.ppermute(rows[:, :early], "zh", swap)
+    same[1], other, table = lax.optimization_barrier((same[1], other, table))
+    for step in range(1, ring // 2 - 1):
+        same.append(hop(same[-1]))
+        cross.append(hop(cross[-1]))
+    rows = spread(jnp.concatenate([rows, other], axis=1), Y)
+    rows = spread(rows.reshape(-1, width + early), "x")
+    same.append(hop(same[-1]))
+    same[-1], cross[-1] = lax.optimization_barrier((same[-1], cross[-1]))
+    far_twin = lax.ppermute(same[-1], "c", swap)
+    far_twin, rows = lax.optimization_barrier((far_twin, rows))
+    rows = rows.reshape(-1, tile, width + early)
+    late = lax.ppermute(rows[:, :, early:width], "zh", swap)
+
     blocks = same + cross[1:]
-    sizes = (n_x, n_zh * n_y * held, tile, share)
+    near, far = n_x * n_yl, n_yh * n_zh
+    sizes = (near, far * held, tile, share)
     send = gram(table, twin, far_twin, blocks, *sizes)
     received = lax.ppermute(send, "c", swap)
     terms = gram(table, own, same[-1], blocks, *sizes) + received
-    terms = jnp.sum(lax.all_to_all(terms, "x", 0, 0), axis=0)
-    terms = lax.all_to_all(terms.reshape(n_zh * n_y, -1, terms.shape[1]), ("zh",) + Y, 0, 0)
-    terms = terms.reshape((n_zh, n_y) + terms.shape[1:])
+    terms = lax.all_to_all(terms, NEAR, 0, 0)
+    terms = functools.reduce(jnp.add, [terms[n] for n in range(near)])
+    terms, late = lax.optimization_barrier((terms, late))
+    terms = lax.all_to_all(terms.reshape(far, -1, terms.shape[1]), FAR, 0, 0)
+    terms = terms.reshape((n_yh, n_zh) + terms.shape[1:])
     factor_tiles = sum_join(terms, held, tile, cols, 1.0 / (tokens * owners))
+
+    half = owner_slots // n_zh
+    theirs = (assignment // half != upper).astype(jnp.int32)
+    place_of = jnp.concatenate([assignment % half, theirs]).astype(jnp.int32)
+    preconditioned = place(place_of, rows, late)
     return factor_tiles, preconditioned
 
 

time: 164 us -> 155 us (0.945)
  blocking collectives: 27.7 us -> 0 us
  waiting for transfers between devices: 27.5 us -> 53.2 us
  starting transfers between devices: 70.1 us -> 64.2 us
  Pallas kernels: 17.6 us -> 15.5 us
    all_to_all x1 -> x0, blocking collectives: 27.7 us -> none  [body(): terms = jnp.sum(lax.all_to_all(terms, 'x', 0, 0), axis=0)]
    all_to_all x1 -> x2, waiting for transfers between devices: 10.7 us -> 28 us  [the longest x1 19.8 us: body(): terms = lax.all_to_all(terms, NEAR, 0, 0)]
    all_to_all x2, waiting for transfers between devices: 0.01 us -> 10 us  [spread(): return lax.all_to_all(copies, axis, 0, 0)]
    ppermute x7, waiting for transfers between devices: 16.8 us -> 10.4 us  [hop(): return lax.ppermute(block, ('zh', 'zl', 'c'), hops)]
    unnamed x12 -> x22, local copies, waits for them, and re-layouts: 1.85 us -> 5.32 us
    ppermute x1 -> x2, waiting for transfers between devices: 0.01 us -> 3.32 us  [the longest x1 3.31 us: body(): other = lax.ppermute(rows[:, :early], 'zh', swap)]
    ppermute x1, starting transfers between devices: 7.22 us -> 4.41 us  [body(): far_twin = lax.ppermute(same[-1], 'c', swap)]
    reduce_sum x1 -> x0, other arithmetic: 2.42 us -> none  [body(): terms = jnp.sum(lax.all_to_all(terms, 'x', 0, 0), axis=0)]
  transfers between devices with their start and end apart: 14 -> 16, of which waited for: 6 -> 8; matrix products, arithmetic and copies ran while one was open for 7% -> 7% of each run, Pallas kernels for 6% -> 6%
where the time goes in v5:
time: 155 us; the launch traced here: 152 us
  starting transfers between devices  64.2 us (41%)
  waiting for transfers between devices  53.2 us (34%)
  Pallas kernels  15.5 us (10%)
  local copies, waits for them, and re-layouts  11.6 us (7%)
  other arithmetic  4.68 us (3%)
    ppermute x7, starting transfers between devices, hop(): return lax.ppermute(block, ('zh', 'zl', 'c'), hops)  23.7 us
    all_to_all x1, waiting for transfers between devices, body(): terms = lax.all_to_all(terms, NEAR, 0, 0)  19.8 us
    all_to_all x2, starting transfers between devices, spread(): return lax.all_to_all(copies, axis, 0, 0)  11 us
    ppermute x7, waiting for transfers between devices, hop(): return lax.ppermute(block, ('zh', 'zl', 'c'), hops)  10.4 us
    all_to_all x2, waiting for transfers between devices, spread(): return lax.all_to_all(copies, axis, 0, 0)  10 us
    pallas_call x2, Pallas kernels, gram(): pl.pallas_call(lambda table_ref, *refs: gram_kernel(table_ref, slots, *re...  9.98 us
    ppermute x1, starting transfers between devices, body(): twin = lax.ppermute(own, 'c', swap)  8.92 us
    all_to_all x1, waiting for transfers between devices, body(): terms = lax.all_to_all(terms.reshape(far, -1, terms.shape[1]), FAR, 0, 0)  8.24 us
  transfers between devices with their start and end apart: 16, of which 8 were waited for; matrix products, arithmetic and copies ran while one was open for 7% of the time, Pallas kernels for 6%

profile of v5, /device:TPU:1, one launch (start us, length us, event | category | flops | bytes accessed | tf_op | source)
XLA Modules:
  0.0 151.9 jit_solution(11729035035272142335)
XLA Ops:
  0.6 0.0 copy-start
  0.6 0.0 copy-start.10
  0.7 8.9 %collective-permute-start.1 = (bf16[288,1024]{1,0:T(8,128)(2,1)}, bf16[288,1024]{1,0:T(8,128)(2,1)S(1)}, u32[]{:S(2)}, u32[]{:S(2)}) collective-permute-start(bf16[288,1024]{1,0:T(8,128)(2,1)} %bitcast.25), channel_id=1, source_target_pairs={{0,1},{1,0},{2,3},{3,2},{4,5},{5,4},{6,7},{7,6},{8,9},{9,8},{10,11... | collective-permute-start | bytes 1769480 | tf_op jit(solution)/shard_map/ppermute | solution.py:177
  9.6 5.3 %collective-permute-start = (bf16[288,1024]{1,0:T(8,128)(2,1)}, bf16[288,1024]{1,0:T(8,128)(2,1)S(1)}, u32[]{:S(2)}, u32[]{:S(2)}) collective-permute-start(bf16[288,1024]{1,0:T(8,128)(2,1)} %bitcast.26), channel_id=1, source_target_pairs={{0,2},{2,4},{4,6},{6,256},{256,258},{258,260},{260,262},{262,0},{1... | collective-permute-start | bytes 1769480 | tf_op jit(solution)/shard_map/ppermute | solution.py:158
  14.9 0.0 collective-permute-done.1.refs_0_
  14.9 0.0 copy-start.6
  14.9 0.0 copy-done
  14.9 1.5 %convolution_convert_fusion = bf16[48,384]{1,0:T(8,128)(2,1)S(1)} fusion(bf16[48,2304]{1,0:T(8,128)(2,1)} %bitcast.31, bf16[2304,384]{1,0:T(8,128)(2,1)S(1)} %copy-done), kind=kOutput, calls=%fused_computation.1 | convolution fusion | flops 84953088 | bytes 2027520 | tf_op jit(solution)/shard_map/dot_general | solution.py:181
  16.5 0.0 copy-start.9
  16.5 0.6 copy-done.9
  17.1 0.6 slice.40
  17.7 1.9 %collective-permute-start.2 = (bf16[48,256]{1,0:T(8,128)(2,1)}, bf16[48,256]{1,0:T(8,128)(2,1)}, u32[]{:S(2)}, u32[]{:S(2)}) collective-permute-start(bf16[48,256]{1,0:T(8,128)(2,1)} %slice.40), channel_id=1, source_target_pairs={{0,256},{256,0},{1,257},{257,1},{2,258},{258,2},{3,259},{259,3},{4... | collective-permute-start | bytes 73736 | tf_op jit(solution)/shard_map/ppermute | solution.py:185
  19.6 0.0 copy-done.10
  19.9 0.9 scatter_custom_fusion
  20.8 0.2 reshape.29
  21.0 0.1 reshape.30
  21.1 0.1 concatenate.9.table_ref
  21.2 2.2 %collective-permute-start.6 = (bf16[288,1024]{1,0:T(8,128)(2,1)S(1)}, bf16[288,1024]{1,0:T(8,128)(2,1)S(1)}, u32[]{:S(2)}, u32[]{:S(2)}) collective-permute-start(bf16[288,1024]{1,0:T(8,128)(2,1)S(1)} %collective-permute-done.1.refs_0_), channel_id=1, source_target_pairs={{0,2},{2,4},{4,6},{6,256},{256,258},{258,260},{260,262},{262,0},{1... | collective-permute-start | bytes 1769480 | tf_op jit(solution)/shard_map/ppermute | solution.py:158
  23.4 0.0 collective-permute-done.refs_3_
  23.4 3.3 %collective-permute-done.2 = bf16[48,256]{1,0:T(8,128)(2,1)} collective-permute-done((bf16[48,256]{1,0:T(8,128)(2,1)}, bf16[48,256]{1,0:T(8,128)(2,1)}, u32[]{:S(2)}, u32[]{:S(2)}) %collective-permute-start.2) | collective-permute-done | bytes 24608 | tf_op jit(solution)/shard_map/ppermute | solution.py:185
  26.7 2.4 %collective-permute-start.3 = (bf16[288,1024]{1,0:T(8,128)(2,1)S(1)}, bf16[288,1024]{1,0:T(8,128)(2,1)}, u32[]{:S(2)}, u32[]{:S(2)}) collective-permute-start(bf16[288,1024]{1,0:T(8,128)(2,1)S(1)} %collective-permute-done.refs_3_), channel_id=1, source_target_pairs={{0,2},{2,4},{4,6},{6,256},{256,258},{258,260},{260,262},{262,0},{1... | collective-permute-start | bytes 1769480 | tf_op jit(solution)/shard_map/ppermute | solution.py:158
  29.1 0.8 pad_maximum_fusion
  29.9 0.8 broadcast_in_dim.21
  30.8 0.0 copy-done.6
  30.8 6.5 %all-to-all-start = ((bf16[8,48,640]{2,1,0:T(8,128)(2,1)}), bf16[8,48,640]{2,1,0:T(8,128)(2,1)}, u32[]{:S(2)}, u32[]{:S(2)}) async-start(bf16[8,48,640]{2,1,0:T(8,128)(2,1)} %broadcast_in_dim.21), calls=%async_computation | async-start | bytes 983040 | tf_op jit(solution)/shard_map/all_to_all | solution.py:141
  37.2 0.0 collective-permute-done.6.refs_7_
  37.2 0.0 copy-start.2
  37.2 2.3 %collective-permute-start.7 = (bf16[288,1024]{1,0:T(8,128)(2,1)S(1)}, bf16[288,1024]{1,0:T(8,128)(2,1)}, u32[]{:S(2)}, u32[]{:S(2)}) collective-permute-start(bf16[288,1024]{1,0:T(8,128)(2,1)S(1)} %collective-permute-done.6.refs_7_), channel_id=1, source_target_pairs={{0,2},{2,4},{4,6},{6,256},{256,258},{258,260},{260,262},{262,0},{1... | collective-permute-start | bytes 1769480 | tf_op jit(solution)/shard_map/ppermute | solution.py:158
  39.5 0.0 collective-permute-done.3.refs_4_
  39.5 4.0 %collective-permute-start.4 = (bf16[288,1024]{1,0:T(8,128)(2,1)}, bf16[288,1024]{1,0:T(8,128)(2,1)}, u32[]{:S(2)}, u32[]{:S(2)}) collective-permute-start(bf16[288,1024]{1,0:T(8,128)(2,1)} %collective-permute-done.3.refs_4_), channel_id=1, source_target_pairs={{0,2},{2,4},{4,6},{6,256},{256,258},{258,260},{260,262},{262,0},{1... | collective-permute-start | bytes 1769480 | tf_op jit(solution)/shard_map/ppermute | solution.py:158
  43.6 9.8 %all-to-all-done = bf16[8,48,640]{2,1,0:T(8,128)(2,1)} async-done(((bf16[8,48,640]{2,1,0:T(8,128)(2,1)}), bf16[8,48,640]{2,1,0:T(8,128)(2,1)}, u32[]{:S(2)}, u32[]{:S(2)}) %all-to-all-start) | async-done | bytes 491552 | tf_op jit(solution)/shard_map/all_to_all | solution.py:141
  53.4 2.5 %broadcast_in_dim.23 = bf16[4,384,640]{2,1,0:T(8,128)(2,1)} broadcast(bf16[384,640]{1,0:T(8,128)(2,1)} %bitcast.17), dimensions={1,2} | broadcast | bytes 2457600 | tf_op jit(solution)/shard_map/broadcast_in_dim | solution.py:140
  55.9 0.0 copy-done.2
  55.9 4.6 %all-to-all-start.1 = ((bf16[4,384,640]{2,1,0:T(8,128)(2,1)}), bf16[4,384,640]{2,1,0:T(8,128)(2,1)}, u32[]{:S(2)}, u32[]{:S(2)}) async-start(bf16[4,384,640]{2,1,0:T(8,128)(2,1)} %broadcast_in_dim.23), calls=%async_computation.1 | async-start | bytes 3932160 | tf_op jit(solution)/shard_map/all_to_all | solution.py:141
  60.4 0.0 collective-permute-done.7.refs_8_
  60.4 1.9 %collective-permute-start.8 = (bf16[288,1024]{1,0:T(8,128)(2,1)}, bf16[288,1024]{1,0:T(8,128)(2,1)S(1)}, u32[]{:S(2)}, u32[]{:S(2)}) collective-permute-start(bf16[288,1024]{1,0:T(8,128)(2,1)} %collective-permute-done.7.refs_8_), channel_id=1, source_target_pairs={{0,2},{2,4},{4,6},{6,256},{256,258},{258,260},{260,262},{262,0},{1... | collective-permute-start | bytes 1769480 | tf_op jit(solution)/shard_map/ppermute | solution.py:158
  62.4 0.0 collective-permute-done.4.refs_5_
  62.4 5.6 %collective-permute-start.5 = (bf16[288,1024]{1,0:T(8,128)(2,1)}, bf16[288,1024]{1,0:T(8,128)(2,1)S(1)}, u32[]{:S(2)}, u32[]{:S(2)}) collective-permute-start(bf16[288,1024]{1,0:T(8,128)(2,1)} %collective-permute-done.4.refs_5_), channel_id=1, source_target_pairs={{0,2},{2,4},{4,6},{6,256},{256,258},{258,260},{260,262},{262,0},{1... | collective-permute-start | bytes 1769480 | tf_op jit(solution)/shard_map/ppermute | solution.py:158
  68.0 4.8 %collective-permute-done.8.refs_9_ = bf16[288,1024]{1,0:T(8,128)(2,1)S(1)} collective-permute-done((bf16[288,1024]{1,0:T(8,128)(2,1)}, bf16[288,1024]{1,0:T(8,128)(2,1)S(1)}, u32[]{:S(2)}, u32[]{:S(2)}) %collective-permute-start.8) | collective-permute-done | bytes 589856 | tf_op jit(solution)/shard_map/ppermute | solution.py:158
  72.8 0.8 copy-done.4
  73.6 5.5 %collective-permute-done.5.refs_1_.refs_6_ = bf16[288,1024]{1,0:T(8,128)(2,1)S(1)} collective-permute-done((bf16[288,1024]{1,0:T(8,128)(2,1)}, bf16[288,1024]{1,0:T(8,128)(2,1)S(1)}, u32[]{:S(2)}, u32[]{:S(2)}) %collective-permute-start.5) | collective-permute-done | bytes 589856 | tf_op jit(solution)/shard_map/ppermute | solution.py:158
  79.1 4.4 %collective-permute-start.9 = (bf16[288,1024]{1,0:T(8,128)(2,1)S(1)}, bf16[288,1024]{1,0:T(8,128)(2,1)}, u32[]{:S(2)}, u32[]{:S(2)}) collective-permute-start(bf16[288,1024]{1,0:T(8,128)(2,1)S(1)} %collective-permute-done.5.refs_1_.refs_6_), channel_id=1, source_target_pairs={{0,1},{1,0},{2,3},{3,2},{4,5},{5,4},{6,7},{7,6},{8,9},{9,8},{10,11... | collective-permute-start | bytes 1769480 | tf_op jit(solution)/shard_map/ppermute | solution.py:194
  83.5 0.2 all-to-all-done.1
  83.8 1.5 collective-permute-done.9.refs_1_
  85.3 1.1 copy-done.3
  86.3 1.1 copy-done.5
  87.4 1.1 copy-done.7
  88.5 5.1 %shard_map.60 = f32[8,448,128]{2,1,0:T(8,128)S(1)} custom-call(s32[145]{0:T(256)S(1)} %concatenate.9.table_ref, bf16[288,1024]{1,0:T(8,128)(2,1)S(1)} %copy-done.7, bf16[288,1024]{1,0:T(8,128)(2,1)} %collective-permute-done.9.refs_1_, bf16[288,1024]{1,0:T(8,128)(2,1)S(1)} %bitcast.27, bf16[288,1024]{1,0:T(8,128)(2,1)S(1)} %collective-permute-done.refs_3_, ...), custom_call_target="tpu_custom_call" | custom-call | tf_op jit(solution)/shard_map/pallas_call | solution.py:60
  93.6 3.0 %collective-permute-start.10 = (f32[8,448,128]{2,1,0:T(8,128)S(1)}, f32[8,448,128]{2,1,0:T(8,128)S(1)}, u32[]{:S(2)}, u32[]{:S(2)}) collective-permute-start(f32[8,448,128]{2,1,0:T(8,128)S(1)} %shard_map.60), channel_id=1, source_target_pairs={{0,1},{1,0},{2,3},{3,2},{4,5},{5,4},{6,7},{7,6},{8,9},{9,8},{10,11... | collective-permute-start | bytes 5505032 | tf_op jit(solution)/shard_map/ppermute | solution.py:203
  96.6 4.9 %shard_map.59 = f32[8,448,128]{2,1,0:T(8,128)S(1)} custom-call(s32[145]{0:T(256)S(1)} %concatenate.9.table_ref, bf16[288,1024]{1,0:T(8,128)(2,1)S(1)} %bitcast.28, bf16[288,1024]{1,0:T(8,128)(2,1)S(1)} %collective-permute-done.5.refs_1_.refs_6_, bf16[288,1024]{1,0:T(8,128)(2,1)S(1)} %bitcast.29, bf16[288,1024]{1,0:T(8,128)(2,1)S(1)} %collective-permute-done.refs_3_, ...), custom_call_target="tpu_custom_call" | custom-call | tf_op jit(solution)/shard_map/pallas_call | solution.py:60
  101.5 0.0 collective-permute-done.10
  101.5 1.5 add.156
  102.9 4.3 %all-to-all-start.2 = ((f32[8,448,128]{2,1,0:T(8,128)}), f32[8,448,128]{2,1,0:T(8,128)}, u32[]{:S(2)}, u32[]{:S(2)}) async-start(f32[8,448,128]{2,1,0:T(8,128)} %add.156), calls=%async_computation.2 | async-start | bytes 3670016 | tf_op jit(solution)/shard_map/all_to_all | solution.py:205
  107.3 1.0 slice.49
  108.3 3.5 %collective-permute-start.11 = (bf16[64,24,128]{2,1,0:T(8,128)(2,1)S(1)}, bf16[64,24,128]{2,1,0:T(8,128)(2,1)S(1)}, u32[]{:S(2)}, u32[]{:S(2)}) collective-permute-start(bf16[64,24,128]{2,1,0:T(8,128)(2,1)S(1)} %slice.49), channel_id=1, source_target_pairs={{0,256},{256,0},{1,257},{257,1},{2,258},{258,2},{3,259},{259,3},{4... | collective-permute-start | bytes 1179656 | tf_op jit(solution)/shard_map/ppermute | solution.py:197
  111.8 19.8 %all-to-all-done.2 = f32[8,448,128]{2,1,0:T(8,128)} async-done(((f32[8,448,128]{2,1,0:T(8,128)}), f32[8,448,128]{2,1,0:T(8,128)}, u32[]{:S(2)}, u32[]{:S(2)}) %all-to-all-start.2) | async-done | bytes 1835040 | tf_op jit(solution)/shard_map/all_to_all | solution.py:205
  131.6 2.3 %fusion = f32[448,128]{1,0:T(8,128)} fusion(f32[8,448,128]{2,1,0:T(8,128)} %all-to-all-done.2), kind=kLoop, calls=%fused_computation.3 | loop fusion | flops 401408 | bytes 2064384 | tf_op jit(solution)/shard_map/add | solution.py:206
  133.9 0.0 collective-permute-done.11.late_ref
  133.9 3.4 %all-to-all-start.3 = ((f32[8,56,128]{2,1,0:T(8,128)}), f32[8,56,128]{2,1,0:T(8,128)S(1)}, u32[]{:S(2)}, u32[]{:S(2)}) async-start(f32[8,56,128]{2,1,0:T(8,128)} %bitcast.20), calls=%async_computation.3 | async-start | bytes 458752 | tf_op jit(solution)/shard_map/all_to_all | solution.py:208
  137.4 0.1 pad_add_fusion.place_of
  137.4 3.8 %shard_map.62 = bf16[2304,384]{1,0:T(8,128)(2,1)} custom-call(s32[192]{0:T(256)S(1)} %pad_add_fusion.place_of, bf16[64,24,640]{2,1,0:T(8,128)(2,1)} %bitcast.19.rows_ref, bf16[64,24,128]{2,1,0:T(8,128)(2,1)S(1)} %collective-permute-done.11.late_ref), custom_call_target="tpu_custom_call" | custom-call | tf_op jit(solution)/shard_map/pallas_call | solution.py:123
  141.2 8.2 %all-to-all-done.3 = f32[8,56,128]{2,1,0:T(8,128)S(1)} async-done(((f32[8,56,128]{2,1,0:T(8,128)}), f32[8,56,128]{2,1,0:T(8,128)S(1)}, u32[]{:S(2)}, u32[]{:S(2)}) %all-to-all-start.3) | async-done | bytes 229408 | tf_op jit(solution)/shard_map/all_to_all | solution.py:208
  149.5 0.7 copy-done.8
  150.2 1.7 %shard_map.61 = f32[2,24,288]{2,1,0:T(8,128)} custom-call(f32[4,2,56,128]{3,2,1,0:T(8,128)} %bitcast.30), custom_call_target="tpu_custom_call" | custom-call | tf_op jit(solution)/shard_map/pallas_call | solution.py:95
  (11 shorter events, 0.1 us)
Async XLA Ops:
  0.6 14.3 %copy-start = (bf16[2304,384]{1,0:T(8,128)(2,1)S(1)}, bf16[2304,384]{1,0:T(8,128)(2,1)}, u32[]{:S(2)}) copy-start(bf16[2304,384]{1,0:T(8,128)(2,1)} %param.7) | copy-start | bytes 5308420
  0.6 19.0 %copy-start.10 = (s32[96]{0:T(128)S(1)}, s32[96]{0:T(128)}, u32[]{:S(2)}) copy-start(s32[96]{0:T(128)} %param.5) | copy-start | bytes 1156
  0.7 14.2 %collective-permute-start.1 = (bf16[288,1024]{1,0:T(8,128)(2,1)}, bf16[288,1024]{1,0:T(8,128)(2,1)S(1)}, u32[]{:S(2)}, u32[]{:S(2)}) collective-permute-start(bf16[288,1024]{1,0:T(8,128)(2,1)} %bitcast.25), channel_id=1, source_target_pairs={{0,1},{1,0},{2,3},{3,2},{4,5},{5,4},{6,7},{7,6},{8,9},{9,8},{10,11... | collective-permute-start | bytes 1769480 | tf_op jit(solution)/shard_map/ppermute | solution.py:177
  9.6 13.8 %collective-permute-start = (bf16[288,1024]{1,0:T(8,128)(2,1)}, bf16[288,1024]{1,0:T(8,128)(2,1)S(1)}, u32[]{:S(2)}, u32[]{:S(2)}) collective-permute-start(bf16[288,1024]{1,0:T(8,128)(2,1)} %bitcast.26), channel_id=1, source_target_pairs={{0,2},{2,4},{4,6},{6,256},{256,258},{258,260},{260,262},{262,0},{1... | collective-permute-start | bytes 1769480 | tf_op jit(solution)/shard_map/ppermute | solution.py:158
  14.9 15.9 %copy-start.6 = (bf16[288,1024]{1,0:T(8,128)(2,1)}, bf16[288,1024]{1,0:T(8,128)(2,1)S(1)}, u32[]{:S(2)}) copy-start(bf16[288,1024]{1,0:T(8,128)(2,1)S(1)} %collective-permute-done.1.refs_0_) | copy-start | bytes 1769476
  16.5 0.6 copy-start.9
  17.7 9.0 %collective-permute-start.2 = (bf16[48,256]{1,0:T(8,128)(2,1)}, bf16[48,256]{1,0:T(8,128)(2,1)}, u32[]{:S(2)}, u32[]{:S(2)}) collective-permute-start(bf16[48,256]{1,0:T(8,128)(2,1)} %slice.40), channel_id=1, source_target_pairs={{0,256},{256,0},{1,257},{257,1},{2,258},{258,2},{3,259},{259,3},{4... | collective-permute-start | bytes 73736 | tf_op jit(solution)/shard_map/ppermute | solution.py:185
  21.2 16.0 %collective-permute-start.6 = (bf16[288,1024]{1,0:T(8,128)(2,1)S(1)}, bf16[288,1024]{1,0:T(8,128)(2,1)S(1)}, u32[]{:S(2)}, u32[]{:S(2)}) collective-permute-start(bf16[288,1024]{1,0:T(8,128)(2,1)S(1)} %collective-permute-done.1.refs_0_), channel_id=1, source_target_pairs={{0,2},{2,4},{4,6},{6,256},{256,258},{258,260},{260,262},{262,0},{1... | collective-permute-start | bytes 1769480 | tf_op jit(solution)/shard_map/ppermute | solution.py:158
  26.7 12.8 %collective-permute-start.3 = (bf16[288,1024]{1,0:T(8,128)(2,1)S(1)}, bf16[288,1024]{1,0:T(8,128)(2,1)}, u32[]{:S(2)}, u32[]{:S(2)}) collective-permute-start(bf16[288,1024]{1,0:T(8,128)(2,1)S(1)} %collective-permute-done.refs_3_), channel_id=1, source_target_pairs={{0,2},{2,4},{4,6},{6,256},{256,258},{258,260},{260,262},{262,0},{1... | collective-permute-start | bytes 1769480 | tf_op jit(solution)/shard_map/ppermute | solution.py:158
  30.8 22.6 %all-to-all-start = ((bf16[8,48,640]{2,1,0:T(8,128)(2,1)}), bf16[8,48,640]{2,1,0:T(8,128)(2,1)}, u32[]{:S(2)}, u32[]{:S(2)}) async-start(bf16[8,48,640]{2,1,0:T(8,128)(2,1)} %broadcast_in_dim.21), calls=%async_computation | async-start | bytes 983040 | tf_op jit(solution)/shard_map/all_to_all | solution.py:141
  37.2 18.6 %copy-start.2 = (bf16[288,1024]{1,0:T(8,128)(2,1)}, bf16[288,1024]{1,0:T(8,128)(2,1)S(1)}, u32[]{:S(2)}) copy-start(bf16[288,1024]{1,0:T(8,128)(2,1)S(1)} %collective-permute-done.6.refs_7_) | copy-start | bytes 1769476
  37.2 23.2 %collective-permute-start.7 = (bf16[288,1024]{1,0:T(8,128)(2,1)S(1)}, bf16[288,1024]{1,0:T(8,128)(2,1)}, u32[]{:S(2)}, u32[]{:S(2)}) collective-permute-start(bf16[288,1024]{1,0:T(8,128)(2,1)S(1)} %collective-permute-done.6.refs_7_), channel_id=1, source_target_pairs={{0,2},{2,4},{4,6},{6,256},{256,258},{258,260},{260,262},{262,0},{1... | collective-permute-start | bytes 1769480 | tf_op jit(solution)/shard_map/ppermute | solution.py:158
  39.5 22.8 %collective-permute-start.4 = (bf16[288,1024]{1,0:T(8,128)(2,1)}, bf16[288,1024]{1,0:T(8,128)(2,1)}, u32[]{:S(2)}, u32[]{:S(2)}) collective-permute-start(bf16[288,1024]{1,0:T(8,128)(2,1)} %collective-permute-done.3.refs_4_), channel_id=1, source_target_pairs={{0,2},{2,4},{4,6},{6,256},{256,258},{258,260},{260,262},{262,0},{1... | collective-permute-start | bytes 1769480 | tf_op jit(solution)/shard_map/ppermute | solution.py:158
  55.9 29.4 %copy-start.1 = (bf16[1024,288]{0,1:T(8,128)(2,1)S(1)}, bf16[1024,288]{0,1:T(8,128)(2,1)}, u32[]{:S(2)}) copy-start(bf16[1024,288]{0,1:T(8,128)(2,1)} %param.4) | copy-start | bytes 1769476
  55.9 27.9 %all-to-all-start.1 = ((bf16[4,384,640]{2,1,0:T(8,128)(2,1)}), bf16[4,384,640]{2,1,0:T(8,128)(2,1)}, u32[]{:S(2)}, u32[]{:S(2)}) async-start(bf16[4,384,640]{2,1,0:T(8,128)(2,1)} %broadcast_in_dim.23), calls=%async_computation.1 | async-start | bytes 3932160 | tf_op jit(solution)/shard_map/all_to_all | solution.py:141
  60.4 12.4 %collective-permute-start.8 = (bf16[288,1024]{1,0:T(8,128)(2,1)}, bf16[288,1024]{1,0:T(8,128)(2,1)S(1)}, u32[]{:S(2)}, u32[]{:S(2)}) collective-permute-start(bf16[288,1024]{1,0:T(8,128)(2,1)} %collective-permute-done.7.refs_8_), channel_id=1, source_target_pairs={{0,2},{2,4},{4,6},{6,256},{256,258},{258,260},{260,262},{262,0},{1... | collective-permute-start | bytes 1769480 | tf_op jit(solution)/shard_map/ppermute | solution.py:158
  62.4 16.7 %collective-permute-start.5 = (bf16[288,1024]{1,0:T(8,128)(2,1)}, bf16[288,1024]{1,0:T(8,128)(2,1)S(1)}, u32[]{:S(2)}, u32[]{:S(2)}) collective-permute-start(bf16[288,1024]{1,0:T(8,128)(2,1)} %collective-permute-done.4.refs_5_), channel_id=1, source_target_pairs={{0,2},{2,4},{4,6},{6,256},{256,258},{258,260},{260,262},{262,0},{1... | collective-permute-start | bytes 1769480 | tf_op jit(solution)/shard_map/ppermute | solution.py:158
  72.8 0.8 copy-start.4
  79.1 6.2 %collective-permute-start.9 = (bf16[288,1024]{1,0:T(8,128)(2,1)S(1)}, bf16[288,1024]{1,0:T(8,128)(2,1)}, u32[]{:S(2)}, u32[]{:S(2)}) collective-permute-start(bf16[288,1024]{1,0:T(8,128)(2,1)S(1)} %collective-permute-done.5.refs_1_.refs_6_), channel_id=1, source_target_pairs={{0,1},{1,0},{2,3},{3,2},{4,5},{5,4},{6,7},{7,6},{8,9},{9,8},{10,11... | collective-permute-start | bytes 1769480 | tf_op jit(solution)/shard_map/ppermute | solution.py:194
  85.3 1.1 copy-start.3
  86.3 1.1 copy-start.5
  87.4 1.1 copy-start.7
  93.6 7.9 %collective-permute-start.10 = (f32[8,448,128]{2,1,0:T(8,128)S(1)}, f32[8,448,128]{2,1,0:T(8,128)S(1)}, u32[]{:S(2)}, u32[]{:S(2)}) collective-permute-start(f32[8,448,128]{2,1,0:T(8,128)S(1)} %shard_map.60), channel_id=1, source_target_pairs={{0,1},{1,0},{2,3},{3,2},{4,5},{5,4},{6,7},{7,6},{8,9},{9,8},{10,11... | collective-permute-start | bytes 5505032 | tf_op jit(solution)/shard_map/ppermute | solution.py:203
  102.9 28.7 %all-to-all-start.2 = ((f32[8,448,128]{2,1,0:T(8,128)}), f32[8,448,128]{2,1,0:T(8,128)}, u32[]{:S(2)}, u32[]{:S(2)}) async-start(f32[8,448,128]{2,1,0:T(8,128)} %add.156), calls=%async_computation.2 | async-start | bytes 3670016 | tf_op jit(solution)/shard_map/all_to_all | solution.py:205
  108.3 25.6 %collective-permute-start.11 = (bf16[64,24,128]{2,1,0:T(8,128)(2,1)S(1)}, bf16[64,24,128]{2,1,0:T(8,128)(2,1)S(1)}, u32[]{:S(2)}, u32[]{:S(2)}) collective-permute-start(bf16[64,24,128]{2,1,0:T(8,128)(2,1)S(1)} %slice.49), channel_id=1, source_target_pairs={{0,256},{256,0},{1,257},{257,1},{2,258},{258,2},{3,259},{259,3},{4... | collective-permute-start | bytes 1179656 | tf_op jit(solution)/shard_map/ppermute | solution.py:197
  133.9 15.5 %all-to-all-start.3 = ((f32[8,56,128]{2,1,0:T(8,128)}), f32[8,56,128]{2,1,0:T(8,128)S(1)}, u32[]{:S(2)}, u32[]{:S(2)}) async-start(f32[8,56,128]{2,1,0:T(8,128)} %bitcast.20), calls=%async_computation.3 | async-start | bytes 458752 | tf_op jit(solution)/shard_map/all_to_all | solution.py:208
  149.5 0.7 copy-start.8

commit v6 on v4

--- a/solution.py
+++ b/solution.py
@@ -65,7 +65,7 @@
             scratch_shapes=[pltpu.VMEM((len(blocks) * cols, share), jnp.float32)],
         ),
         out_shape=out,
-        compiler_params=pltpu.CompilerParams(vmem_limit_bytes=48 * 2**20),
+        compiler_params=pltpu.CompilerParams(vmem_limit_bytes=24 * 2**20),
     )(table, *given)
 
 
@@ -96,29 +96,36 @@
     )(parts)
 
 
-def place_kernel(slot_of, rows_ref, out_ref):
+def place_kernel(place_of, *refs):
+    *blocks, out_ref, rows_ref = refs
     tile = rows_ref.shape[1]
+    at = 0
+    for block in blocks:
+        rows_ref[at : at + block.shape[0]] = block[...]
+        at += block.shape[0]
     for pair in range(out_ref.shape[0] // (2 * tile)):
-        both = [rows_ref[slot_of[2 * pair + n]].astype(jnp.float32) for n in range(2)]
+        both = [rows_ref[place_of[2 * pair + n]].astype(jnp.float32) for n in range(2)]
         out_ref[2 * tile * pair : 2 * tile * (pair + 1), :] = jnp.concatenate(both).astype(
             out_ref.dtype
         )
 
 
-def place(slot_of, rows):
-    slots, tile, cols = rows.shape
-    tiles = slot_of.shape[0]
+def place(place_of, blocks):
+    _, tile, cols = blocks[0].shape
+    slots = sum(block.shape[0] for block in blocks)
+    tiles = place_of.shape[0]
     return pl.pallas_call(
         place_kernel,
         grid_spec=pltpu.PrefetchScalarGridSpec(
             num_scalar_prefetch=1,
             grid=(1,),
-            in_specs=[pl.BlockSpec((slots, tile, cols), lambda i, s: (0, 0, 0))],
+            in_specs=[pl.BlockSpec(block.shape, lambda i, s: (0, 0, 0)) for block in blocks],
             out_specs=pl.BlockSpec((tiles * tile, cols), lambda i, s: (0, 0)),
+            scratch_shapes=[pltpu.VMEM((slots, tile, cols), blocks[0].dtype)],
         ),
-        out_shape=jax.ShapeDtypeStruct((tiles * tile, cols), rows.dtype),
-        compiler_params=pltpu.CompilerParams(vmem_limit_bytes=32 * 2**20),
-    )(slot_of, rows)
+        out_shape=jax.ShapeDtypeStruct((tiles * tile, cols), blocks[0].dtype),
+        compiler_params=pltpu.CompilerParams(vmem_limit_bytes=20 * 2**20),
+    )(place_of, *blocks)
 
 
 def spread(rows, axis):
@@ -142,34 +149,10 @@
     def hop(block):
         return lax.ppermute(block, ("zh", "zl", "c"), hops)
 
-    own = sampled.T
-    twin = lax.ppermute(own, "c", swap)
-    same, cross = [own], [twin]
-    for step in range(ring // 2):
-        same.append(hop(same[-1]))
-        if step < ring // 2 - 1:
-            cross.append(hop(cross[-1]))
-    far_twin = lax.ppermute(same[-1], "c", swap)
-
-    mine = jnp.dot(
-        inverse_rows.reshape(held * tile, order), gradient, preferred_element_type=jnp.float32
-    ).astype(jnp.bfloat16)
-    other = lax.ppermute(mine, "zh", [(0, 1), (1, 0)])
-    first = lax.axis_index("zh") == 0
-    rows = jnp.stack([jnp.where(first, mine, other), jnp.where(first, other, mine)])
-    rows = spread(rows.reshape(n_zh * held * tile, width), Y)
-    rows = rows.reshape(n_yh * n_yl * n_zh * held * tile, width)
-    rows, cross[2] = lax.optimization_barrier((rows, cross[2]))
-    rows = spread(rows, "x").reshape(owners * held, tile, width)
-    far_twin, rows = lax.optimization_barrier((far_twin, rows))
-    place_of = jnp.arange(owners * held, dtype=jnp.int32).reshape(n_x, n_yh * n_yl, n_zh, held)
-    slot_place = place_of.transpose(2, 0, 1, 3).reshape(-1)
-    preconditioned = place(slot_place[assignment], rows)
-
-    n_y = n_yh * n_yl
+    owner_slots = owners * held
     index = jnp.arange(tiles, dtype=jnp.int32)
-    table = jnp.full((owners * held,), -1, jnp.int32).at[assignment].set(index)
-    table = table.reshape(n_zh, n_x, n_y, held).transpose(1, 0, 2, 3).reshape(-1)
+    table = jnp.full((owner_slots,), -1, jnp.int32).at[assignment].set(index)
+    table = table.reshape(n_zh, n_x, n_yh, n_yl, held).transpose(1, 0, 2, 3, 4).reshape(-1)
     core, upper = lax.axis_index("c"), lax.axis_index("zh")
     here = upper * (ring // n_zh) + lax.axis_index("zl")
     share = cols // n_zh
@@ -181,15 +164,66 @@
         row = (chip % (ring // n_zh) * 2 + side) * cols
         more += [row, (chip // (ring // n_zh) != upper).astype(jnp.int32)]
     table = jnp.concatenate([table, jnp.stack(more).astype(jnp.int32)])
+
+    own = sampled.T
+    twin = lax.ppermute(own, "c", swap)
+    same, cross = [own, hop(own)], [twin, hop(twin)]
+
+    inverse_rows, twin = lax.optimization_barrier((inverse_rows, twin))
+    mine = jnp.dot(
+        inverse_rows.reshape(held * tile, order), gradient, preferred_element_type=jnp.float32
+    ).astype(jnp.bfloat16)
+    other = lax.ppermute(mine, "zh", swap)
+    same[1], other, table = lax.optimization_barrier((same[1], other, table))
+    rows = jnp.where(upper == 0, jnp.stack([mine, other]), jnp.stack([other, mine]))
+    rows = spread(rows.reshape(n_zh * held * tile, width), "x")
+    same.append(hop(same[1]))
+    cross.append(hop(cross[1]))
+    same[2], rows = lax.optimization_barrier((same[2], rows))
+    rows = rows.reshape(-1, tile, width)
+    n_y = n_yh * n_yl
+    up = [(n, (n + 1) % n_y) for n in range(n_y)]
+    down = [(n, (n - 1) % n_y) for n in range(n_y)]
+    below, above = [rows], [rows]
+
+    def pass_on():
+        below.append(lax.ppermute(below[-1], Y, up))
+        if len(below) <= n_y // 2:
+            above.append(lax.ppermute(above[-1], Y, down))
+
+    pass_on()
+    for step in range(2, ring // 2):
+        if step == ring // 2 - 1:
+            same[-1], below[1], above[1] = lax.optimization_barrier((same[-1], below[1], above[1]))
+        same.append(hop(same[-1]))
+        if step < ring // 2 - 1:
+            cross.append(hop(cross[-1]))
+    same[-1], cross[-1] = lax.optimization_barrier((same[-1], cross[-1]))
+    pass_on()
+    same[-1], below[2], above[2] = lax.optimization_barrier((same[-1], below[2], above[2]))
+    far_twin = lax.ppermute(same[-1], "c", swap)
+    pass_on()
+    pass_on()
+
     blocks = same + cross[1:]
-    sizes = (n_x, n_zh * n_y * held, tile, share)
+    near, far = n_x, n_zh * n_y
+    sizes = (near, far * held, tile, share)
     send = gram(table, twin, far_twin, blocks, *sizes)
     received = lax.ppermute(send, "c", swap)
     terms = gram(table, own, same[-1], blocks, *sizes) + received
-    terms = jnp.sum(lax.all_to_all(terms, "x", 0, 0), axis=0)
-    terms = lax.all_to_all(terms.reshape(n_zh * n_y, -1, terms.shape[1]), ("zh",) + Y, 0, 0)
+    terms = lax.all_to_all(terms, "x", 0, 0)
+    terms = functools.reduce(jnp.add, [terms[n] for n in range(near)])
+    terms, below[-1], above[-1] = lax.optimization_barrier((terms, below[-1], above[-1]))
+    terms = lax.all_to_all(terms.reshape(far, -1, terms.shape[1]), ("zh",) + Y, 0, 0)
     terms = terms.reshape((n_zh, n_y) + terms.shape[1:])
     factor_tiles = sum_join(terms, held, tile, cols, 1.0 / (tokens * owners))
+
+    owner, slot = assignment // held, assignment % held
+    down_by = (lax.axis_index(Y) - owner) % n_y
+    place_of = (down_by * n_x + owner // n_y % n_x) * n_zh + owner // (n_y * n_x)
+    preconditioned = place(
+        (place_of * held + slot).astype(jnp.int32), below + above[:0:-1]
+    )
     return factor_tiles, preconditioned
 
 

time: 164 us -> 152 us (0.927)
  blocking collectives: 27.7 us -> 0 us
  waiting for transfers between devices: 27.5 us -> 39.6 us
  starting transfers between devices: 70.1 us -> 81.4 us
  Pallas kernels: 17.6 us -> 13.7 us
  local copies, waits for them, and re-layouts: 10.8 us -> 7.3 us
    all_to_all x1 -> x0, blocking collectives: 27.7 us -> none  [body(): terms = jnp.sum(lax.all_to_all(terms, 'x', 0, 0), axis=0)]
    ppermute x1 -> x8, starting transfers between devices: 5.25 us -> 25 us  [the longest x4 13.9 us: pass_on(): below.append(lax.ppermute(below[-1], Y, up))]
    ppermute x7, waiting for transfers between devices: 16.8 us -> 2.18 us  [hop(): return lax.ppermute(block, ('zh', 'zl', 'c'), hops)]
    ppermute x1 -> x8, waiting for transfers between devices: 0.01 us -> 11.9 us  [the longest x4 5.17 us: pass_on(): below.append(lax.ppermute(below[-1], Y, up))]
    all_to_all x1 -> x2, waiting for transfers between devices: 10.7 us -> 19 us  [the longest x1 10.6 us: body(): lax.all_to_all(terms.reshape(far, -1, terms.shape[1]), ('zh',) + Y, 0, 0)]
    all_to_all x2 -> x1, starting transfers between devices: 11.5 us -> 4.08 us  [spread(): return lax.all_to_all(copies, axis, 0, 0)]
    all_to_all x1 -> x2, starting transfers between devices: 8.51 us -> 13.9 us  [the longest x1 9.35 us: body(): lax.all_to_all(terms.reshape(far, -1, terms.shape[1]), ('zh',) + Y, 0, 0)]
    all_to_all x2 -> x1, waiting for transfers between devices: 0.01 us -> 4.94 us  [spread(): return lax.all_to_all(copies, axis, 0, 0)]
  transfers between devices with their start and end apart: 14 -> 21, of which waited for: 6 -> 9; matrix products, arithmetic and copies ran while one was open for 7% -> 5% of each run, Pallas kernels for 6% -> 5%
where the time goes in v6:
time: 152 us; the launch traced here: 150 us
  starting transfers between devices  81.4 us (54%)
  waiting for transfers between devices  39.6 us (26%)
  Pallas kernels  13.7 us (9%)
  local copies, waits for them, and re-layouts  7.3 us (5%)
  other arithmetic  4.58 us (3%)
  matrix products  2 us (1%)
    ppermute x7, starting transfers between devices, hop(): return lax.ppermute(block, ('zh', 'zl', 'c'), hops)  20 us
    ppermute x4, starting transfers between devices, pass_on(): below.append(lax.ppermute(below[-1], Y, up))  13.9 us
    all_to_all x1, waiting for transfers between devices, body(): lax.all_to_all(terms.reshape(far, -1, terms.shape[1]), ('zh',) + Y, 0, 0)  10.6 us
    all_to_all x1, starting transfers between devices, body(): lax.all_to_all(terms.reshape(far, -1, terms.shape[1]), ('zh',) + Y, 0, 0)  9.35 us
    ppermute x3, starting transfers between devices, pass_on(): above.append(lax.ppermute(above[-1], Y, down))  9.17 us
    ppermute x1, starting transfers between devices, body(): twin = lax.ppermute(own, 'c', swap)  8.92 us
    pallas_call x2, Pallas kernels, gram(): pl.pallas_call(lambda table_ref, *refs: gram_kernel(table_ref, slots, *re...  8.69 us
    all_to_all x1, waiting for transfers between devices, body(): terms = lax.all_to_all(terms, 'x', 0, 0)  8.38 us
  transfers between devices with their start and end apart: 21, of which 9 were waited for; matrix products, arithmetic and copies ran while one was open for 5% of the time, Pallas kernels for 5%

profile of v6, /device:TPU:1, one launch (start us, length us, event | category | flops | bytes accessed | tf_op | source)
XLA Modules:
  0.0 149.8 jit_solution(8585594032161636754)
XLA Ops:
  0.6 0.0 copy-start
  0.7 8.9 %collective-permute-start.1 = (bf16[288,1024]{1,0:T(8,128)(2,1)}, bf16[288,1024]{1,0:T(8,128)(2,1)S(1)}, u32[]{:S(2)}, u32[]{:S(2)}) collective-permute-start(bf16[288,1024]{1,0:T(8,128)(2,1)} %bitcast.27), channel_id=1, source_target_pairs={{0,1},{1,0},{2,3},{3,2},{4,5},{5,4},{6,7},{7,6},{8,9},{9,8},{10,11... | collective-permute-start | bytes 1769480 | tf_op jit(solution)/shard_map/ppermute | solution.py:169
  9.6 5.3 %collective-permute-start = (bf16[288,1024]{1,0:T(8,128)(2,1)}, bf16[288,1024]{1,0:T(8,128)(2,1)S(1)}, u32[]{:S(2)}, u32[]{:S(2)}) collective-permute-start(bf16[288,1024]{1,0:T(8,128)(2,1)} %bitcast.28), channel_id=1, source_target_pairs={{0,2},{2,4},{4,6},{6,256},{256,258},{258,260},{260,262},{262,0},{1... | collective-permute-start | bytes 1769480 | tf_op jit(solution)/shard_map/ppermute | solution.py:150
  14.9 0.0 collective-permute-done.1.refs_0_
  14.9 0.0 copy-start.2
  14.9 0.8 copy-done.2
  15.7 2.0 %convolution_convert_fusion = bf16[48,384]{1,0:T(8,128)(2,1)} fusion(bf16[48,2304]{1,0:T(8,128)(2,1)} %bitcast.34, bf16[2304,384]{1,0:T(8,128)(2,1)S(1)} %copy-done), kind=kOutput, calls=%fused_computation.1 | convolution fusion | flops 84953088 | bytes 2027520 | tf_op jit(solution)/shard_map/dot_general | solution.py:173
  17.7 1.9 %collective-permute-start.2 = (bf16[48,384]{1,0:T(8,128)(2,1)}, bf16[48,384]{1,0:T(8,128)(2,1)}, u32[]{:S(2)}, u32[]{:S(2)}) collective-permute-start(bf16[48,384]{1,0:T(8,128)(2,1)} %convolution_convert_fusion), channel_id=1, source_target_pairs={{0,256},{256,0},{1,257},{257,1},{2,258},{258,2},{3,259},{259,3},{4... | collective-permute-start | bytes 110600 | tf_op jit(solution)/shard_map/ppermute | solution.py:176
  19.9 0.9 scatter_custom_fusion
  20.8 0.2 reshape.37
  21.0 0.1 reshape.38
  21.1 0.1 concatenate.3.table_ref
  21.2 2.2 %collective-permute-start.8 = (bf16[288,1024]{1,0:T(8,128)(2,1)}, bf16[288,1024]{1,0:T(8,128)(2,1)S(1)}, u32[]{:S(2)}, u32[]{:S(2)}) collective-permute-start(bf16[288,1024]{1,0:T(8,128)(2,1)} %copy-done.2), channel_id=1, source_target_pairs={{0,2},{2,4},{4,6},{6,256},{256,258},{258,260},{260,262},{262,0},{1... | collective-permute-start | bytes 1769480 | tf_op jit(solution)/shard_map/ppermute | solution.py:150
  23.4 0.0 collective-permute-done.refs_3_
  23.4 3.6 %collective-permute-done.2 = bf16[48,384]{1,0:T(8,128)(2,1)} collective-permute-done((bf16[48,384]{1,0:T(8,128)(2,1)}, bf16[48,384]{1,0:T(8,128)(2,1)}, u32[]{:S(2)}, u32[]{:S(2)}) %collective-permute-start.2) | collective-permute-done | bytes 36896 | tf_op jit(solution)/shard_map/ppermute | solution.py:176
  27.0 2.6 %collective-permute-start.3 = (bf16[288,1024]{1,0:T(8,128)(2,1)S(1)}, bf16[288,1024]{1,0:T(8,128)(2,1)}, u32[]{:S(2)}, u32[]{:S(2)}) collective-permute-start(bf16[288,1024]{1,0:T(8,128)(2,1)S(1)} %collective-permute-done.refs_3_), channel_id=1, source_target_pairs={{0,2},{2,4},{4,6},{6,256},{256,258},{258,260},{260,262},{262,0},{1... | collective-permute-start | bytes 1769480 | tf_op jit(solution)/shard_map/ppermute | solution.py:150
  29.7 0.9 maximum_select_fusion
  30.6 0.7 broadcast_in_dim.13
  31.3 4.1 %all-to-all-start = ((bf16[4,96,384]{2,1,0:T(8,128)(2,1)}), bf16[4,96,384]{2,1,0:T(8,128)(2,1)}, u32[]{:S(2)}, u32[]{:S(2)}) async-start(bf16[4,96,384]{2,1,0:T(8,128)(2,1)} %broadcast_in_dim.13), calls=%async_computation | async-start | bytes 589824 | tf_op jit(solution)/shard_map/all_to_all | solution.py:133
  35.4 0.0 collective-permute-done.8.refs_7_
  35.4 1.9 %collective-permute-start.9 = (bf16[288,1024]{1,0:T(8,128)(2,1)S(1)}, bf16[288,1024]{1,0:T(8,128)(2,1)}, u32[]{:S(2)}, u32[]{:S(2)}) collective-permute-start(bf16[288,1024]{1,0:T(8,128)(2,1)S(1)} %collective-permute-done.8.refs_7_), channel_id=1, source_target_pairs={{0,2},{2,4},{4,6},{6,256},{256,258},{258,260},{260,262},{262,0},{1... | collective-permute-start | bytes 1769480 | tf_op jit(solution)/shard_map/ppermute | solution.py:150
  37.3 4.9 %all-to-all-done = bf16[4,96,384]{2,1,0:T(8,128)(2,1)} async-done(((bf16[4,96,384]{2,1,0:T(8,128)(2,1)}), bf16[4,96,384]{2,1,0:T(8,128)(2,1)}, u32[]{:S(2)}, u32[]{:S(2)}) %all-to-all-start) | async-done | bytes 294944 | tf_op jit(solution)/shard_map/all_to_all | solution.py:133
  42.3 0.0 collective-permute-done.3.refs_4_
  42.3 1.9 %collective-permute-start.4 = (bf16[288,1024]{1,0:T(8,128)(2,1)}, bf16[288,1024]{1,0:T(8,128)(2,1)S(1)}, u32[]{:S(2)}, u32[]{:S(2)}) collective-permute-start(bf16[288,1024]{1,0:T(8,128)(2,1)} %collective-permute-done.3.refs_4_), channel_id=1, source_target_pairs={{0,2},{2,4},{4,6},{6,256},{256,258},{258,260},{260,262},{262,0},{1... | collective-permute-start | bytes 1769480 | tf_op jit(solution)/shard_map/ppermute | solution.py:150
  44.2 2.7 %collective-permute-start.5 = (bf16[16,24,384]{2,1,0:T(8,128)(2,1)}, bf16[16,24,384]{2,1,0:T(8,128)(2,1)S(1)}, u32[]{:S(2)}, u32[]{:S(2)}) collective-permute-start(bf16[16,24,384]{2,1,0:T(8,128)(2,1)} %bitcast.20.refs_0_), channel_id=1, source_target_pairs={{0,8},{8,16},{16,24},{24,32},{32,40},{40,48},{48,56},{56,0},{1,9},... | collective-permute-start | bytes 884744 | tf_op jit(solution)/shard_map/ppermute | solution.py:190
  46.9 3.8 %collective-permute-start.6 = (bf16[16,24,384]{2,1,0:T(8,128)(2,1)}, bf16[16,24,384]{2,1,0:T(8,128)(2,1)S(1)}, u32[]{:S(2)}, u32[]{:S(2)}) collective-permute-start(bf16[16,24,384]{2,1,0:T(8,128)(2,1)} %bitcast.20.refs_0_), channel_id=1, source_target_pairs={{0,56},{8,0},{16,8},{24,16},{32,24},{40,32},{48,40},{56,48},{1,57}... | collective-permute-start | bytes 884744 | tf_op jit(solution)/shard_map/ppermute | solution.py:192
  50.7 0.0 collective-permute-done.9.refs_8_
  50.7 3.0 %collective-permute-start.10 = (bf16[288,1024]{1,0:T(8,128)(2,1)}, bf16[288,1024]{1,0:T(8,128)(2,1)S(1)}, u32[]{:S(2)}, u32[]{:S(2)}) collective-permute-start(bf16[288,1024]{1,0:T(8,128)(2,1)} %collective-permute-done.9.refs_8_), channel_id=1, source_target_pairs={{0,2},{2,4},{4,6},{6,256},{256,258},{258,260},{260,262},{262,0},{1... | collective-permute-start | bytes 1769480 | tf_op jit(solution)/shard_map/ppermute | solution.py:150
  53.8 0.0 collective-permute-done.5.refs_1_
  53.8 1.1 collective-permute-done.6.refs_7_
  54.9 0.0 collective-permute-done.4.refs_5_
  54.9 3.0 %collective-permute-start.7 = (bf16[288,1024]{1,0:T(8,128)(2,1)S(1)}, bf16[288,1024]{1,0:T(8,128)(2,1)S(1)}, u32[]{:S(2)}, u32[]{:S(2)}) collective-permute-start(bf16[288,1024]{1,0:T(8,128)(2,1)S(1)} %collective-permute-done.4.refs_5_), channel_id=1, source_target_pairs={{0,2},{2,4},{4,6},{6,256},{256,258},{258,260},{260,262},{262,0},{1... | collective-permute-start | bytes 1769480 | tf_op jit(solution)/shard_map/ppermute | solution.py:150
  57.9 3.2 %collective-permute-start.11 = (bf16[16,24,384]{2,1,0:T(8,128)(2,1)S(1)}, bf16[16,24,384]{2,1,0:T(8,128)(2,1)S(1)}, u32[]{:S(2)}, u32[]{:S(2)}) collective-permute-start(bf16[16,24,384]{2,1,0:T(8,128)(2,1)S(1)} %collective-permute-done.5.refs_1_), channel_id=1, source_target_pairs={{0,8},{8,16},{16,24},{24,32},{32,40},{40,48},{48,56},{56,0},{1,9},... | collective-permute-start | bytes 884744 | tf_op jit(solution)/shard_map/ppermute | solution.py:190
  61.1 0.7 copy-done.4
  61.8 3.4 %collective-permute-start.12 = (bf16[16,24,384]{2,1,0:T(8,128)(2,1)S(1)}, bf16[16,24,384]{2,1,0:T(8,128)(2,1)S(1)}, u32[]{:S(2)}, u32[]{:S(2)}) collective-permute-start(bf16[16,24,384]{2,1,0:T(8,128)(2,1)S(1)} %collective-permute-done.6.refs_7_), channel_id=1, source_target_pairs={{0,56},{8,0},{16,8},{24,16},{32,24},{40,32},{48,40},{56,48},{1,57}... | collective-permute-start | bytes 884744 | tf_op jit(solution)/shard_map/ppermute | solution.py:192
  65.3 0.7 copy-done.6
  66.0 0.0 collective-permute-done.10.refs_9_
  66.0 2.2 %collective-permute-done.7.refs_1_.refs_6_ = bf16[288,1024]{1,0:T(8,128)(2,1)S(1)} collective-permute-done((bf16[288,1024]{1,0:T(8,128)(2,1)S(1)}, bf16[288,1024]{1,0:T(8,128)(2,1)S(1)}, u32[]{:S(2)}, u32[]{:S(2)}) %collective-permute-start.7) | collective-permute-done | bytes 589856 | tf_op jit(solution)/shard_map/ppermute | solution.py:150
  68.2 0.0 collective-permute-done.11.refs_2_
  68.2 2.0 %collective-permute-done.12.refs_6_ = bf16[16,24,384]{2,1,0:T(8,128)(2,1)S(1)} collective-permute-done((bf16[16,24,384]{2,1,0:T(8,128)(2,1)S(1)}, bf16[16,24,384]{2,1,0:T(8,128)(2,1)S(1)}, u32[]{:S(2)}, u32[]{:S(2)}) %collective-permute-start.12) | collective-permute-done | bytes 294944 | tf_op jit(solution)/shard_map/ppermute | solution.py:192
  70.2 7.2 %collective-permute-start.13 = (bf16[288,1024]{1,0:T(8,128)(2,1)S(1)}, bf16[288,1024]{1,0:T(8,128)(2,1)S(1)}, u32[]{:S(2)}, u32[]{:S(2)}) collective-permute-start(bf16[288,1024]{1,0:T(8,128)(2,1)S(1)} %collective-permute-done.7.refs_1_.refs_6_), channel_id=1, source_target_pairs={{0,1},{1,0},{2,3},{3,2},{4,5},{5,4},{6,7},{7,6},{8,9},{9,8},{10,11... | collective-permute-start | bytes 1769480 | tf_op jit(solution)/shard_map/ppermute | solution.py:204
  77.4 1.6 %collective-permute-done.13.refs_1_ = bf16[288,1024]{1,0:T(8,128)(2,1)S(1)} collective-permute-done((bf16[288,1024]{1,0:T(8,128)(2,1)S(1)}, bf16[288,1024]{1,0:T(8,128)(2,1)S(1)}, u32[]{:S(2)}, u32[]{:S(2)}) %collective-permute-start.13) | collective-permute-done | bytes 589856 | tf_op jit(solution)/shard_map/ppermute | solution.py:204
  79.0 1.1 copy-done.3
  80.1 4.3 %shard_map.60 = f32[4,896,128]{2,1,0:T(8,128)S(1)} custom-call(s32[145]{0:T(256)S(1)} %concatenate.3.table_ref, bf16[288,1024]{1,0:T(8,128)(2,1)S(1)} %copy-done.3, bf16[288,1024]{1,0:T(8,128)(2,1)S(1)} %collective-permute-done.13.refs_1_, bf16[288,1024]{1,0:T(8,128)(2,1)S(1)} %bitcast.29, bf16[288,1024]{1,0:T(8,128)(2,1)S(1)} %collective-permute-done.refs_3_, ...), custom_call_target="tpu_custom_call" | custom-call | tf_op jit(solution)/shard_map/pallas_call | solution.py:58
  84.4 2.3 %collective-permute-start.14 = (f32[4,896,128]{2,1,0:T(8,128)S(1)}, f32[4,896,128]{2,1,0:T(8,128)S(1)}, u32[]{:S(2)}, u32[]{:S(2)}) collective-permute-start(f32[4,896,128]{2,1,0:T(8,128)S(1)} %shard_map.60), channel_id=1, source_target_pairs={{0,1},{1,0},{2,3},{3,2},{4,5},{5,4},{6,7},{7,6},{8,9},{9,8},{10,11... | collective-permute-start | bytes 5505032 | tf_op jit(solution)/shard_map/ppermute | solution.py:212
  86.7 4.4 %shard_map.59 = f32[4,896,128]{2,1,0:T(8,128)S(1)} custom-call(s32[145]{0:T(256)S(1)} %concatenate.3.table_ref, bf16[288,1024]{1,0:T(8,128)(2,1)S(1)} %bitcast.30, bf16[288,1024]{1,0:T(8,128)(2,1)S(1)} %collective-permute-done.7.refs_1_.refs_6_, bf16[288,1024]{1,0:T(8,128)(2,1)S(1)} %bitcast.31, bf16[288,1024]{1,0:T(8,128)(2,1)S(1)} %collective-permute-done.refs_3_, ...), custom_call_target="tpu_custom_call" | custom-call | tf_op jit(solution)/shard_map/pallas_call | solution.py:58
  91.1 0.0 collective-permute-done.14
  91.1 1.4 add.165
  92.5 4.5 %all-to-all-start.1 = ((f32[4,896,128]{2,1,0:T(8,128)}), f32[4,896,128]{2,1,0:T(8,128)}, u32[]{:S(2)}, u32[]{:S(2)}) async-start(f32[4,896,128]{2,1,0:T(8,128)} %add.165), calls=%async_computation.1 | async-start | bytes 3670016 | tf_op jit(solution)/shard_map/all_to_all | solution.py:214
  97.1 4.7 %collective-permute-start.15 = (bf16[16,24,384]{2,1,0:T(8,128)(2,1)S(1)}, bf16[16,24,384]{2,1,0:T(8,128)(2,1)S(1)}, u32[]{:S(2)}, u32[]{:S(2)}) collective-permute-start(bf16[16,24,384]{2,1,0:T(8,128)(2,1)S(1)} %copy-done.9), channel_id=1, source_target_pairs={{0,8},{8,16},{16,24},{24,32},{32,40},{40,48},{48,56},{56,0},{1,9},... | collective-permute-start | bytes 884744 | tf_op jit(solution)/shard_map/ppermute | solution.py:190
  101.8 1.9 %collective-permute-start.17 = (bf16[16,24,384]{2,1,0:T(8,128)(2,1)S(1)}, bf16[16,24,384]{2,1,0:T(8,128)(2,1)S(1)}, u32[]{:S(2)}, u32[]{:S(2)}) collective-permute-start(bf16[16,24,384]{2,1,0:T(8,128)(2,1)S(1)} %copy-done.11), channel_id=1, source_target_pairs={{0,56},{8,0},{16,8},{24,16},{32,24},{40,32},{48,40},{56,48},{1,57}... | collective-permute-start | bytes 884744 | tf_op jit(solution)/shard_map/ppermute | solution.py:192
  103.7 5.2 %collective-permute-done.15.refs_3_ = bf16[16,24,384]{2,1,0:T(8,128)(2,1)S(1)} collective-permute-done((bf16[16,24,384]{2,1,0:T(8,128)(2,1)S(1)}, bf16[16,24,384]{2,1,0:T(8,128)(2,1)S(1)}, u32[]{:S(2)}, u32[]{:S(2)}) %collective-permute-start.15) | collective-permute-done | bytes 294944 | tf_op jit(solution)/shard_map/ppermute | solution.py:190
  108.9 3.3 %collective-permute-start.16 = (bf16[16,24,384]{2,1,0:T(8,128)(2,1)S(1)}, bf16[16,24,384]{2,1,0:T(8,128)(2,1)}, u32[]{:S(2)}, u32[]{:S(2)}) collective-permute-start(bf16[16,24,384]{2,1,0:T(8,128)(2,1)S(1)} %collective-permute-done.15.refs_3_), channel_id=1, source_target_pairs={{0,8},{8,16},{16,24},{24,32},{32,40},{40,48},{48,56},{56,0},{1,9},... | collective-permute-start | bytes 884744 | tf_op jit(solution)/shard_map/ppermute | solution.py:190
  112.2 8.4 %all-to-all-done.1 = f32[4,896,128]{2,1,0:T(8,128)} async-done(((f32[4,896,128]{2,1,0:T(8,128)}), f32[4,896,128]{2,1,0:T(8,128)}, u32[]{:S(2)}, u32[]{:S(2)}) %all-to-all-start.1) | async-done | bytes 1835040 | tf_op jit(solution)/shard_map/all_to_all | solution.py:214
  120.6 2.3 %fusion = f32[896,128]{1,0:T(8,128)} fusion(f32[4,896,128]{2,1,0:T(8,128)} %all-to-all-done.1), kind=kLoop, calls=%fused_computation.3 | loop fusion | flops 344064 | bytes 2293760 | tf_op jit(solution)/shard_map/add | solution.py:215
  122.9 0.0 collective-permute-done.17.refs_5_
  122.9 0.0 collective-permute-done.16.refs_4_
  122.9 9.3 %all-to-all-start.2 = ((f32[16,56,128]{2,1,0:T(8,128)}), f32[16,56,128]{2,1,0:T(8,128)}, u32[]{:S(2)}, u32[]{:S(2)}) async-start(f32[16,56,128]{2,1,0:T(8,128)} %bitcast.32), calls=%async_computation.2 | async-start | bytes 917504 | tf_op jit(solution)/shard_map/all_to_all | solution.py:217
  132.3 0.0 copy-start.13
  132.3 1.0 copy-done.13
  133.3 1.0 copy-done.15
  134.2 3.2 %shard_map.62 = bf16[2304,384]{1,0:T(8,128)(2,1)} custom-call(s32[96]{0:T(128)S(1)} %get-tuple-element.38.place_of, bf16[16,24,384]{2,1,0:T(8,128)(2,1)} %bitcast.20.refs_0_, bf16[16,24,384]{2,1,0:T(8,128)(2,1)S(1)} %copy-done.5, bf16[16,24,384]{2,1,0:T(8,128)(2,1)S(1)} %copy-done.9, bf16[16,24,384]{2,1,0:T(8,128)(2,1)S(1)} %copy-done.13, ...), custom_call_target="tpu_custom_call" | custom-call | tf_op jit(solution)/shard_map/pallas_call | solution.py:117
  137.4 10.6 %all-to-all-done.2 = f32[16,56,128]{2,1,0:T(8,128)} async-done(((f32[16,56,128]{2,1,0:T(8,128)}), f32[16,56,128]{2,1,0:T(8,128)}, u32[]{:S(2)}, u32[]{:S(2)}) %all-to-all-start.2) | async-done | bytes 458784 | tf_op jit(solution)/shard_map/all_to_all | solution.py:217
  148.0 1.8 %shard_map.61 = f32[2,24,288]{2,1,0:T(8,128)} custom-call(f32[2,8,56,128]{3,2,1,0:T(8,128)} %bitcast.23.parts_ref), custom_call_target="tpu_custom_call" | custom-call | tf_op jit(solution)/shard_map/pallas_call | solution.py:93
  (28 shorter events, 0.1 us)
Async XLA Ops:
  0.6 15.1 %copy-start = (bf16[2304,384]{1,0:T(8,128)(2,1)S(1)}, bf16[2304,384]{1,0:T(8,128)(2,1)}, u32[]{:S(2)}) copy-start(bf16[2304,384]{1,0:T(8,128)(2,1)} %param.7) | copy-start | bytes 5308420
  0.6 19.0 %copy-start.16 = (s32[96]{0:T(128)S(1)}, s32[96]{0:T(128)}, u32[]{:S(2)}) copy-start(s32[96]{0:T(128)} %param.5) | copy-start | bytes 1156
  0.7 14.2 %collective-permute-start.1 = (bf16[288,1024]{1,0:T(8,128)(2,1)}, bf16[288,1024]{1,0:T(8,128)(2,1)S(1)}, u32[]{:S(2)}, u32[]{:S(2)}) collective-permute-start(bf16[288,1024]{1,0:T(8,128)(2,1)} %bitcast.27), channel_id=1, source_target_pairs={{0,1},{1,0},{2,3},{3,2},{4,5},{5,4},{6,7},{7,6},{8,9},{9,8},{10,11... | collective-permute-start | bytes 1769480 | tf_op jit(solution)/shard_map/ppermute | solution.py:169
  9.6 13.8 %collective-permute-start = (bf16[288,1024]{1,0:T(8,128)(2,1)}, bf16[288,1024]{1,0:T(8,128)(2,1)S(1)}, u32[]{:S(2)}, u32[]{:S(2)}) collective-permute-start(bf16[288,1024]{1,0:T(8,128)(2,1)} %bitcast.28), channel_id=1, source_target_pairs={{0,2},{2,4},{4,6},{6,256},{256,258},{258,260},{260,262},{262,0},{1... | collective-permute-start | bytes 1769480 | tf_op jit(solution)/shard_map/ppermute | solution.py:150
  14.9 0.8 copy-start.2
  15.7 63.3 %copy-start.1 = (bf16[1024,288]{0,1:T(8,128)(2,1)S(1)}, bf16[1024,288]{0,1:T(8,128)(2,1)}, u32[]{:S(2)}) copy-start(bf16[1024,288]{0,1:T(8,128)(2,1)} %param.4) | copy-start | bytes 1769476
  17.7 9.3 %collective-permute-start.2 = (bf16[48,384]{1,0:T(8,128)(2,1)}, bf16[48,384]{1,0:T(8,128)(2,1)}, u32[]{:S(2)}, u32[]{:S(2)}) collective-permute-start(bf16[48,384]{1,0:T(8,128)(2,1)} %convolution_convert_fusion), channel_id=1, source_target_pairs={{0,256},{256,0},{1,257},{257,1},{2,258},{258,2},{3,259},{259,3},{4... | collective-permute-start | bytes 110600 | tf_op jit(solution)/shard_map/ppermute | solution.py:176
  21.2 14.1 %collective-permute-start.8 = (bf16[288,1024]{1,0:T(8,128)(2,1)}, bf16[288,1024]{1,0:T(8,128)(2,1)S(1)}, u32[]{:S(2)}, u32[]{:S(2)}) collective-permute-start(bf16[288,1024]{1,0:T(8,128)(2,1)} %copy-done.2), channel_id=1, source_target_pairs={{0,2},{2,4},{4,6},{6,256},{256,258},{258,260},{260,262},{262,0},{1... | collective-permute-start | bytes 1769480 | tf_op jit(solution)/shard_map/ppermute | solution.py:150
  27.0 15.2 %collective-permute-start.3 = (bf16[288,1024]{1,0:T(8,128)(2,1)S(1)}, bf16[288,1024]{1,0:T(8,128)(2,1)}, u32[]{:S(2)}, u32[]{:S(2)}) collective-permute-start(bf16[288,1024]{1,0:T(8,128)(2,1)S(1)} %collective-permute-done.refs_3_), channel_id=1, source_target_pairs={{0,2},{2,4},{4,6},{6,256},{256,258},{258,260},{260,262},{262,0},{1... | collective-permute-start | bytes 1769480 | tf_op jit(solution)/shard_map/ppermute | solution.py:150
  31.3 11.0 %all-to-all-start = ((bf16[4,96,384]{2,1,0:T(8,128)(2,1)}), bf16[4,96,384]{2,1,0:T(8,128)(2,1)}, u32[]{:S(2)}, u32[]{:S(2)}) async-start(bf16[4,96,384]{2,1,0:T(8,128)(2,1)} %broadcast_in_dim.13), calls=%async_computation | async-start | bytes 589824 | tf_op jit(solution)/shard_map/all_to_all | solution.py:133
  35.4 15.3 %collective-permute-start.9 = (bf16[288,1024]{1,0:T(8,128)(2,1)S(1)}, bf16[288,1024]{1,0:T(8,128)(2,1)}, u32[]{:S(2)}, u32[]{:S(2)}) collective-permute-start(bf16[288,1024]{1,0:T(8,128)(2,1)S(1)} %collective-permute-done.8.refs_7_), channel_id=1, source_target_pairs={{0,2},{2,4},{4,6},{6,256},{256,258},{258,260},{260,262},{262,0},{1... | collective-permute-start | bytes 1769480 | tf_op jit(solution)/shard_map/ppermute | solution.py:150
  42.3 12.6 %collective-permute-start.4 = (bf16[288,1024]{1,0:T(8,128)(2,1)}, bf16[288,1024]{1,0:T(8,128)(2,1)S(1)}, u32[]{:S(2)}, u32[]{:S(2)}) collective-permute-start(bf16[288,1024]{1,0:T(8,128)(2,1)} %collective-permute-done.3.refs_4_), channel_id=1, source_target_pairs={{0,2},{2,4},{4,6},{6,256},{256,258},{258,260},{260,262},{262,0},{1... | collective-permute-start | bytes 1769480 | tf_op jit(solution)/shard_map/ppermute | solution.py:150
  44.2 9.6 %collective-permute-start.5 = (bf16[16,24,384]{2,1,0:T(8,128)(2,1)}, bf16[16,24,384]{2,1,0:T(8,128)(2,1)S(1)}, u32[]{:S(2)}, u32[]{:S(2)}) collective-permute-start(bf16[16,24,384]{2,1,0:T(8,128)(2,1)} %bitcast.20.refs_0_), channel_id=1, source_target_pairs={{0,8},{8,16},{16,24},{24,32},{32,40},{40,48},{48,56},{56,0},{1,9},... | collective-permute-start | bytes 884744 | tf_op jit(solution)/shard_map/ppermute | solution.py:190
  46.9 8.0 %collective-permute-start.6 = (bf16[16,24,384]{2,1,0:T(8,128)(2,1)}, bf16[16,24,384]{2,1,0:T(8,128)(2,1)S(1)}, u32[]{:S(2)}, u32[]{:S(2)}) collective-permute-start(bf16[16,24,384]{2,1,0:T(8,128)(2,1)} %bitcast.20.refs_0_), channel_id=1, source_target_pairs={{0,56},{8,0},{16,8},{24,16},{32,24},{40,32},{48,40},{56,48},{1,57}... | collective-permute-start | bytes 884744 | tf_op jit(solution)/shard_map/ppermute | solution.py:192
  50.7 15.3 %collective-permute-start.10 = (bf16[288,1024]{1,0:T(8,128)(2,1)}, bf16[288,1024]{1,0:T(8,128)(2,1)S(1)}, u32[]{:S(2)}, u32[]{:S(2)}) collective-permute-start(bf16[288,1024]{1,0:T(8,128)(2,1)} %collective-permute-done.9.refs_8_), channel_id=1, source_target_pairs={{0,2},{2,4},{4,6},{6,256},{256,258},{258,260},{260,262},{262,0},{1... | collective-permute-start | bytes 1769480 | tf_op jit(solution)/shard_map/ppermute | solution.py:150
  54.9 13.3 %collective-permute-start.7 = (bf16[288,1024]{1,0:T(8,128)(2,1)S(1)}, bf16[288,1024]{1,0:T(8,128)(2,1)S(1)}, u32[]{:S(2)}, u32[]{:S(2)}) collective-permute-start(bf16[288,1024]{1,0:T(8,128)(2,1)S(1)} %collective-permute-done.4.refs_5_), channel_id=1, source_target_pairs={{0,2},{2,4},{4,6},{6,256},{256,258},{258,260},{260,262},{262,0},{1... | collective-permute-start | bytes 1769480 | tf_op jit(solution)/shard_map/ppermute | solution.py:150
  57.9 10.3 %collective-permute-start.11 = (bf16[16,24,384]{2,1,0:T(8,128)(2,1)S(1)}, bf16[16,24,384]{2,1,0:T(8,128)(2,1)S(1)}, u32[]{:S(2)}, u32[]{:S(2)}) collective-permute-start(bf16[16,24,384]{2,1,0:T(8,128)(2,1)S(1)} %collective-permute-done.5.refs_1_), channel_id=1, source_target_pairs={{0,8},{8,16},{16,24},{24,32},{32,40},{40,48},{48,56},{56,0},{1,9},... | collective-permute-start | bytes 884744 | tf_op jit(solution)/shard_map/ppermute | solution.py:190
  61.1 0.7 copy-start.4
  61.8 8.4 %collective-permute-start.12 = (bf16[16,24,384]{2,1,0:T(8,128)(2,1)S(1)}, bf16[16,24,384]{2,1,0:T(8,128)(2,1)S(1)}, u32[]{:S(2)}, u32[]{:S(2)}) collective-permute-start(bf16[16,24,384]{2,1,0:T(8,128)(2,1)S(1)} %collective-permute-done.6.refs_7_), channel_id=1, source_target_pairs={{0,56},{8,0},{16,8},{24,16},{32,24},{40,32},{48,40},{56,48},{1,57}... | collective-permute-start | bytes 884744 | tf_op jit(solution)/shard_map/ppermute | solution.py:192
  65.3 0.7 copy-start.6
  68.2 9.2 %copy-start.8 = (bf16[16,24,384]{2,1,0:T(8,128)(2,1)}, bf16[16,24,384]{2,1,0:T(8,128)(2,1)S(1)}, u32[]{:S(2)}) copy-start(bf16[16,24,384]{2,1,0:T(8,128)(2,1)S(1)} %collective-permute-done.11.refs_2_) | copy-start | bytes 884740
  70.2 7.2 %copy-start.10 = (bf16[16,24,384]{2,1,0:T(8,128)(2,1)}, bf16[16,24,384]{2,1,0:T(8,128)(2,1)S(1)}, u32[]{:S(2)}) copy-start(bf16[16,24,384]{2,1,0:T(8,128)(2,1)S(1)} %collective-permute-done.12.refs_6_) | copy-start | bytes 884740
  70.2 8.8 %collective-permute-start.13 = (bf16[288,1024]{1,0:T(8,128)(2,1)S(1)}, bf16[288,1024]{1,0:T(8,128)(2,1)S(1)}, u32[]{:S(2)}, u32[]{:S(2)}) collective-permute-start(bf16[288,1024]{1,0:T(8,128)(2,1)S(1)} %collective-permute-done.7.refs_1_.refs_6_), channel_id=1, source_target_pairs={{0,1},{1,0},{2,3},{3,2},{4,5},{5,4},{6,7},{7,6},{8,9},{9,8},{10,11... | collective-permute-start | bytes 1769480 | tf_op jit(solution)/shard_map/ppermute | solution.py:204
  79.0 1.1 copy-start.3
  84.4 6.7 %collective-permute-start.14 = (f32[4,896,128]{2,1,0:T(8,128)S(1)}, f32[4,896,128]{2,1,0:T(8,128)S(1)}, u32[]{:S(2)}, u32[]{:S(2)}) collective-permute-start(f32[4,896,128]{2,1,0:T(8,128)S(1)} %shard_map.60), channel_id=1, source_target_pairs={{0,1},{1,0},{2,3},{3,2},{4,5},{5,4},{6,7},{7,6},{8,9},{9,8},{10,11... | collective-permute-start | bytes 5505032 | tf_op jit(solution)/shard_map/ppermute | solution.py:212
  92.5 4.5 %copy-start.9 = (bf16[16,24,384]{2,1,0:T(8,128)(2,1)S(1)}, bf16[16,24,384]{2,1,0:T(8,128)(2,1)}, u32[]{:S(2)}) copy-start(bf16[16,24,384]{2,1,0:T(8,128)(2,1)} %copy-done.8) | copy-start | bytes 884740
  92.5 9.3 %copy-start.11 = (bf16[16,24,384]{2,1,0:T(8,128)(2,1)S(1)}, bf16[16,24,384]{2,1,0:T(8,128)(2,1)}, u32[]{:S(2)}) copy-start(bf16[16,24,384]{2,1,0:T(8,128)(2,1)} %copy-done.10) | copy-start | bytes 884740
  92.5 28.1 %all-to-all-start.1 = ((f32[4,896,128]{2,1,0:T(8,128)}), f32[4,896,128]{2,1,0:T(8,128)}, u32[]{:S(2)}, u32[]{:S(2)}) async-start(f32[4,896,128]{2,1,0:T(8,128)} %add.165), calls=%async_computation.1 | async-start | bytes 3670016 | tf_op jit(solution)/shard_map/all_to_all | solution.py:214
  97.0 35.2 %copy-start.5 = (bf16[16,24,384]{2,1,0:T(8,128)(2,1)S(1)}, bf16[16,24,384]{2,1,0:T(8,128)(2,1)}, u32[]{:S(2)}) copy-start(bf16[16,24,384]{2,1,0:T(8,128)(2,1)} %copy-done.4) | copy-start | bytes 884740
  97.0 35.2 %copy-start.7 = (bf16[16,24,384]{2,1,0:T(8,128)(2,1)S(1)}, bf16[16,24,384]{2,1,0:T(8,128)(2,1)}, u32[]{:S(2)}) copy-start(bf16[16,24,384]{2,1,0:T(8,128)(2,1)} %copy-done.6) | copy-start | bytes 884740
  97.1 11.8 %collective-permute-start.15 = (bf16[16,24,384]{2,1,0:T(8,128)(2,1)S(1)}, bf16[16,24,384]{2,1,0:T(8,128)(2,1)S(1)}, u32[]{:S(2)}, u32[]{:S(2)}) collective-permute-start(bf16[16,24,384]{2,1,0:T(8,128)(2,1)S(1)} %copy-done.9), channel_id=1, source_target_pairs={{0,8},{8,16},{16,24},{24,32},{32,40},{40,48},{48,56},{56,0},{1,9},... | collective-permute-start | bytes 884744 | tf_op jit(solution)/shard_map/ppermute | solution.py:190
  101.8 21.1 %collective-permute-start.17 = (bf16[16,24,384]{2,1,0:T(8,128)(2,1)S(1)}, bf16[16,24,384]{2,1,0:T(8,128)(2,1)S(1)}, u32[]{:S(2)}, u32[]{:S(2)}) collective-permute-start(bf16[16,24,384]{2,1,0:T(8,128)(2,1)S(1)} %copy-done.11), channel_id=1, source_target_pairs={{0,56},{8,0},{16,8},{24,16},{32,24},{40,32},{48,40},{56,48},{1,57}... | collective-permute-start | bytes 884744 | tf_op jit(solution)/shard_map/ppermute | solution.py:192
  108.9 14.0 %copy-start.12 = (bf16[16,24,384]{2,1,0:T(8,128)(2,1)}, bf16[16,24,384]{2,1,0:T(8,128)(2,1)S(1)}, u32[]{:S(2)}) copy-start(bf16[16,24,384]{2,1,0:T(8,128)(2,1)S(1)} %collective-permute-done.15.refs_3_) | copy-start | bytes 884740
  108.9 14.0 %collective-permute-start.16 = (bf16[16,24,384]{2,1,0:T(8,128)(2,1)S(1)}, bf16[16,24,384]{2,1,0:T(8,128)(2,1)}, u32[]{:S(2)}, u32[]{:S(2)}) collective-permute-start(bf16[16,24,384]{2,1,0:T(8,128)(2,1)S(1)} %collective-permute-done.15.refs_3_), channel_id=1, source_target_pairs={{0,8},{8,16},{16,24},{24,32},{32,40},{40,48},{48,56},{56,0},{1,9},... | collective-permute-start | bytes 884744 | tf_op jit(solution)/shard_map/ppermute | solution.py:190
  122.9 9.4 %copy-start.14 = (bf16[16,24,384]{2,1,0:T(8,128)(2,1)}, bf16[16,24,384]{2,1,0:T(8,128)(2,1)S(1)}, u32[]{:S(2)}) copy-start(bf16[16,24,384]{2,1,0:T(8,128)(2,1)S(1)} %collective-permute-done.17.refs_5_) | copy-start | bytes 884740
  122.9 25.1 %all-to-all-start.2 = ((f32[16,56,128]{2,1,0:T(8,128)}), f32[16,56,128]{2,1,0:T(8,128)}, u32[]{:S(2)}, u32[]{:S(2)}) async-start(f32[16,56,128]{2,1,0:T(8,128)} %bitcast.32), calls=%async_computation.2 | async-start | bytes 917504 | tf_op jit(solution)/shard_map/all_to_all | solution.py:217
  132.3 1.0 copy-start.13
  133.3 1.0 copy-start.15

commit v7 on v6

--- a/solution.py
+++ b/solution.py
@@ -187,9 +187,13 @@
     below, above = [rows], [rows]
 
     def pass_on():
-        below.append(lax.ppermute(below[-1], Y, up))
-        if len(below) <= n_y // 2:
+        if len(below) < n_y // 2:
+            below.append(lax.ppermute(below[-1], Y, up))
             above.append(lax.ppermute(above[-1], Y, down))
+        else:
+            cut = below[-1].shape[0] // 2
+            below.append(lax.ppermute(below[-1][:cut], Y, up))
+            above.append(lax.ppermute(above[-1][cut:], Y, down))
 
     pass_on()
     for step in range(2, ring // 2):

time: 152 us -> 153 us (level)
  waiting for transfers between devices: 39.6 us -> 35.8 us
  starting transfers between devices: 81.4 us -> 84.6 us
    ppermute x0 -> x2, starting transfers between devices: none -> 6.48 us  [the longest x1 3.35 us: pass_on(): below.append(lax.ppermute(below[-1][:cut], Y, up))]
    all_to_all x1, waiting for transfers between devices: 8.38 us -> 4.53 us  [body(): terms = lax.all_to_all(terms, 'x', 0, 0)]
    ppermute x4 -> x3, starting transfers between devices: 13.9 us -> 10.6 us  [pass_on(): below.append(lax.ppermute(below[-1], Y, up))]
    unnamed x34 -> x32, local copies, waits for them, and re-layouts: 5.28 us -> 5.22 us
    ppermute x4 -> x3, waiting for transfers between devices: 5.17 us -> 5.16 us  [pass_on(): below.append(lax.ppermute(below[-1], Y, up))]
  transfers between devices with their start and end apart: 21 -> 22, of which waited for: 9 -> 9; matrix products, arithmetic and copies ran while one was open for 5% -> 5% of each run, Pallas kernels for 5% -> 5%
where the time goes in v7:
time: 153 us; the launch traced here: 150 us
  starting transfers between devices  84.6 us (55%)
  waiting for transfers between devices  35.8 us (23%)
  Pallas kernels  13.6 us (9%)
  local copies, waits for them, and re-layouts  7.93 us (5%)
  other arithmetic  4.58 us (3%)
  matrix products  2 us (1%)
    ppermute x7, starting transfers between devices, hop(): return lax.ppermute(block, ('zh', 'zl', 'c'), hops)  20 us
    all_to_all x1, waiting for transfers between devices, body(): lax.all_to_all(terms.reshape(far, -1, terms.shape[1]), ('zh',) + Y, 0, 0)  10.7 us
    ppermute x3, starting transfers between devices, pass_on(): below.append(lax.ppermute(below[-1], Y, up))  10.6 us
    all_to_all x1, starting transfers between devices, body(): lax.all_to_all(terms.reshape(far, -1, terms.shape[1]), ('zh',) + Y, 0, 0)  9.36 us
    ppermute x3, starting transfers between devices, pass_on(): above.append(lax.ppermute(above[-1], Y, down))  9.17 us
    ppermute x1, starting transfers between devices, body(): twin = lax.ppermute(own, 'c', swap)  8.92 us
    pallas_call x2, Pallas kernels, gram(): pl.pallas_call(lambda table_ref, *refs: gram_kernel(table_ref, slots, *re...  8.7 us
    ppermute x1, starting transfers between devices, body(): far_twin = lax.ppermute(same[-1], 'c', swap)  7.21 us
  transfers between devices with their start and end apart: 22, of which 9 were waited for; matrix products, arithmetic and copies ran while one was open for 5% of the time, Pallas kernels for 5%

profile of v7, /device:TPU:1, one launch (start us, length us, event | category | flops | bytes accessed | tf_op | source)
XLA Modules:
  0.0 149.8 jit_solution(15309450004944191110)
XLA Ops:
  0.6 0.0 copy-start
  0.7 8.9 %collective-permute-start.1 = (bf16[288,1024]{1,0:T(8,128)(2,1)}, bf16[288,1024]{1,0:T(8,128)(2,1)S(1)}, u32[]{:S(2)}, u32[]{:S(2)}) collective-permute-start(bf16[288,1024]{1,0:T(8,128)(2,1)} %bitcast.27), channel_id=1, source_target_pairs={{0,1},{1,0},{2,3},{3,2},{4,5},{5,4},{6,7},{7,6},{8,9},{9,8},{10,11... | collective-permute-start | bytes 1769480 | tf_op jit(solution)/shard_map/ppermute | solution.py:169
  9.6 5.3 %collective-permute-start = (bf16[288,1024]{1,0:T(8,128)(2,1)}, bf16[288,1024]{1,0:T(8,128)(2,1)S(1)}, u32[]{:S(2)}, u32[]{:S(2)}) collective-permute-start(bf16[288,1024]{1,0:T(8,128)(2,1)} %bitcast.28), channel_id=1, source_target_pairs={{0,2},{2,4},{4,6},{6,256},{256,258},{258,260},{260,262},{262,0},{1... | collective-permute-start | bytes 1769480 | tf_op jit(solution)/shard_map/ppermute | solution.py:150
  14.9 0.0 collective-permute-done.1.refs_0_
  14.9 0.0 copy-start.2
  14.9 0.8 copy-done.2
  15.7 2.0 %convolution_convert_fusion = bf16[48,384]{1,0:T(8,128)(2,1)} fusion(bf16[48,2304]{1,0:T(8,128)(2,1)} %bitcast.34, bf16[2304,384]{1,0:T(8,128)(2,1)S(1)} %copy-done), kind=kOutput, calls=%fused_computation.1 | convolution fusion | flops 84953088 | bytes 2027520 | tf_op jit(solution)/shard_map/dot_general | solution.py:173
  17.7 1.9 %collective-permute-start.2 = (bf16[48,384]{1,0:T(8,128)(2,1)}, bf16[48,384]{1,0:T(8,128)(2,1)}, u32[]{:S(2)}, u32[]{:S(2)}) collective-permute-start(bf16[48,384]{1,0:T(8,128)(2,1)} %convolution_convert_fusion), channel_id=1, source_target_pairs={{0,256},{256,0},{1,257},{257,1},{2,258},{258,2},{3,259},{259,3},{4... | collective-permute-start | bytes 110600 | tf_op jit(solution)/shard_map/ppermute | solution.py:176
  19.9 0.9 scatter_custom_fusion
  20.8 0.2 reshape.37
  21.0 0.1 reshape.38
  21.1 0.1 concatenate.3.table_ref
  21.2 2.2 %collective-permute-start.8 = (bf16[288,1024]{1,0:T(8,128)(2,1)}, bf16[288,1024]{1,0:T(8,128)(2,1)S(1)}, u32[]{:S(2)}, u32[]{:S(2)}) collective-permute-start(bf16[288,1024]{1,0:T(8,128)(2,1)} %copy-done.2), channel_id=1, source_target_pairs={{0,2},{2,4},{4,6},{6,256},{256,258},{258,260},{260,262},{262,0},{1... | collective-permute-start | bytes 1769480 | tf_op jit(solution)/shard_map/ppermute | solution.py:150
  23.4 0.0 collective-permute-done.refs_3_
  23.4 3.6 %collective-permute-done.2 = bf16[48,384]{1,0:T(8,128)(2,1)} collective-permute-done((bf16[48,384]{1,0:T(8,128)(2,1)}, bf16[48,384]{1,0:T(8,128)(2,1)}, u32[]{:S(2)}, u32[]{:S(2)}) %collective-permute-start.2) | collective-permute-done | bytes 36896 | tf_op jit(solution)/shard_map/ppermute | solution.py:176
  27.0 2.6 %collective-permute-start.3 = (bf16[288,1024]{1,0:T(8,128)(2,1)S(1)}, bf16[288,1024]{1,0:T(8,128)(2,1)}, u32[]{:S(2)}, u32[]{:S(2)}) collective-permute-start(bf16[288,1024]{1,0:T(8,128)(2,1)S(1)} %collective-permute-done.refs_3_), channel_id=1, source_target_pairs={{0,2},{2,4},{4,6},{6,256},{256,258},{258,260},{260,262},{262,0},{1... | collective-permute-start | bytes 1769480 | tf_op jit(solution)/shard_map/ppermute | solution.py:150
  29.7 0.9 maximum_select_fusion
  30.6 0.7 broadcast_in_dim.13
  31.3 4.1 %all-to-all-start = ((bf16[4,96,384]{2,1,0:T(8,128)(2,1)}), bf16[4,96,384]{2,1,0:T(8,128)(2,1)}, u32[]{:S(2)}, u32[]{:S(2)}) async-start(bf16[4,96,384]{2,1,0:T(8,128)(2,1)} %broadcast_in_dim.13), calls=%async_computation | async-start | bytes 589824 | tf_op jit(solution)/shard_map/all_to_all | solution.py:133
  35.4 0.0 collective-permute-done.8.refs_7_
  35.4 1.9 %collective-permute-start.9 = (bf16[288,1024]{1,0:T(8,128)(2,1)S(1)}, bf16[288,1024]{1,0:T(8,128)(2,1)}, u32[]{:S(2)}, u32[]{:S(2)}) collective-permute-start(bf16[288,1024]{1,0:T(8,128)(2,1)S(1)} %collective-permute-done.8.refs_7_), channel_id=1, source_target_pairs={{0,2},{2,4},{4,6},{6,256},{256,258},{258,260},{260,262},{262,0},{1... | collective-permute-start | bytes 1769480 | tf_op jit(solution)/shard_map/ppermute | solution.py:150
  37.3 4.9 %all-to-all-done = bf16[4,96,384]{2,1,0:T(8,128)(2,1)} async-done(((bf16[4,96,384]{2,1,0:T(8,128)(2,1)}), bf16[4,96,384]{2,1,0:T(8,128)(2,1)}, u32[]{:S(2)}, u32[]{:S(2)}) %all-to-all-start) | async-done | bytes 294944 | tf_op jit(solution)/shard_map/all_to_all | solution.py:133
  42.3 0.0 collective-permute-done.3.refs_4_
  42.3 1.9 %collective-permute-start.4 = (bf16[288,1024]{1,0:T(8,128)(2,1)}, bf16[288,1024]{1,0:T(8,128)(2,1)S(1)}, u32[]{:S(2)}, u32[]{:S(2)}) collective-permute-start(bf16[288,1024]{1,0:T(8,128)(2,1)} %collective-permute-done.3.refs_4_), channel_id=1, source_target_pairs={{0,2},{2,4},{4,6},{6,256},{256,258},{258,260},{260,262},{262,0},{1... | collective-permute-start | bytes 1769480 | tf_op jit(solution)/shard_map/ppermute | solution.py:150
  44.2 2.7 %collective-permute-start.5 = (bf16[16,24,384]{2,1,0:T(8,128)(2,1)}, bf16[16,24,384]{2,1,0:T(8,128)(2,1)S(1)}, u32[]{:S(2)}, u32[]{:S(2)}) collective-permute-start(bf16[16,24,384]{2,1,0:T(8,128)(2,1)} %bitcast.20.refs_0_), channel_id=1, source_target_pairs={{0,8},{8,16},{16,24},{24,32},{32,40},{40,48},{48,56},{56,0},{1,9},... | collective-permute-start | bytes 884744 | tf_op jit(solution)/shard_map/ppermute | solution.py:191
  46.9 3.8 %collective-permute-start.6 = (bf16[16,24,384]{2,1,0:T(8,128)(2,1)}, bf16[16,24,384]{2,1,0:T(8,128)(2,1)S(1)}, u32[]{:S(2)}, u32[]{:S(2)}) collective-permute-start(bf16[16,24,384]{2,1,0:T(8,128)(2,1)} %bitcast.20.refs_0_), channel_id=1, source_target_pairs={{0,56},{8,0},{16,8},{24,16},{32,24},{40,32},{48,40},{56,48},{1,57}... | collective-permute-start | bytes 884744 | tf_op jit(solution)/shard_map/ppermute | solution.py:192
  50.7 0.0 collective-permute-done.9.refs_8_
  50.7 3.0 %collective-permute-start.10 = (bf16[288,1024]{1,0:T(8,128)(2,1)}, bf16[288,1024]{1,0:T(8,128)(2,1)S(1)}, u32[]{:S(2)}, u32[]{:S(2)}) collective-permute-start(bf16[288,1024]{1,0:T(8,128)(2,1)} %collective-permute-done.9.refs_8_), channel_id=1, source_target_pairs={{0,2},{2,4},{4,6},{6,256},{256,258},{258,260},{260,262},{262,0},{1... | collective-permute-start | bytes 1769480 | tf_op jit(solution)/shard_map/ppermute | solution.py:150
  53.8 0.0 collective-permute-done.5.refs_1_
  53.8 1.1 collective-permute-done.6.refs_8_
  54.9 0.0 collective-permute-done.4.refs_5_
  54.9 3.0 %collective-permute-start.7 = (bf16[288,1024]{1,0:T(8,128)(2,1)S(1)}, bf16[288,1024]{1,0:T(8,128)(2,1)S(1)}, u32[]{:S(2)}, u32[]{:S(2)}) collective-permute-start(bf16[288,1024]{1,0:T(8,128)(2,1)S(1)} %collective-permute-done.4.refs_5_), channel_id=1, source_target_pairs={{0,2},{2,4},{4,6},{6,256},{256,258},{258,260},{260,262},{262,0},{1... | collective-permute-start | bytes 1769480 | tf_op jit(solution)/shard_map/ppermute | solution.py:150
  57.9 3.2 %collective-permute-start.11 = (bf16[16,24,384]{2,1,0:T(8,128)(2,1)S(1)}, bf16[16,24,384]{2,1,0:T(8,128)(2,1)S(1)}, u32[]{:S(2)}, u32[]{:S(2)}) collective-permute-start(bf16[16,24,384]{2,1,0:T(8,128)(2,1)S(1)} %collective-permute-done.5.refs_1_), channel_id=1, source_target_pairs={{0,8},{8,16},{16,24},{24,32},{32,40},{40,48},{48,56},{56,0},{1,9},... | collective-permute-start | bytes 884744 | tf_op jit(solution)/shard_map/ppermute | solution.py:191
  61.1 0.7 copy-done.4
  61.8 3.4 %collective-permute-start.12 = (bf16[16,24,384]{2,1,0:T(8,128)(2,1)S(1)}, bf16[16,24,384]{2,1,0:T(8,128)(2,1)S(1)}, u32[]{:S(2)}, u32[]{:S(2)}) collective-permute-start(bf16[16,24,384]{2,1,0:T(8,128)(2,1)S(1)} %collective-permute-done.6.refs_8_), channel_id=1, source_target_pairs={{0,56},{8,0},{16,8},{24,16},{32,24},{40,32},{48,40},{56,48},{1,57}... | collective-permute-start | bytes 884744 | tf_op jit(solution)/shard_map/ppermute | solution.py:192
  65.3 0.7 copy-done.6
  66.0 0.0 collective-permute-done.10.refs_9_
  66.0 2.2 %collective-permute-done.7.refs_1_.refs_6_ = bf16[288,1024]{1,0:T(8,128)(2,1)S(1)} collective-permute-done((bf16[288,1024]{1,0:T(8,128)(2,1)S(1)}, bf16[288,1024]{1,0:T(8,128)(2,1)S(1)}, u32[]{:S(2)}, u32[]{:S(2)}) %collective-permute-start.7) | collective-permute-done | bytes 589856 | tf_op jit(solution)/shard_map/ppermute | solution.py:150
  68.2 0.0 collective-permute-done.11.refs_2_
  68.2 2.0 %collective-permute-done.12.refs_7_ = bf16[16,24,384]{2,1,0:T(8,128)(2,1)S(1)} collective-permute-done((bf16[16,24,384]{2,1,0:T(8,128)(2,1)S(1)}, bf16[16,24,384]{2,1,0:T(8,128)(2,1)S(1)}, u32[]{:S(2)}, u32[]{:S(2)}) %collective-permute-start.12) | collective-permute-done | bytes 294944 | tf_op jit(solution)/shard_map/ppermute | solution.py:192
  70.2 7.2 %collective-permute-start.13 = (bf16[288,1024]{1,0:T(8,128)(2,1)S(1)}, bf16[288,1024]{1,0:T(8,128)(2,1)S(1)}, u32[]{:S(2)}, u32[]{:S(2)}) collective-permute-start(bf16[288,1024]{1,0:T(8,128)(2,1)S(1)} %collective-permute-done.7.refs_1_.refs_6_), channel_id=1, source_target_pairs={{0,1},{1,0},{2,3},{3,2},{4,5},{5,4},{6,7},{7,6},{8,9},{9,8},{10,11... | collective-permute-start | bytes 1769480 | tf_op jit(solution)/shard_map/ppermute | solution.py:208
  77.4 1.6 %collective-permute-done.13.refs_1_ = bf16[288,1024]{1,0:T(8,128)(2,1)S(1)} collective-permute-done((bf16[288,1024]{1,0:T(8,128)(2,1)S(1)}, bf16[288,1024]{1,0:T(8,128)(2,1)S(1)}, u32[]{:S(2)}, u32[]{:S(2)}) %collective-permute-start.13) | collective-permute-done | bytes 589856 | tf_op jit(solution)/shard_map/ppermute | solution.py:208
  79.0 1.1 copy-done.3
  80.1 4.3 %shard_map.60 = f32[4,896,128]{2,1,0:T(8,128)S(1)} custom-call(s32[145]{0:T(256)S(1)} %concatenate.3.table_ref, bf16[288,1024]{1,0:T(8,128)(2,1)S(1)} %copy-done.3, bf16[288,1024]{1,0:T(8,128)(2,1)S(1)} %collective-permute-done.13.refs_1_, bf16[288,1024]{1,0:T(8,128)(2,1)S(1)} %bitcast.29, bf16[288,1024]{1,0:T(8,128)(2,1)S(1)} %collective-permute-done.refs_3_, ...), custom_call_target="tpu_custom_call" | custom-call | tf_op jit(solution)/shard_map/pallas_call | solution.py:58
  84.4 2.3 %collective-permute-start.14 = (f32[4,896,128]{2,1,0:T(8,128)S(1)}, f32[4,896,128]{2,1,0:T(8,128)S(1)}, u32[]{:S(2)}, u32[]{:S(2)}) collective-permute-start(f32[4,896,128]{2,1,0:T(8,128)S(1)} %shard_map.60), channel_id=1, source_target_pairs={{0,1},{1,0},{2,3},{3,2},{4,5},{5,4},{6,7},{7,6},{8,9},{9,8},{10,11... | collective-permute-start | bytes 5505032 | tf_op jit(solution)/shard_map/ppermute | solution.py:216
  86.7 4.4 %shard_map.59 = f32[4,896,128]{2,1,0:T(8,128)S(1)} custom-call(s32[145]{0:T(256)S(1)} %concatenate.3.table_ref, bf16[288,1024]{1,0:T(8,128)(2,1)S(1)} %bitcast.30, bf16[288,1024]{1,0:T(8,128)(2,1)S(1)} %collective-permute-done.7.refs_1_.refs_6_, bf16[288,1024]{1,0:T(8,128)(2,1)S(1)} %bitcast.31, bf16[288,1024]{1,0:T(8,128)(2,1)S(1)} %collective-permute-done.refs_3_, ...), custom_call_target="tpu_custom_call" | custom-call | tf_op jit(solution)/shard_map/pallas_call | solution.py:58
  91.1 1.4 add.165
  92.5 4.5 %all-to-all-start.1 = ((f32[4,896,128]{2,1,0:T(8,128)}), f32[4,896,128]{2,1,0:T(8,128)}, u32[]{:S(2)}, u32[]{:S(2)}) async-start(f32[4,896,128]{2,1,0:T(8,128)} %add.165), calls=%async_computation.1 | async-start | bytes 3670016 | tf_op jit(solution)/shard_map/all_to_all | solution.py:218
  97.1 4.7 %collective-permute-start.15 = (bf16[16,24,384]{2,1,0:T(8,128)(2,1)S(1)}, bf16[16,24,384]{2,1,0:T(8,128)(2,1)S(1)}, u32[]{:S(2)}, u32[]{:S(2)}) collective-permute-start(bf16[16,24,384]{2,1,0:T(8,128)(2,1)S(1)} %copy-done.9), channel_id=1, source_target_pairs={{0,8},{8,16},{16,24},{24,32},{32,40},{40,48},{48,56},{56,0},{1,9},... | collective-permute-start | bytes 884744 | tf_op jit(solution)/shard_map/ppermute | solution.py:191
  101.8 1.9 %collective-permute-start.17 = (bf16[16,24,384]{2,1,0:T(8,128)(2,1)S(1)}, bf16[16,24,384]{2,1,0:T(8,128)(2,1)S(1)}, u32[]{:S(2)}, u32[]{:S(2)}) collective-permute-start(bf16[16,24,384]{2,1,0:T(8,128)(2,1)S(1)} %copy-done.11), channel_id=1, source_target_pairs={{0,56},{8,0},{16,8},{24,16},{32,24},{40,32},{48,40},{56,48},{1,57}... | collective-permute-start | bytes 884744 | tf_op jit(solution)/shard_map/ppermute | solution.py:192
  103.7 5.2 %collective-permute-done.15.refs_3_ = bf16[16,24,384]{2,1,0:T(8,128)(2,1)S(1)} collective-permute-done((bf16[16,24,384]{2,1,0:T(8,128)(2,1)S(1)}, bf16[16,24,384]{2,1,0:T(8,128)(2,1)S(1)}, u32[]{:S(2)}, u32[]{:S(2)}) %collective-permute-start.15) | collective-permute-done | bytes 294944 | tf_op jit(solution)/shard_map/ppermute | solution.py:191
  108.9 0.7 slice.28
  109.5 3.4 %collective-permute-start.16 = (bf16[8,24,384]{2,1,0:T(8,128)(2,1)}, bf16[8,24,384]{2,1,0:T(8,128)(2,1)}, u32[]{:S(2)}, u32[]{:S(2)}) collective-permute-start(bf16[8,24,384]{2,1,0:T(8,128)(2,1)} %slice.28), channel_id=1, source_target_pairs={{0,8},{8,16},{16,24},{24,32},{32,40},{40,48},{48,56},{56,0},{1,9},... | collective-permute-start | bytes 442376 | tf_op jit(solution)/shard_map/ppermute | solution.py:195
  112.9 0.0 collective-permute-done.17.refs_6_
  112.9 3.1 %collective-permute-start.18 = (bf16[8,24,384]{2,1,0:T(8,128)(2,1)S(1)}, bf16[8,24,384]{2,1,0:T(8,128)(2,1)S(1)}, u32[]{:S(2)}, u32[]{:S(2)}) collective-permute-start(bf16[8,24,384]{2,1,0:T(8,128)(2,1)S(1)} %slice.29), channel_id=1, source_target_pairs={{0,56},{8,0},{16,8},{24,16},{32,24},{40,32},{48,40},{56,48},{1,57}... | collective-permute-start | bytes 442376 | tf_op jit(solution)/shard_map/ppermute | solution.py:196
  116.1 4.5 %all-to-all-done.1 = f32[4,896,128]{2,1,0:T(8,128)} async-done(((f32[4,896,128]{2,1,0:T(8,128)}), f32[4,896,128]{2,1,0:T(8,128)}, u32[]{:S(2)}, u32[]{:S(2)}) %all-to-all-start.1) | async-done | bytes 1835040 | tf_op jit(solution)/shard_map/all_to_all | solution.py:218
  120.6 2.3 %fusion = f32[896,128]{1,0:T(8,128)} fusion(f32[4,896,128]{2,1,0:T(8,128)} %all-to-all-done.1), kind=kLoop, calls=%fused_computation.3 | loop fusion | flops 344064 | bytes 2293760 | tf_op jit(solution)/shard_map/add | solution.py:219
  122.9 0.0 collective-permute-done.16.refs_4_
  122.9 9.4 %all-to-all-start.2 = ((f32[16,56,128]{2,1,0:T(8,128)}), f32[16,56,128]{2,1,0:T(8,128)}, u32[]{:S(2)}, u32[]{:S(2)}) async-start(f32[16,56,128]{2,1,0:T(8,128)} %bitcast.32), calls=%async_computation.2 | async-start | bytes 917504 | tf_op jit(solution)/shard_map/all_to_all | solution.py:221
  132.3 1.0 copy-done.12
  133.3 0.9 copy-done.14
  134.2 3.1 %shard_map.62 = bf16[2304,384]{1,0:T(8,128)(2,1)} custom-call(s32[96]{0:T(128)S(1)} %get-tuple-element.38.place_of, bf16[16,24,384]{2,1,0:T(8,128)(2,1)} %bitcast.20.refs_0_, bf16[16,24,384]{2,1,0:T(8,128)(2,1)S(1)} %copy-done.5, bf16[16,24,384]{2,1,0:T(8,128)(2,1)S(1)} %copy-done.9, bf16[16,24,384]{2,1,0:T(8,128)(2,1)S(1)} %collective-permute-done.15.refs_3_, ...), custom_call_target="tpu_custom_call" | custom-call | tf_op jit(solution)/shard_map/pallas_call | solution.py:117
  137.3 10.7 %all-to-all-done.2 = f32[16,56,128]{2,1,0:T(8,128)} async-done(((f32[16,56,128]{2,1,0:T(8,128)}), f32[16,56,128]{2,1,0:T(8,128)}, u32[]{:S(2)}, u32[]{:S(2)}) %all-to-all-start.2) | async-done | bytes 458784 | tf_op jit(solution)/shard_map/all_to_all | solution.py:221
  148.0 1.8 %shard_map.61 = f32[2,24,288]{2,1,0:T(8,128)} custom-call(f32[2,8,56,128]{3,2,1,0:T(8,128)} %bitcast.23.parts_ref), custom_call_target="tpu_custom_call" | custom-call | tf_op jit(solution)/shard_map/pallas_call | solution.py:93
  (30 shorter events, 0.1 us)
Async XLA Ops:
  0.6 15.1 %copy-start = (bf16[2304,384]{1,0:T(8,128)(2,1)S(1)}, bf16[2304,384]{1,0:T(8,128)(2,1)}, u32[]{:S(2)}) copy-start(bf16[2304,384]{1,0:T(8,128)(2,1)} %param.7) | copy-start | bytes 5308420
  0.6 19.0 %copy-start.15 = (s32[96]{0:T(128)S(1)}, s32[96]{0:T(128)}, u32[]{:S(2)}) copy-start(s32[96]{0:T(128)} %param.5) | copy-start | bytes 1156
  0.7 14.2 %collective-permute-start.1 = (bf16[288,1024]{1,0:T(8,128)(2,1)}, bf16[288,1024]{1,0:T(8,128)(2,1)S(1)}, u32[]{:S(2)}, u32[]{:S(2)}) collective-permute-start(bf16[288,1024]{1,0:T(8,128)(2,1)} %bitcast.27), channel_id=1, source_target_pairs={{0,1},{1,0},{2,3},{3,2},{4,5},{5,4},{6,7},{7,6},{8,9},{9,8},{10,11... | collective-permute-start | bytes 1769480 | tf_op jit(solution)/shard_map/ppermute | solution.py:169
  9.6 13.8 %collective-permute-start = (bf16[288,1024]{1,0:T(8,128)(2,1)}, bf16[288,1024]{1,0:T(8,128)(2,1)S(1)}, u32[]{:S(2)}, u32[]{:S(2)}) collective-permute-start(bf16[288,1024]{1,0:T(8,128)(2,1)} %bitcast.28), channel_id=1, source_target_pairs={{0,2},{2,4},{4,6},{6,256},{256,258},{258,260},{260,262},{262,0},{1... | collective-permute-start | bytes 1769480 | tf_op jit(solution)/shard_map/ppermute | solution.py:150
  14.9 0.8 copy-start.2
  15.7 63.3 %copy-start.1 = (bf16[1024,288]{0,1:T(8,128)(2,1)S(1)}, bf16[1024,288]{0,1:T(8,128)(2,1)}, u32[]{:S(2)}) copy-start(bf16[1024,288]{0,1:T(8,128)(2,1)} %param.4) | copy-start | bytes 1769476
  17.7 9.3 %collective-permute-start.2 = (bf16[48,384]{1,0:T(8,128)(2,1)}, bf16[48,384]{1,0:T(8,128)(2,1)}, u32[]{:S(2)}, u32[]{:S(2)}) collective-permute-start(bf16[48,384]{1,0:T(8,128)(2,1)} %convolution_convert_fusion), channel_id=1, source_target_pairs={{0,256},{256,0},{1,257},{257,1},{2,258},{258,2},{3,259},{259,3},{4... | collective-permute-start | bytes 110600 | tf_op jit(solution)/shard_map/ppermute | solution.py:176
  21.2 14.1 %collective-permute-start.8 = (bf16[288,1024]{1,0:T(8,128)(2,1)}, bf16[288,1024]{1,0:T(8,128)(2,1)S(1)}, u32[]{:S(2)}, u32[]{:S(2)}) collective-permute-start(bf16[288,1024]{1,0:T(8,128)(2,1)} %copy-done.2), channel_id=1, source_target_pairs={{0,2},{2,4},{4,6},{6,256},{256,258},{258,260},{260,262},{262,0},{1... | collective-permute-start | bytes 1769480 | tf_op jit(solution)/shard_map/ppermute | solution.py:150
  27.0 15.2 %collective-permute-start.3 = (bf16[288,1024]{1,0:T(8,128)(2,1)S(1)}, bf16[288,1024]{1,0:T(8,128)(2,1)}, u32[]{:S(2)}, u32[]{:S(2)}) collective-permute-start(bf16[288,1024]{1,0:T(8,128)(2,1)S(1)} %collective-permute-done.refs_3_), channel_id=1, source_target_pairs={{0,2},{2,4},{4,6},{6,256},{256,258},{258,260},{260,262},{262,0},{1... | collective-permute-start | bytes 1769480 | tf_op jit(solution)/shard_map/ppermute | solution.py:150
  31.3 11.0 %all-to-all-start = ((bf16[4,96,384]{2,1,0:T(8,128)(2,1)}), bf16[4,96,384]{2,1,0:T(8,128)(2,1)}, u32[]{:S(2)}, u32[]{:S(2)}) async-start(bf16[4,96,384]{2,1,0:T(8,128)(2,1)} %broadcast_in_dim.13), calls=%async_computation | async-start | bytes 589824 | tf_op jit(solution)/shard_map/all_to_all | solution.py:133
  35.4 15.3 %collective-permute-start.9 = (bf16[288,1024]{1,0:T(8,128)(2,1)S(1)}, bf16[288,1024]{1,0:T(8,128)(2,1)}, u32[]{:S(2)}, u32[]{:S(2)}) collective-permute-start(bf16[288,1024]{1,0:T(8,128)(2,1)S(1)} %collective-permute-done.8.refs_7_), channel_id=1, source_target_pairs={{0,2},{2,4},{4,6},{6,256},{256,258},{258,260},{260,262},{262,0},{1... | collective-permute-start | bytes 1769480 | tf_op jit(solution)/shard_map/ppermute | solution.py:150
  42.3 12.6 %collective-permute-start.4 = (bf16[288,1024]{1,0:T(8,128)(2,1)}, bf16[288,1024]{1,0:T(8,128)(2,1)S(1)}, u32[]{:S(2)}, u32[]{:S(2)}) collective-permute-start(bf16[288,1024]{1,0:T(8,128)(2,1)} %collective-permute-done.3.refs_4_), channel_id=1, source_target_pairs={{0,2},{2,4},{4,6},{6,256},{256,258},{258,260},{260,262},{262,0},{1... | collective-permute-start | bytes 1769480 | tf_op jit(solution)/shard_map/ppermute | solution.py:150
  44.2 9.6 %collective-permute-start.5 = (bf16[16,24,384]{2,1,0:T(8,128)(2,1)}, bf16[16,24,384]{2,1,0:T(8,128)(2,1)S(1)}, u32[]{:S(2)}, u32[]{:S(2)}) collective-permute-start(bf16[16,24,384]{2,1,0:T(8,128)(2,1)} %bitcast.20.refs_0_), channel_id=1, source_target_pairs={{0,8},{8,16},{16,24},{24,32},{32,40},{40,48},{48,56},{56,0},{1,9},... | collective-permute-start | bytes 884744 | tf_op jit(solution)/shard_map/ppermute | solution.py:191
  46.9 8.0 %collective-permute-start.6 = (bf16[16,24,384]{2,1,0:T(8,128)(2,1)}, bf16[16,24,384]{2,1,0:T(8,128)(2,1)S(1)}, u32[]{:S(2)}, u32[]{:S(2)}) collective-permute-start(bf16[16,24,384]{2,1,0:T(8,128)(2,1)} %bitcast.20.refs_0_), channel_id=1, source_target_pairs={{0,56},{8,0},{16,8},{24,16},{32,24},{40,32},{48,40},{56,48},{1,57}... | collective-permute-start | bytes 884744 | tf_op jit(solution)/shard_map/ppermute | solution.py:192
  50.7 15.3 %collective-permute-start.10 = (bf16[288,1024]{1,0:T(8,128)(2,1)}, bf16[288,1024]{1,0:T(8,128)(2,1)S(1)}, u32[]{:S(2)}, u32[]{:S(2)}) collective-permute-start(bf16[288,1024]{1,0:T(8,128)(2,1)} %collective-permute-done.9.refs_8_), channel_id=1, source_target_pairs={{0,2},{2,4},{4,6},{6,256},{256,258},{258,260},{260,262},{262,0},{1... | collective-permute-start | bytes 1769480 | tf_op jit(solution)/shard_map/ppermute | solution.py:150
  54.9 13.3 %collective-permute-start.7 = (bf16[288,1024]{1,0:T(8,128)(2,1)S(1)}, bf16[288,1024]{1,0:T(8,128)(2,1)S(1)}, u32[]{:S(2)}, u32[]{:S(2)}) collective-permute-start(bf16[288,1024]{1,0:T(8,128)(2,1)S(1)} %collective-permute-done.4.refs_5_), channel_id=1, source_target_pairs={{0,2},{2,4},{4,6},{6,256},{256,258},{258,260},{260,262},{262,0},{1... | collective-permute-start | bytes 1769480 | tf_op jit(solution)/shard_map/ppermute | solution.py:150
  57.9 10.3 %collective-permute-start.11 = (bf16[16,24,384]{2,1,0:T(8,128)(2,1)S(1)}, bf16[16,24,384]{2,1,0:T(8,128)(2,1)S(1)}, u32[]{:S(2)}, u32[]{:S(2)}) collective-permute-start(bf16[16,24,384]{2,1,0:T(8,128)(2,1)S(1)} %collective-permute-done.5.refs_1_), channel_id=1, source_target_pairs={{0,8},{8,16},{16,24},{24,32},{32,40},{40,48},{48,56},{56,0},{1,9},... | collective-permute-start | bytes 884744 | tf_op jit(solution)/shard_map/ppermute | solution.py:191
  61.1 0.7 copy-start.4
  61.8 8.4 %collective-permute-start.12 = (bf16[16,24,384]{2,1,0:T(8,128)(2,1)S(1)}, bf16[16,24,384]{2,1,0:T(8,128)(2,1)S(1)}, u32[]{:S(2)}, u32[]{:S(2)}) collective-permute-start(bf16[16,24,384]{2,1,0:T(8,128)(2,1)S(1)} %collective-permute-done.6.refs_8_), channel_id=1, source_target_pairs={{0,56},{8,0},{16,8},{24,16},{32,24},{40,32},{48,40},{56,48},{1,57}... | collective-permute-start | bytes 884744 | tf_op jit(solution)/shard_map/ppermute | solution.py:192
  65.3 0.7 copy-start.6
  68.2 9.2 %copy-start.8 = (bf16[16,24,384]{2,1,0:T(8,128)(2,1)}, bf16[16,24,384]{2,1,0:T(8,128)(2,1)S(1)}, u32[]{:S(2)}) copy-start(bf16[16,24,384]{2,1,0:T(8,128)(2,1)S(1)} %collective-permute-done.11.refs_2_) | copy-start | bytes 884740
  70.2 7.2 %copy-start.10 = (bf16[16,24,384]{2,1,0:T(8,128)(2,1)}, bf16[16,24,384]{2,1,0:T(8,128)(2,1)S(1)}, u32[]{:S(2)}) copy-start(bf16[16,24,384]{2,1,0:T(8,128)(2,1)S(1)} %collective-permute-done.12.refs_7_) | copy-start | bytes 884740
  70.2 8.8 %collective-permute-start.13 = (bf16[288,1024]{1,0:T(8,128)(2,1)S(1)}, bf16[288,1024]{1,0:T(8,128)(2,1)S(1)}, u32[]{:S(2)}, u32[]{:S(2)}) collective-permute-start(bf16[288,1024]{1,0:T(8,128)(2,1)S(1)} %collective-permute-done.7.refs_1_.refs_6_), channel_id=1, source_target_pairs={{0,1},{1,0},{2,3},{3,2},{4,5},{5,4},{6,7},{7,6},{8,9},{9,8},{10,11... | collective-permute-start | bytes 1769480 | tf_op jit(solution)/shard_map/ppermute | solution.py:208
  79.0 1.1 copy-start.3
  84.4 6.7 %collective-permute-start.14 = (f32[4,896,128]{2,1,0:T(8,128)S(1)}, f32[4,896,128]{2,1,0:T(8,128)S(1)}, u32[]{:S(2)}, u32[]{:S(2)}) collective-permute-start(f32[4,896,128]{2,1,0:T(8,128)S(1)} %shard_map.60), channel_id=1, source_target_pairs={{0,1},{1,0},{2,3},{3,2},{4,5},{5,4},{6,7},{7,6},{8,9},{9,8},{10,11... | collective-permute-start | bytes 5505032 | tf_op jit(solution)/shard_map/ppermute | solution.py:216
  92.5 4.5 %copy-start.9 = (bf16[16,24,384]{2,1,0:T(8,128)(2,1)S(1)}, bf16[16,24,384]{2,1,0:T(8,128)(2,1)}, u32[]{:S(2)}) copy-start(bf16[16,24,384]{2,1,0:T(8,128)(2,1)} %copy-done.8) | copy-start | bytes 884740
  92.5 9.3 %copy-start.11 = (bf16[16,24,384]{2,1,0:T(8,128)(2,1)S(1)}, bf16[16,24,384]{2,1,0:T(8,128)(2,1)}, u32[]{:S(2)}) copy-start(bf16[16,24,384]{2,1,0:T(8,128)(2,1)} %copy-done.10) | copy-start | bytes 884740
  92.5 28.1 %all-to-all-start.1 = ((f32[4,896,128]{2,1,0:T(8,128)}), f32[4,896,128]{2,1,0:T(8,128)}, u32[]{:S(2)}, u32[]{:S(2)}) async-start(f32[4,896,128]{2,1,0:T(8,128)} %add.165), calls=%async_computation.1 | async-start | bytes 3670016 | tf_op jit(solution)/shard_map/all_to_all | solution.py:218
  97.0 35.2 %copy-start.5 = (bf16[16,24,384]{2,1,0:T(8,128)(2,1)S(1)}, bf16[16,24,384]{2,1,0:T(8,128)(2,1)}, u32[]{:S(2)}) copy-start(bf16[16,24,384]{2,1,0:T(8,128)(2,1)} %copy-done.4) | copy-start | bytes 884740
  97.0 35.2 %copy-start.7 = (bf16[16,24,384]{2,1,0:T(8,128)(2,1)S(1)}, bf16[16,24,384]{2,1,0:T(8,128)(2,1)}, u32[]{:S(2)}) copy-start(bf16[16,24,384]{2,1,0:T(8,128)(2,1)} %copy-done.6) | copy-start | bytes 884740
  97.1 11.8 %collective-permute-start.15 = (bf16[16,24,384]{2,1,0:T(8,128)(2,1)S(1)}, bf16[16,24,384]{2,1,0:T(8,128)(2,1)S(1)}, u32[]{:S(2)}, u32[]{:S(2)}) collective-permute-start(bf16[16,24,384]{2,1,0:T(8,128)(2,1)S(1)} %copy-done.9), channel_id=1, source_target_pairs={{0,8},{8,16},{16,24},{24,32},{32,40},{40,48},{48,56},{56,0},{1,9},... | collective-permute-start | bytes 884744 | tf_op jit(solution)/shard_map/ppermute | solution.py:191
  101.8 11.1 %collective-permute-start.17 = (bf16[16,24,384]{2,1,0:T(8,128)(2,1)S(1)}, bf16[16,24,384]{2,1,0:T(8,128)(2,1)S(1)}, u32[]{:S(2)}, u32[]{:S(2)}) collective-permute-start(bf16[16,24,384]{2,1,0:T(8,128)(2,1)S(1)} %copy-done.11), channel_id=1, source_target_pairs={{0,56},{8,0},{16,8},{24,16},{32,24},{40,32},{48,40},{56,48},{1,57}... | collective-permute-start | bytes 884744 | tf_op jit(solution)/shard_map/ppermute | solution.py:192
  109.5 13.3 %collective-permute-start.16 = (bf16[8,24,384]{2,1,0:T(8,128)(2,1)}, bf16[8,24,384]{2,1,0:T(8,128)(2,1)}, u32[]{:S(2)}, u32[]{:S(2)}) collective-permute-start(bf16[8,24,384]{2,1,0:T(8,128)(2,1)} %slice.28), channel_id=1, source_target_pairs={{0,8},{8,16},{16,24},{24,32},{32,40},{40,48},{48,56},{56,0},{1,9},... | collective-permute-start | bytes 442376 | tf_op jit(solution)/shard_map/ppermute | solution.py:195
  112.9 10.0 %collective-permute-start.18 = (bf16[8,24,384]{2,1,0:T(8,128)(2,1)S(1)}, bf16[8,24,384]{2,1,0:T(8,128)(2,1)S(1)}, u32[]{:S(2)}, u32[]{:S(2)}) collective-permute-start(bf16[8,24,384]{2,1,0:T(8,128)(2,1)S(1)} %slice.29), channel_id=1, source_target_pairs={{0,56},{8,0},{16,8},{24,16},{32,24},{40,32},{48,40},{56,48},{1,57}... | collective-permute-start | bytes 442376 | tf_op jit(solution)/shard_map/ppermute | solution.py:196
  122.9 9.4 %copy-start.13 = (bf16[8,24,384]{2,1,0:T(8,128)(2,1)}, bf16[8,24,384]{2,1,0:T(8,128)(2,1)S(1)}, u32[]{:S(2)}) copy-start(bf16[8,24,384]{2,1,0:T(8,128)(2,1)S(1)} %collective-permute-done.18.refs_5_) | copy-start | bytes 442372
  122.9 25.1 %all-to-all-start.2 = ((f32[16,56,128]{2,1,0:T(8,128)}), f32[16,56,128]{2,1,0:T(8,128)}, u32[]{:S(2)}, u32[]{:S(2)}) async-start(f32[16,56,128]{2,1,0:T(8,128)} %bitcast.32), calls=%async_computation.2 | async-start | bytes 917504 | tf_op jit(solution)/shard_map/all_to_all | solution.py:221
  132.3 1.0 copy-start.12
  133.3 0.9 copy-start.14

commit v8 on v6

--- a/solution.py
+++ b/solution.py
@@ -71,13 +71,13 @@
 
 def sum_join_kernel(scale, parts_ref, out_ref):
     held, tile, cols = out_ref.shape
-    halves, rows = parts_ref.shape[0], held * tile
+    halves, rows = parts_ref.shape[1], held * tile
     extra = cols // halves - 128
     pieces = []
     for half in range(halves):
-        total = parts_ref[half, 0]
-        for n in range(1, parts_ref.shape[1]):
-            total = total + parts_ref[half, n]
+        total = parts_ref[0, half]
+        for n in range(1, parts_ref.shape[0]):
+            total = total + parts_ref[n, half]
         total = total * scale
         pieces.append(total[:rows])
         rest = total[rows:]
@@ -152,7 +152,7 @@
     owner_slots = owners * held
     index = jnp.arange(tiles, dtype=jnp.int32)
     table = jnp.full((owner_slots,), -1, jnp.int32).at[assignment].set(index)
-    table = table.reshape(n_zh, n_x, n_yh, n_yl, held).transpose(1, 0, 2, 3, 4).reshape(-1)
+    table = table.reshape(n_zh, n_x, n_yh, n_yl, held).transpose(1, 2, 3, 0, 4).reshape(-1)
     core, upper = lax.axis_index("c"), lax.axis_index("zh")
     here = upper * (ring // n_zh) + lax.axis_index("zl")
     share = cols // n_zh
@@ -214,8 +214,8 @@
     terms = lax.all_to_all(terms, "x", 0, 0)
     terms = functools.reduce(jnp.add, [terms[n] for n in range(near)])
     terms, below[-1], above[-1] = lax.optimization_barrier((terms, below[-1], above[-1]))
-    terms = lax.all_to_all(terms.reshape(far, -1, terms.shape[1]), ("zh",) + Y, 0, 0)
-    terms = terms.reshape((n_zh, n_y) + terms.shape[1:])
+    terms = lax.all_to_all(terms.reshape(far, -1, terms.shape[1]), Y + ("zh",), 0, 0)
+    terms = terms.reshape((n_y, n_zh) + terms.shape[1:])
     factor_tiles = sum_join(terms, held, tile, cols, 1.0 / (tokens * owners))
 
     owner, slot = assignment // held, assignment % held

time: 152 us -> 154 us (1.013)
  waiting for transfers between devices: 39.6 us -> 42.4 us
    all_to_all x1, waiting for transfers between devices: 10.6 us -> 13.6 us  [body(): lax.all_to_all(terms.reshape(far, -1, terms.shape[1]), Y + ('zh',), 0, 0)]
where the time goes in v8:
time: 154 us; the launch traced here: 153 us
  starting transfers between devices  81.6 us (53%)
  waiting for transfers between devices  42.4 us (28%)
  Pallas kernels  13.7 us (9%)
  local copies, waits for them, and re-layouts  7.32 us (5%)
  other arithmetic  4.58 us (3%)
  matrix products  2 us (1%)
    ppermute x7, starting transfers between devices, hop(): return lax.ppermute(block, ('zh', 'zl', 'c'), hops)  20.2 us
    ppermute x4, starting transfers between devices, pass_on(): below.append(lax.ppermute(below[-1], Y, up))  14 us
    all_to_all x1, waiting for transfers between devices, body(): lax.all_to_all(terms.reshape(far, -1, terms.shape[1]), Y + ('zh',), 0, 0)  13.6 us
    all_to_all x1, starting transfers between devices, body(): lax.all_to_all(terms.reshape(far, -1, terms.shape[1]), Y + ('zh',), 0, 0)  9.42 us
    ppermute x3, starting transfers between devices, pass_on(): above.append(lax.ppermute(above[-1], Y, down))  9.17 us
    ppermute x1, starting transfers between devices, body(): twin = lax.ppermute(own, 'c', swap)  8.92 us
    pallas_call x2, Pallas kernels, gram(): pl.pallas_call(lambda table_ref, *refs: gram_kernel(table_ref, slots, *re...  8.69 us
    all_to_all x1, waiting for transfers between devices, body(): terms = lax.all_to_all(terms, 'x', 0, 0)  8.38 us
  transfers between devices with their start and end apart: 21, of which 9 were waited for; matrix products, arithmetic and copies ran while one was open for 5% of the time, Pallas kernels for 5%

profile of v8, /device:TPU:1, one launch (start us, length us, event | category | flops | bytes accessed | tf_op | source)
XLA Modules:
  0.0 152.8 jit_solution(17308569471438174501)
XLA Ops:
  0.6 0.0 copy-start
  0.7 8.9 %collective-permute-start.1 = (bf16[288,1024]{1,0:T(8,128)(2,1)}, bf16[288,1024]{1,0:T(8,128)(2,1)S(1)}, u32[]{:S(2)}, u32[]{:S(2)}) collective-permute-start(bf16[288,1024]{1,0:T(8,128)(2,1)} %bitcast.27), channel_id=1, source_target_pairs={{0,1},{1,0},{2,3},{3,2},{4,5},{5,4},{6,7},{7,6},{8,9},{9,8},{10,11... | collective-permute-start | bytes 1769480 | tf_op jit(solution)/shard_map/ppermute | solution.py:169
  9.6 5.3 %collective-permute-start = (bf16[288,1024]{1,0:T(8,128)(2,1)}, bf16[288,1024]{1,0:T(8,128)(2,1)S(1)}, u32[]{:S(2)}, u32[]{:S(2)}) collective-permute-start(bf16[288,1024]{1,0:T(8,128)(2,1)} %bitcast.28), channel_id=1, source_target_pairs={{0,2},{2,4},{4,6},{6,256},{256,258},{258,260},{260,262},{262,0},{1... | collective-permute-start | bytes 1769480 | tf_op jit(solution)/shard_map/ppermute | solution.py:150
  14.9 0.0 collective-permute-done.1.refs_0_
  14.9 0.0 copy-start.2
  14.9 0.8 copy-done.2
  15.7 2.0 %convolution_convert_fusion = bf16[48,384]{1,0:T(8,128)(2,1)} fusion(bf16[48,2304]{1,0:T(8,128)(2,1)} %bitcast.34, bf16[2304,384]{1,0:T(8,128)(2,1)S(1)} %copy-done), kind=kOutput, calls=%fused_computation.1 | convolution fusion | flops 84953088 | bytes 2027520 | tf_op jit(solution)/shard_map/dot_general | solution.py:173
  17.7 1.9 %collective-permute-start.2 = (bf16[48,384]{1,0:T(8,128)(2,1)}, bf16[48,384]{1,0:T(8,128)(2,1)}, u32[]{:S(2)}, u32[]{:S(2)}) collective-permute-start(bf16[48,384]{1,0:T(8,128)(2,1)} %convolution_convert_fusion), channel_id=1, source_target_pairs={{0,256},{256,0},{1,257},{257,1},{2,258},{258,2},{3,259},{259,3},{4... | collective-permute-start | bytes 110600 | tf_op jit(solution)/shard_map/ppermute | solution.py:176
  19.9 0.9 scatter_custom_fusion
  20.8 0.2 reshape.37
  21.0 0.1 reshape.38
  21.2 0.1 concatenate.3.table_ref
  21.3 2.2 %collective-permute-start.8 = (bf16[288,1024]{1,0:T(8,128)(2,1)}, bf16[288,1024]{1,0:T(8,128)(2,1)S(1)}, u32[]{:S(2)}, u32[]{:S(2)}) collective-permute-start(bf16[288,1024]{1,0:T(8,128)(2,1)} %copy-done.2), channel_id=1, source_target_pairs={{0,2},{2,4},{4,6},{6,256},{256,258},{258,260},{260,262},{262,0},{1... | collective-permute-start | bytes 1769480 | tf_op jit(solution)/shard_map/ppermute | solution.py:150
  23.4 0.0 collective-permute-done.refs_3_
  23.5 3.6 %collective-permute-done.2 = bf16[48,384]{1,0:T(8,128)(2,1)} collective-permute-done((bf16[48,384]{1,0:T(8,128)(2,1)}, bf16[48,384]{1,0:T(8,128)(2,1)}, u32[]{:S(2)}, u32[]{:S(2)}) %collective-permute-start.2) | collective-permute-done | bytes 36896 | tf_op jit(solution)/shard_map/ppermute | solution.py:176
  27.0 2.6 %collective-permute-start.3 = (bf16[288,1024]{1,0:T(8,128)(2,1)S(1)}, bf16[288,1024]{1,0:T(8,128)(2,1)}, u32[]{:S(2)}, u32[]{:S(2)}) collective-permute-start(bf16[288,1024]{1,0:T(8,128)(2,1)S(1)} %collective-permute-done.refs_3_), channel_id=1, source_target_pairs={{0,2},{2,4},{4,6},{6,256},{256,258},{258,260},{260,262},{262,0},{1... | collective-permute-start | bytes 1769480 | tf_op jit(solution)/shard_map/ppermute | solution.py:150
  29.7 0.9 maximum_select_fusion
  30.6 0.7 broadcast_in_dim.13
  31.3 4.1 %all-to-all-start = ((bf16[4,96,384]{2,1,0:T(8,128)(2,1)}), bf16[4,96,384]{2,1,0:T(8,128)(2,1)}, u32[]{:S(2)}, u32[]{:S(2)}) async-start(bf16[4,96,384]{2,1,0:T(8,128)(2,1)} %broadcast_in_dim.13), calls=%async_computation | async-start | bytes 589824 | tf_op jit(solution)/shard_map/all_to_all | solution.py:133
  35.4 0.0 collective-permute-done.8.refs_7_
  35.4 1.9 %collective-permute-start.9 = (bf16[288,1024]{1,0:T(8,128)(2,1)S(1)}, bf16[288,1024]{1,0:T(8,128)(2,1)}, u32[]{:S(2)}, u32[]{:S(2)}) collective-permute-start(bf16[288,1024]{1,0:T(8,128)(2,1)S(1)} %collective-permute-done.8.refs_7_), channel_id=1, source_target_pairs={{0,2},{2,4},{4,6},{6,256},{256,258},{258,260},{260,262},{262,0},{1... | collective-permute-start | bytes 1769480 | tf_op jit(solution)/shard_map/ppermute | solution.py:150
  37.3 4.9 %all-to-all-done = bf16[4,96,384]{2,1,0:T(8,128)(2,1)} async-done(((bf16[4,96,384]{2,1,0:T(8,128)(2,1)}), bf16[4,96,384]{2,1,0:T(8,128)(2,1)}, u32[]{:S(2)}, u32[]{:S(2)}) %all-to-all-start) | async-done | bytes 294944 | tf_op jit(solution)/shard_map/all_to_all | solution.py:133
  42.2 0.0 collective-permute-done.3.refs_4_
  42.2 1.9 %collective-permute-start.4 = (bf16[288,1024]{1,0:T(8,128)(2,1)}, bf16[288,1024]{1,0:T(8,128)(2,1)S(1)}, u32[]{:S(2)}, u32[]{:S(2)}) collective-permute-start(bf16[288,1024]{1,0:T(8,128)(2,1)} %collective-permute-done.3.refs_4_), channel_id=1, source_target_pairs={{0,2},{2,4},{4,6},{6,256},{256,258},{258,260},{260,262},{262,0},{1... | collective-permute-start | bytes 1769480 | tf_op jit(solution)/shard_map/ppermute | solution.py:150
  44.2 2.7 %collective-permute-start.5 = (bf16[16,24,384]{2,1,0:T(8,128)(2,1)}, bf16[16,24,384]{2,1,0:T(8,128)(2,1)S(1)}, u32[]{:S(2)}, u32[]{:S(2)}) collective-permute-start(bf16[16,24,384]{2,1,0:T(8,128)(2,1)} %bitcast.20.refs_0_), channel_id=1, source_target_pairs={{0,8},{8,16},{16,24},{24,32},{32,40},{40,48},{48,56},{56,0},{1,9},... | collective-permute-start | bytes 884744 | tf_op jit(solution)/shard_map/ppermute | solution.py:190
  46.9 3.8 %collective-permute-start.6 = (bf16[16,24,384]{2,1,0:T(8,128)(2,1)}, bf16[16,24,384]{2,1,0:T(8,128)(2,1)S(1)}, u32[]{:S(2)}, u32[]{:S(2)}) collective-permute-start(bf16[16,24,384]{2,1,0:T(8,128)(2,1)} %bitcast.20.refs_0_), channel_id=1, source_target_pairs={{0,56},{8,0},{16,8},{24,16},{32,24},{40,32},{48,40},{56,48},{1,57}... | collective-permute-start | bytes 884744 | tf_op jit(solution)/shard_map/ppermute | solution.py:192
  50.7 0.0 collective-permute-done.9.refs_8_
  50.7 3.1 %collective-permute-start.10 = (bf16[288,1024]{1,0:T(8,128)(2,1)}, bf16[288,1024]{1,0:T(8,128)(2,1)S(1)}, u32[]{:S(2)}, u32[]{:S(2)}) collective-permute-start(bf16[288,1024]{1,0:T(8,128)(2,1)} %collective-permute-done.9.refs_8_), channel_id=1, source_target_pairs={{0,2},{2,4},{4,6},{6,256},{256,258},{258,260},{260,262},{262,0},{1... | collective-permute-start | bytes 1769480 | tf_op jit(solution)/shard_map/ppermute | solution.py:150
  53.8 0.0 collective-permute-done.5.refs_1_
  53.8 1.0 collective-permute-done.6.refs_7_
  54.8 0.0 collective-permute-done.4.refs_5_
  54.8 3.1 %collective-permute-start.7 = (bf16[288,1024]{1,0:T(8,128)(2,1)S(1)}, bf16[288,1024]{1,0:T(8,128)(2,1)S(1)}, u32[]{:S(2)}, u32[]{:S(2)}) collective-permute-start(bf16[288,1024]{1,0:T(8,128)(2,1)S(1)} %collective-permute-done.4.refs_5_), channel_id=1, source_target_pairs={{0,2},{2,4},{4,6},{6,256},{256,258},{258,260},{260,262},{262,0},{1... | collective-permute-start | bytes 1769480 | tf_op jit(solution)/shard_map/ppermute | solution.py:150
  57.9 3.2 %collective-permute-start.11 = (bf16[16,24,384]{2,1,0:T(8,128)(2,1)S(1)}, bf16[16,24,384]{2,1,0:T(8,128)(2,1)S(1)}, u32[]{:S(2)}, u32[]{:S(2)}) collective-permute-start(bf16[16,24,384]{2,1,0:T(8,128)(2,1)S(1)} %collective-permute-done.5.refs_1_), channel_id=1, source_target_pairs={{0,8},{8,16},{16,24},{24,32},{32,40},{40,48},{48,56},{56,0},{1,9},... | collective-permute-start | bytes 884744 | tf_op jit(solution)/shard_map/ppermute | solution.py:190
  61.2 0.7 copy-done.4
  61.9 3.4 %collective-permute-start.12 = (bf16[16,24,384]{2,1,0:T(8,128)(2,1)S(1)}, bf16[16,24,384]{2,1,0:T(8,128)(2,1)S(1)}, u32[]{:S(2)}, u32[]{:S(2)}) collective-permute-start(bf16[16,24,384]{2,1,0:T(8,128)(2,1)S(1)} %collective-permute-done.6.refs_7_), channel_id=1, source_target_pairs={{0,56},{8,0},{16,8},{24,16},{32,24},{40,32},{48,40},{56,48},{1,57}... | collective-permute-start | bytes 884744 | tf_op jit(solution)/shard_map/ppermute | solution.py:192
  65.3 0.7 copy-done.6
  66.0 0.0 collective-permute-done.10.refs_9_
  66.1 2.1 %collective-permute-done.7.refs_1_.refs_6_ = bf16[288,1024]{1,0:T(8,128)(2,1)S(1)} collective-permute-done((bf16[288,1024]{1,0:T(8,128)(2,1)S(1)}, bf16[288,1024]{1,0:T(8,128)(2,1)S(1)}, u32[]{:S(2)}, u32[]{:S(2)}) %collective-permute-start.7) | collective-permute-done | bytes 589856 | tf_op jit(solution)/shard_map/ppermute | solution.py:150
  68.1 0.0 collective-permute-done.11.refs_2_
  68.1 2.1 %collective-permute-done.12.refs_6_ = bf16[16,24,384]{2,1,0:T(8,128)(2,1)S(1)} collective-permute-done((bf16[16,24,384]{2,1,0:T(8,128)(2,1)S(1)}, bf16[16,24,384]{2,1,0:T(8,128)(2,1)S(1)}, u32[]{:S(2)}, u32[]{:S(2)}) %collective-permute-start.12) | collective-permute-done | bytes 294944 | tf_op jit(solution)/shard_map/ppermute | solution.py:192
  70.2 7.1 %collective-permute-start.13 = (bf16[288,1024]{1,0:T(8,128)(2,1)S(1)}, bf16[288,1024]{1,0:T(8,128)(2,1)S(1)}, u32[]{:S(2)}, u32[]{:S(2)}) collective-permute-start(bf16[288,1024]{1,0:T(8,128)(2,1)S(1)} %collective-permute-done.7.refs_1_.refs_6_), channel_id=1, source_target_pairs={{0,1},{1,0},{2,3},{3,2},{4,5},{5,4},{6,7},{7,6},{8,9},{9,8},{10,11... | collective-permute-start | bytes 1769480 | tf_op jit(solution)/shard_map/ppermute | solution.py:204
  77.4 1.6 %collective-permute-done.13.refs_1_ = bf16[288,1024]{1,0:T(8,128)(2,1)S(1)} collective-permute-done((bf16[288,1024]{1,0:T(8,128)(2,1)S(1)}, bf16[288,1024]{1,0:T(8,128)(2,1)S(1)}, u32[]{:S(2)}, u32[]{:S(2)}) %collective-permute-start.13) | collective-permute-done | bytes 589856 | tf_op jit(solution)/shard_map/ppermute | solution.py:204
  79.0 1.1 copy-done.3
  80.0 4.3 %shard_map.60 = f32[4,896,128]{2,1,0:T(8,128)S(1)} custom-call(s32[145]{0:T(256)S(1)} %concatenate.3.table_ref, bf16[288,1024]{1,0:T(8,128)(2,1)S(1)} %copy-done.3, bf16[288,1024]{1,0:T(8,128)(2,1)S(1)} %collective-permute-done.13.refs_1_, bf16[288,1024]{1,0:T(8,128)(2,1)S(1)} %bitcast.29, bf16[288,1024]{1,0:T(8,128)(2,1)S(1)} %collective-permute-done.refs_3_, ...), custom_call_target="tpu_custom_call" | custom-call | tf_op jit(solution)/shard_map/pallas_call | solution.py:58
  84.4 2.3 %collective-permute-start.14 = (f32[4,896,128]{2,1,0:T(8,128)S(1)}, f32[4,896,128]{2,1,0:T(8,128)S(1)}, u32[]{:S(2)}, u32[]{:S(2)}) collective-permute-start(f32[4,896,128]{2,1,0:T(8,128)S(1)} %shard_map.60), channel_id=1, source_target_pairs={{0,1},{1,0},{2,3},{3,2},{4,5},{5,4},{6,7},{7,6},{8,9},{9,8},{10,11... | collective-permute-start | bytes 5505032 | tf_op jit(solution)/shard_map/ppermute | solution.py:212
  86.7 4.4 %shard_map.59 = f32[4,896,128]{2,1,0:T(8,128)S(1)} custom-call(s32[145]{0:T(256)S(1)} %concatenate.3.table_ref, bf16[288,1024]{1,0:T(8,128)(2,1)S(1)} %bitcast.30, bf16[288,1024]{1,0:T(8,128)(2,1)S(1)} %collective-permute-done.7.refs_1_.refs_6_, bf16[288,1024]{1,0:T(8,128)(2,1)S(1)} %bitcast.31, bf16[288,1024]{1,0:T(8,128)(2,1)S(1)} %collective-permute-done.refs_3_, ...), custom_call_target="tpu_custom_call" | custom-call | tf_op jit(solution)/shard_map/pallas_call | solution.py:58
  91.0 0.0 collective-permute-done.14
  91.1 1.4 add.165
  92.5 4.5 %all-to-all-start.1 = ((f32[4,896,128]{2,1,0:T(8,128)}), f32[4,896,128]{2,1,0:T(8,128)}, u32[]{:S(2)}, u32[]{:S(2)}) async-start(f32[4,896,128]{2,1,0:T(8,128)} %add.165), calls=%async_computation.1 | async-start | bytes 3670016 | tf_op jit(solution)/shard_map/all_to_all | solution.py:214
  97.0 4.7 %collective-permute-start.15 = (bf16[16,24,384]{2,1,0:T(8,128)(2,1)S(1)}, bf16[16,24,384]{2,1,0:T(8,128)(2,1)S(1)}, u32[]{:S(2)}, u32[]{:S(2)}) collective-permute-start(bf16[16,24,384]{2,1,0:T(8,128)(2,1)S(1)} %copy-done.9), channel_id=1, source_target_pairs={{0,8},{8,16},{16,24},{24,32},{32,40},{40,48},{48,56},{56,0},{1,9},... | collective-permute-start | bytes 884744 | tf_op jit(solution)/shard_map/ppermute | solution.py:190
  101.8 1.9 %collective-permute-start.17 = (bf16[16,24,384]{2,1,0:T(8,128)(2,1)S(1)}, bf16[16,24,384]{2,1,0:T(8,128)(2,1)S(1)}, u32[]{:S(2)}, u32[]{:S(2)}) collective-permute-start(bf16[16,24,384]{2,1,0:T(8,128)(2,1)S(1)} %copy-done.11), channel_id=1, source_target_pairs={{0,56},{8,0},{16,8},{24,16},{32,24},{40,32},{48,40},{56,48},{1,57}... | collective-permute-start | bytes 884744 | tf_op jit(solution)/shard_map/ppermute | solution.py:192
  103.7 5.2 %collective-permute-done.15.refs_3_ = bf16[16,24,384]{2,1,0:T(8,128)(2,1)S(1)} collective-permute-done((bf16[16,24,384]{2,1,0:T(8,128)(2,1)S(1)}, bf16[16,24,384]{2,1,0:T(8,128)(2,1)S(1)}, u32[]{:S(2)}, u32[]{:S(2)}) %collective-permute-start.15) | collective-permute-done | bytes 294944 | tf_op jit(solution)/shard_map/ppermute | solution.py:190
  108.9 3.3 %collective-permute-start.16 = (bf16[16,24,384]{2,1,0:T(8,128)(2,1)S(1)}, bf16[16,24,384]{2,1,0:T(8,128)(2,1)}, u32[]{:S(2)}, u32[]{:S(2)}) collective-permute-start(bf16[16,24,384]{2,1,0:T(8,128)(2,1)S(1)} %collective-permute-done.15.refs_3_), channel_id=1, source_target_pairs={{0,8},{8,16},{16,24},{24,32},{32,40},{40,48},{48,56},{56,0},{1,9},... | collective-permute-start | bytes 884744 | tf_op jit(solution)/shard_map/ppermute | solution.py:190
  112.2 8.4 %all-to-all-done.1 = f32[4,896,128]{2,1,0:T(8,128)} async-done(((f32[4,896,128]{2,1,0:T(8,128)}), f32[4,896,128]{2,1,0:T(8,128)}, u32[]{:S(2)}, u32[]{:S(2)}) %all-to-all-start.1) | async-done | bytes 1835040 | tf_op jit(solution)/shard_map/all_to_all | solution.py:214
  120.6 2.3 %fusion = f32[896,128]{1,0:T(8,128)} fusion(f32[4,896,128]{2,1,0:T(8,128)} %all-to-all-done.1), kind=kLoop, calls=%fused_computation.3 | loop fusion | flops 344064 | bytes 2293760 | tf_op jit(solution)/shard_map/add | solution.py:215
  122.9 0.0 collective-permute-done.17.refs_5_
  122.9 0.0 collective-permute-done.16.refs_4_
  122.9 9.4 %all-to-all-start.2 = ((f32[16,56,128]{2,1,0:T(8,128)}), f32[16,56,128]{2,1,0:T(8,128)}, u32[]{:S(2)}, u32[]{:S(2)}) async-start(f32[16,56,128]{2,1,0:T(8,128)} %bitcast.32), calls=%async_computation.2 | async-start | bytes 917504 | tf_op jit(solution)/shard_map/all_to_all | solution.py:217
  132.4 0.0 copy-start.13
  132.4 1.0 copy-done.13
  133.3 1.0 copy-done.15
  134.3 3.2 %shard_map.62 = bf16[2304,384]{1,0:T(8,128)(2,1)} custom-call(s32[96]{0:T(128)S(1)} %get-tuple-element.38.place_of, bf16[16,24,384]{2,1,0:T(8,128)(2,1)} %bitcast.20.refs_0_, bf16[16,24,384]{2,1,0:T(8,128)(2,1)S(1)} %copy-done.5, bf16[16,24,384]{2,1,0:T(8,128)(2,1)S(1)} %copy-done.9, bf16[16,24,384]{2,1,0:T(8,128)(2,1)S(1)} %copy-done.13, ...), custom_call_target="tpu_custom_call" | custom-call | tf_op jit(solution)/shard_map/pallas_call | solution.py:117
  137.5 13.6 %all-to-all-done.2 = f32[16,56,128]{2,1,0:T(8,128)} async-done(((f32[16,56,128]{2,1,0:T(8,128)}), f32[16,56,128]{2,1,0:T(8,128)}, u32[]{:S(2)}, u32[]{:S(2)}) %all-to-all-start.2) | async-done | bytes 458784 | tf_op jit(solution)/shard_map/all_to_all | solution.py:217
  151.0 1.8 %shard_map.61 = f32[2,24,288]{2,1,0:T(8,128)} custom-call(f32[8,2,56,128]{3,2,1,0:T(8,128)} %bitcast.23.parts_ref), custom_call_target="tpu_custom_call" | custom-call | tf_op jit(solution)/shard_map/pallas_call | solution.py:93
  (28 shorter events, 0.1 us)
Async XLA Ops:
  0.6 15.1 %copy-start = (bf16[2304,384]{1,0:T(8,128)(2,1)S(1)}, bf16[2304,384]{1,0:T(8,128)(2,1)}, u32[]{:S(2)}) copy-start(bf16[2304,384]{1,0:T(8,128)(2,1)} %param.7) | copy-start | bytes 5308420
  0.6 19.0 %copy-start.16 = (s32[96]{0:T(128)S(1)}, s32[96]{0:T(128)}, u32[]{:S(2)}) copy-start(s32[96]{0:T(128)} %param.5) | copy-start | bytes 1156
  0.7 14.2 %collective-permute-start.1 = (bf16[288,1024]{1,0:T(8,128)(2,1)}, bf16[288,1024]{1,0:T(8,128)(2,1)S(1)}, u32[]{:S(2)}, u32[]{:S(2)}) collective-permute-start(bf16[288,1024]{1,0:T(8,128)(2,1)} %bitcast.27), channel_id=1, source_target_pairs={{0,1},{1,0},{2,3},{3,2},{4,5},{5,4},{6,7},{7,6},{8,9},{9,8},{10,11... | collective-permute-start | bytes 1769480 | tf_op jit(solution)/shard_map/ppermute | solution.py:169
  9.6 13.9 %collective-permute-start = (bf16[288,1024]{1,0:T(8,128)(2,1)}, bf16[288,1024]{1,0:T(8,128)(2,1)S(1)}, u32[]{:S(2)}, u32[]{:S(2)}) collective-permute-start(bf16[288,1024]{1,0:T(8,128)(2,1)} %bitcast.28), channel_id=1, source_target_pairs={{0,2},{2,4},{4,6},{6,256},{256,258},{258,260},{260,262},{262,0},{1... | collective-permute-start | bytes 1769480 | tf_op jit(solution)/shard_map/ppermute | solution.py:150
  14.9 0.8 copy-start.2
  15.7 63.3 %copy-start.1 = (bf16[1024,288]{0,1:T(8,128)(2,1)S(1)}, bf16[1024,288]{0,1:T(8,128)(2,1)}, u32[]{:S(2)}) copy-start(bf16[1024,288]{0,1:T(8,128)(2,1)} %param.4) | copy-start | bytes 1769476
  17.7 9.3 %collective-permute-start.2 = (bf16[48,384]{1,0:T(8,128)(2,1)}, bf16[48,384]{1,0:T(8,128)(2,1)}, u32[]{:S(2)}, u32[]{:S(2)}) collective-permute-start(bf16[48,384]{1,0:T(8,128)(2,1)} %convolution_convert_fusion), channel_id=1, source_target_pairs={{0,256},{256,0},{1,257},{257,1},{2,258},{258,2},{3,259},{259,3},{4... | collective-permute-start | bytes 110600 | tf_op jit(solution)/shard_map/ppermute | solution.py:176
  21.3 14.1 %collective-permute-start.8 = (bf16[288,1024]{1,0:T(8,128)(2,1)}, bf16[288,1024]{1,0:T(8,128)(2,1)S(1)}, u32[]{:S(2)}, u32[]{:S(2)}) collective-permute-start(bf16[288,1024]{1,0:T(8,128)(2,1)} %copy-done.2), channel_id=1, source_target_pairs={{0,2},{2,4},{4,6},{6,256},{256,258},{258,260},{260,262},{262,0},{1... | collective-permute-start | bytes 1769480 | tf_op jit(solution)/shard_map/ppermute | solution.py:150
  27.0 15.2 %collective-permute-start.3 = (bf16[288,1024]{1,0:T(8,128)(2,1)S(1)}, bf16[288,1024]{1,0:T(8,128)(2,1)}, u32[]{:S(2)}, u32[]{:S(2)}) collective-permute-start(bf16[288,1024]{1,0:T(8,128)(2,1)S(1)} %collective-permute-done.refs_3_), channel_id=1, source_target_pairs={{0,2},{2,4},{4,6},{6,256},{256,258},{258,260},{260,262},{262,0},{1... | collective-permute-start | bytes 1769480 | tf_op jit(solution)/shard_map/ppermute | solution.py:150
  31.3 10.9 %all-to-all-start = ((bf16[4,96,384]{2,1,0:T(8,128)(2,1)}), bf16[4,96,384]{2,1,0:T(8,128)(2,1)}, u32[]{:S(2)}, u32[]{:S(2)}) async-start(bf16[4,96,384]{2,1,0:T(8,128)(2,1)} %broadcast_in_dim.13), calls=%async_computation | async-start | bytes 589824 | tf_op jit(solution)/shard_map/all_to_all | solution.py:133
  35.4 15.3 %collective-permute-start.9 = (bf16[288,1024]{1,0:T(8,128)(2,1)S(1)}, bf16[288,1024]{1,0:T(8,128)(2,1)}, u32[]{:S(2)}, u32[]{:S(2)}) collective-permute-start(bf16[288,1024]{1,0:T(8,128)(2,1)S(1)} %collective-permute-done.8.refs_7_), channel_id=1, source_target_pairs={{0,2},{2,4},{4,6},{6,256},{256,258},{258,260},{260,262},{262,0},{1... | collective-permute-start | bytes 1769480 | tf_op jit(solution)/shard_map/ppermute | solution.py:150
  42.2 12.6 %collective-permute-start.4 = (bf16[288,1024]{1,0:T(8,128)(2,1)}, bf16[288,1024]{1,0:T(8,128)(2,1)S(1)}, u32[]{:S(2)}, u32[]{:S(2)}) collective-permute-start(bf16[288,1024]{1,0:T(8,128)(2,1)} %collective-permute-done.3.refs_4_), channel_id=1, source_target_pairs={{0,2},{2,4},{4,6},{6,256},{256,258},{258,260},{260,262},{262,0},{1... | collective-permute-start | bytes 1769480 | tf_op jit(solution)/shard_map/ppermute | solution.py:150
  44.2 9.7 %collective-permute-start.5 = (bf16[16,24,384]{2,1,0:T(8,128)(2,1)}, bf16[16,24,384]{2,1,0:T(8,128)(2,1)S(1)}, u32[]{:S(2)}, u32[]{:S(2)}) collective-permute-start(bf16[16,24,384]{2,1,0:T(8,128)(2,1)} %bitcast.20.refs_0_), channel_id=1, source_target_pairs={{0,8},{8,16},{16,24},{24,32},{32,40},{40,48},{48,56},{56,0},{1,9},... | collective-permute-start | bytes 884744 | tf_op jit(solution)/shard_map/ppermute | solution.py:190
  46.9 8.0 %collective-permute-start.6 = (bf16[16,24,384]{2,1,0:T(8,128)(2,1)}, bf16[16,24,384]{2,1,0:T(8,128)(2,1)S(1)}, u32[]{:S(2)}, u32[]{:S(2)}) collective-permute-start(bf16[16,24,384]{2,1,0:T(8,128)(2,1)} %bitcast.20.refs_0_), channel_id=1, source_target_pairs={{0,56},{8,0},{16,8},{24,16},{32,24},{40,32},{48,40},{56,48},{1,57}... | collective-permute-start | bytes 884744 | tf_op jit(solution)/shard_map/ppermute | solution.py:192
  50.7 15.4 %collective-permute-start.10 = (bf16[288,1024]{1,0:T(8,128)(2,1)}, bf16[288,1024]{1,0:T(8,128)(2,1)S(1)}, u32[]{:S(2)}, u32[]{:S(2)}) collective-permute-start(bf16[288,1024]{1,0:T(8,128)(2,1)} %collective-permute-done.9.refs_8_), channel_id=1, source_target_pairs={{0,2},{2,4},{4,6},{6,256},{256,258},{258,260},{260,262},{262,0},{1... | collective-permute-start | bytes 1769480 | tf_op jit(solution)/shard_map/ppermute | solution.py:150
  54.8 13.3 %collective-permute-start.7 = (bf16[288,1024]{1,0:T(8,128)(2,1)S(1)}, bf16[288,1024]{1,0:T(8,128)(2,1)S(1)}, u32[]{:S(2)}, u32[]{:S(2)}) collective-permute-start(bf16[288,1024]{1,0:T(8,128)(2,1)S(1)} %collective-permute-done.4.refs_5_), channel_id=1, source_target_pairs={{0,2},{2,4},{4,6},{6,256},{256,258},{258,260},{260,262},{262,0},{1... | collective-permute-start | bytes 1769480 | tf_op jit(solution)/shard_map/ppermute | solution.py:150
  57.9 10.2 %collective-permute-start.11 = (bf16[16,24,384]{2,1,0:T(8,128)(2,1)S(1)}, bf16[16,24,384]{2,1,0:T(8,128)(2,1)S(1)}, u32[]{:S(2)}, u32[]{:S(2)}) collective-permute-start(bf16[16,24,384]{2,1,0:T(8,128)(2,1)S(1)} %collective-permute-done.5.refs_1_), channel_id=1, source_target_pairs={{0,8},{8,16},{16,24},{24,32},{32,40},{40,48},{48,56},{56,0},{1,9},... | collective-permute-start | bytes 884744 | tf_op jit(solution)/shard_map/ppermute | solution.py:190
  61.2 0.7 copy-start.4
  61.9 8.4 %collective-permute-start.12 = (bf16[16,24,384]{2,1,0:T(8,128)(2,1)S(1)}, bf16[16,24,384]{2,1,0:T(8,128)(2,1)S(1)}, u32[]{:S(2)}, u32[]{:S(2)}) collective-permute-start(bf16[16,24,384]{2,1,0:T(8,128)(2,1)S(1)} %collective-permute-done.6.refs_7_), channel_id=1, source_target_pairs={{0,56},{8,0},{16,8},{24,16},{32,24},{40,32},{48,40},{56,48},{1,57}... | collective-permute-start | bytes 884744 | tf_op jit(solution)/shard_map/ppermute | solution.py:192
  65.3 0.7 copy-start.6
  68.1 9.2 %copy-start.8 = (bf16[16,24,384]{2,1,0:T(8,128)(2,1)}, bf16[16,24,384]{2,1,0:T(8,128)(2,1)S(1)}, u32[]{:S(2)}) copy-start(bf16[16,24,384]{2,1,0:T(8,128)(2,1)S(1)} %collective-permute-done.11.refs_2_) | copy-start | bytes 884740
  70.2 7.2 %copy-start.10 = (bf16[16,24,384]{2,1,0:T(8,128)(2,1)}, bf16[16,24,384]{2,1,0:T(8,128)(2,1)S(1)}, u32[]{:S(2)}) copy-start(bf16[16,24,384]{2,1,0:T(8,128)(2,1)S(1)} %collective-permute-done.12.refs_6_) | copy-start | bytes 884740
  70.2 8.7 %collective-permute-start.13 = (bf16[288,1024]{1,0:T(8,128)(2,1)S(1)}, bf16[288,1024]{1,0:T(8,128)(2,1)S(1)}, u32[]{:S(2)}, u32[]{:S(2)}) collective-permute-start(bf16[288,1024]{1,0:T(8,128)(2,1)S(1)} %collective-permute-done.7.refs_1_.refs_6_), channel_id=1, source_target_pairs={{0,1},{1,0},{2,3},{3,2},{4,5},{5,4},{6,7},{7,6},{8,9},{9,8},{10,11... | collective-permute-start | bytes 1769480 | tf_op jit(solution)/shard_map/ppermute | solution.py:204
  79.0 1.1 copy-start.3
  84.4 6.7 %collective-permute-start.14 = (f32[4,896,128]{2,1,0:T(8,128)S(1)}, f32[4,896,128]{2,1,0:T(8,128)S(1)}, u32[]{:S(2)}, u32[]{:S(2)}) collective-permute-start(f32[4,896,128]{2,1,0:T(8,128)S(1)} %shard_map.60), channel_id=1, source_target_pairs={{0,1},{1,0},{2,3},{3,2},{4,5},{5,4},{6,7},{7,6},{8,9},{9,8},{10,11... | collective-permute-start | bytes 5505032 | tf_op jit(solution)/shard_map/ppermute | solution.py:212
  92.5 4.5 %copy-start.9 = (bf16[16,24,384]{2,1,0:T(8,128)(2,1)S(1)}, bf16[16,24,384]{2,1,0:T(8,128)(2,1)}, u32[]{:S(2)}) copy-start(bf16[16,24,384]{2,1,0:T(8,128)(2,1)} %copy-done.8) | copy-start | bytes 884740
  92.5 9.3 %copy-start.11 = (bf16[16,24,384]{2,1,0:T(8,128)(2,1)S(1)}, bf16[16,24,384]{2,1,0:T(8,128)(2,1)}, u32[]{:S(2)}) copy-start(bf16[16,24,384]{2,1,0:T(8,128)(2,1)} %copy-done.10) | copy-start | bytes 884740
  92.5 28.1 %all-to-all-start.1 = ((f32[4,896,128]{2,1,0:T(8,128)}), f32[4,896,128]{2,1,0:T(8,128)}, u32[]{:S(2)}, u32[]{:S(2)}) async-start(f32[4,896,128]{2,1,0:T(8,128)} %add.165), calls=%async_computation.1 | async-start | bytes 3670016 | tf_op jit(solution)/shard_map/all_to_all | solution.py:214
  97.0 35.3 %copy-start.5 = (bf16[16,24,384]{2,1,0:T(8,128)(2,1)S(1)}, bf16[16,24,384]{2,1,0:T(8,128)(2,1)}, u32[]{:S(2)}) copy-start(bf16[16,24,384]{2,1,0:T(8,128)(2,1)} %copy-done.4) | copy-start | bytes 884740
  97.0 35.3 %copy-start.7 = (bf16[16,24,384]{2,1,0:T(8,128)(2,1)S(1)}, bf16[16,24,384]{2,1,0:T(8,128)(2,1)}, u32[]{:S(2)}) copy-start(bf16[16,24,384]{2,1,0:T(8,128)(2,1)} %copy-done.6) | copy-start | bytes 884740
  97.0 11.8 %collective-permute-start.15 = (bf16[16,24,384]{2,1,0:T(8,128)(2,1)S(1)}, bf16[16,24,384]{2,1,0:T(8,128)(2,1)S(1)}, u32[]{:S(2)}, u32[]{:S(2)}) collective-permute-start(bf16[16,24,384]{2,1,0:T(8,128)(2,1)S(1)} %copy-done.9), channel_id=1, source_target_pairs={{0,8},{8,16},{16,24},{24,32},{32,40},{40,48},{48,56},{56,0},{1,9},... | collective-permute-start | bytes 884744 | tf_op jit(solution)/shard_map/ppermute | solution.py:190
  101.8 21.1 %collective-permute-start.17 = (bf16[16,24,384]{2,1,0:T(8,128)(2,1)S(1)}, bf16[16,24,384]{2,1,0:T(8,128)(2,1)S(1)}, u32[]{:S(2)}, u32[]{:S(2)}) collective-permute-start(bf16[16,24,384]{2,1,0:T(8,128)(2,1)S(1)} %copy-done.11), channel_id=1, source_target_pairs={{0,56},{8,0},{16,8},{24,16},{32,24},{40,32},{48,40},{56,48},{1,57}... | collective-permute-start | bytes 884744 | tf_op jit(solution)/shard_map/ppermute | solution.py:192
  108.8 14.0 %copy-start.12 = (bf16[16,24,384]{2,1,0:T(8,128)(2,1)}, bf16[16,24,384]{2,1,0:T(8,128)(2,1)S(1)}, u32[]{:S(2)}) copy-start(bf16[16,24,384]{2,1,0:T(8,128)(2,1)S(1)} %collective-permute-done.15.refs_3_) | copy-start | bytes 884740
  108.9 14.0 %collective-permute-start.16 = (bf16[16,24,384]{2,1,0:T(8,128)(2,1)S(1)}, bf16[16,24,384]{2,1,0:T(8,128)(2,1)}, u32[]{:S(2)}, u32[]{:S(2)}) collective-permute-start(bf16[16,24,384]{2,1,0:T(8,128)(2,1)S(1)} %collective-permute-done.15.refs_3_), channel_id=1, source_target_pairs={{0,8},{8,16},{16,24},{24,32},{32,40},{40,48},{48,56},{56,0},{1,9},... | collective-permute-start | bytes 884744 | tf_op jit(solution)/shard_map/ppermute | solution.py:190
  122.9 9.4 %copy-start.14 = (bf16[16,24,384]{2,1,0:T(8,128)(2,1)}, bf16[16,24,384]{2,1,0:T(8,128)(2,1)S(1)}, u32[]{:S(2)}) copy-start(bf16[16,24,384]{2,1,0:T(8,128)(2,1)S(1)} %collective-permute-done.17.refs_5_) | copy-start | bytes 884740
  122.9 28.1 %all-to-all-start.2 = ((f32[16,56,128]{2,1,0:T(8,128)}), f32[16,56,128]{2,1,0:T(8,128)}, u32[]{:S(2)}, u32[]{:S(2)}) async-start(f32[16,56,128]{2,1,0:T(8,128)} %bitcast.32), calls=%async_computation.2 | async-start | bytes 917504 | tf_op jit(solution)/shard_map/all_to_all | solution.py:217
  132.4 1.0 copy-start.13
  133.3 1.0 copy-start.15
